TPU v7x, 128 devices: a whole 4x4x4 slice. The times are simulated.
128 devices in a mesh: row: 8 (over z, x_hi), col: 16 (over y, x_lo, core).
Axes of the slice: x: 4 (x_hi: 2, x_lo: 2; x = x_hi * 2 + x_lo), y: 4, z: 4, core: 2. Of those that a mesh axis runs over, the one named last changes fastest.
Arguments:
- pages: float32 [16384, 1024], P(('row', 'col')), as said below
- transcripts: float32 [16384, 1024], P(('col', 'row')), as said below
- length_scale: float32 [1], replicated, may hold values from 0.6 to 0.9
Outputs:
- page_grad: float32 [16384, 1024], P(('row', 'col'))
- text_grad: float32 [16384, 1024], P(('col', 'row'))
Inputs may be any that keep to these rules, and one draw needn't show every extreme that they name: `pages`: entries of page embeddings are finite and of magnitude at most 4. `transcripts`: entries of transcription embeddings are finite and of magnitude at most 4.
All inputs are finite; a program needn't handle non-finite values.
Results may differ from a plain program's by a relative error of at most 0.0003.
Values sent between devices are 32-bit elements; how exact they have to be, the bound alone decides.
No kernel may reach another device: no remote copies, remote signals or barrier semaphores. Data moves between devices by JAX's collectives and lax.ppermute only.
A program may use at most 128 MiB of HBM per device.

v0:
```python
import jax
import jax.numpy as jnp
from jax import lax
from jax.sharding import PartitionSpec as P


def kernel_tile(rows, cols, inverse):
    cross = lax.dot_general(
        rows,
        cols,
        (((1,), (1,)), ((), ())),
        precision=lax.Precision.HIGHEST,
        preferred_element_type=jnp.float32,
    )
    first = jnp.sum(rows * rows, axis=1)
    second = jnp.sum(cols * cols, axis=1)
    return jnp.exp(-(first[:, None] + second[None, :] - 2.0 * cross) * inverse)


def on_device(pages, transcripts, length_scale):
    share = pages.shape[0]
    count = share * lax.axis_size("row") * lax.axis_size("col")
    spread_sq = length_scale[0] * length_scale[0]
    inverse = 0.5 / spread_sq
    text_block = lax.all_gather(transcripts, "row", axis=0, tiled=True)
    page_block = lax.all_gather(pages, "col", axis=0, tiled=True)
    kern = kernel_tile(page_block, text_block, inverse)
    height = kern.shape[0]
    breadth = kern.shape[1]
    row_glob = lax.axis_index("row") * height + lax.iota(jnp.int32, height)
    col_glob = lax.axis_index("col") * breadth + lax.iota(jnp.int32, breadth)
    on_diag = (row_glob[:, None] == col_glob[None, :]).astype(jnp.float32)
    col_part = jnp.sum(kern, axis=0)
    row_sums = lax.psum(jnp.sum(kern, axis=1), "col")
    col_sums = lax.psum(col_part, "row")
    total = lax.psum(jnp.sum(col_part), ("row", "col"))
    centred = kern - row_sums[:, None] / count - col_sums[None, :] / count + total / (count * count)
    frob_sq, align = lax.psum(
        (jnp.sum(centred * centred), jnp.sum(centred * on_diag)), ("row", "col")
    )
    frob = jnp.sqrt(frob_sq)
    loss_scale = 4.0 * count
    weight = (
        loss_scale * align / (frob * frob_sq) * centred
        - loss_scale / frob * (on_diag - 1.0 / count)
    ) * kern
    part_weight = weight
    mixed = jnp.dot(
        part_weight, text_block, precision=lax.Precision.HIGHEST, preferred_element_type=jnp.float32
    )
    page_sum = lax.psum_scatter(
        jnp.sum(part_weight, axis=1)[:, None] * page_block - mixed,
        "col",
        scatter_dimension=0,
        tiled=True,
    )
    part_weight = weight
    folded = lax.dot_general(
        part_weight,
        page_block,
        (((0,), (0,)), ((), ())),
        precision=lax.Precision.HIGHEST,
        preferred_element_type=jnp.float32,
    )
    text_sum = lax.psum_scatter(
        folded - jnp.sum(part_weight, axis=0)[:, None] * text_block,
        "row",
        scatter_dimension=0,
        tiled=True,
    )
    page_grad = -page_sum / spread_sq
    text_grad = text_sum / spread_sq
    return (page_grad, text_grad)


def solution(mesh):
    placed = (P(("row", "col"), None), P(("col", "row"), None), P())
    return jax.shard_map(
        on_device,
        mesh=mesh,
        in_specs=placed,
        out_specs=(P(("row", "col"), None), P(("col", "row"), None)),
        check_vma=False,
    )
```

profile of v0, /device:TPU:0, one launch (start us, length us, event | category | flops | bytes accessed | tf_op | source)
XLA Modules:
  0.0 593.3 jit_solution(3481051266907745817)
XLA Ops:
  7.2 0.0 all-gather.5.cloned.1.call-start
  7.2 0.7 all-gather.5.cloned.1.call-update
  7.9 0.0 all-gather.3.cloned.1.call-start
  7.9 0.7 all-gather.3.cloned.1.call-update
  8.6 0.0 reduce-scatter.5.cloned.1.call-start
  9.4 75.0 %all-gather.5.cloned.1.call-done = f32[1024,1024]{1,0:T(8,128)} async-done(((f32[128,1024]{1,0:T(8,128)}), f32[1024,1024]{1,0:T(8,128)}) %all-gather.5.cloned.1.call-update) | async-done | bytes 4194320 | tf_op jit(solution)/shard_map/all_gather | solution.py:25
  84.4 2.5 multiply_reduce_fusion.2
  86.9 49.1 %all-gather.3.cloned.1.call-done = f32[2048,1024]{1,0:T(8,128)} async-done(((f32[128,1024]{1,0:T(8,128)}), f32[2048,1024]{1,0:T(8,128)}) %all-gather.3.cloned.1.call-update) | async-done | bytes 8388624 | tf_op jit(solution)/shard_map/all_gather | solution.py:26
  136.0 0.0 copy-start
  136.0 4.1 multiply_reduce_fusion.1
  140.2 1.6 copy-done
  141.8 33.8 %fusion.6 = (f32[2048]{0:T(1024)S(1)}, f32[]{:T(128)}, f32[1024]{0:T(1024)S(1)}, f32[2048,1024]{1,0:T(8,128)}) fusion(f32[]{:T(128)S(6)} %div.34, f32[2048,1024]{1,0:T(8,128)S(1)} %copy-done, f32[1024,1024]{1,0:T(8,128)} %all-gather.5.cloned.1.call-done, f32[1024]{0:T(1024)S(1)} %multiply_reduce_fusion.2, f32[2048]{0:T(1024)S(1)} %multiply_reduce_fusion.1), kind=kOutput, calls=%fused_computation.21 | convolution fusion | flops 25786576896 | bytes 20996104 | tf_op jit(solution)/shard_map/dot_general | solution.py:8
  175.5 66.5 %psum.37 = f32[]{:T(128)} all-reduce(f32[]{:T(128)} %get-tuple-element.7), channel_id=1, replica_groups=mesh['row'=8,'col'=16] {'row','col'}, use_global_device_ids=true, to_apply=%region_7.0 | all-reduce | flops 1 | bytes 8 | tf_op jit(solution)/shard_map/psum | solution.py:36
  242.0 22.0 %psum.36 = f32[1024]{0:T(1024)S(1)} all-reduce(f32[1024]{0:T(1024)S(1)} %get-tuple-element.8), channel_id=1, replica_groups=mesh['row'=8,'col'=16] {'row'}, use_global_device_ids=true, to_apply=%region_5.0 | all-reduce | flops 1024 | bytes 8192 | tf_op jit(solution)/shard_map/psum | solution.py:35
  264.0 27.9 %psum.35 = f32[2048]{0:T(1024)S(1)} all-reduce(f32[2048]{0:T(1024)S(1)} %get-tuple-element.6), channel_id=1, replica_groups=mesh['row'=8,'col'=16] {'col'}, use_global_device_ids=true, to_apply=%region_3.0 | all-reduce | flops 2048 | bytes 16384 | tf_op jit(solution)/shard_map/psum | solution.py:34
  292.6 6.8 %fusion = (f32[]{:T(128)}, f32[]{:T(128)}) fusion(f32[2048,1024]{1,0:T(8,128)} %get-tuple-element.12, f32[]{:T(128)S(6)} %div.39, f32[1024]{0:T(1024)S(1)} %broadcast_multiply_fusion.1, f32[2048]{0:T(1024)S(1)} %broadcast_multiply_fusion, s32[1024]{0:T(1024)S(1)} %iota_add_fusion.1, s32[2048]{0:T(1024)S(1)} %iota_add_fusion), kind=kLoop, calls=%fused_computation.2 | loop fusion | flops 16777214 | bytes 8413196 | tf_op jit(solution)/shard_map/reduce_sum | solution.py:39
  299.3 62.0 %all-reduce = (f32[]{:T(128)}, f32[]{:T(128)}) all-reduce(f32[]{:T(128)} %get-tuple-element.3, f32[]{:T(128)} %get-tuple-element.2), channel_id=1, replica_groups=mesh['row'=8,'col'=16] {'row','col'}, use_global_device_ids=true, to_apply=%region_11.0 | all-reduce | flops 2 | bytes 16 | tf_op jit(solution)/shard_map/psum | solution.py:38
  363.5 0.0 copy-start.2
  363.5 6.7 %fusion.5 = (f32[1024]{0:T(1024)S(1)}, f32[2048]{0:T(1024)S(1)}, f32[2048,1024]{1,0:T(8,128)S(1)}) fusion(f32[2048,1024]{1,0:T(8,128)} %get-tuple-element.12, s32[1024]{0:T(1024)S(1)} %iota_add_fusion.1, s32[2048]{0:T(1024)S(1)} %iota_add_fusion, f32[]{:T(128)S(6)} %div.41, f32[]{:T(128)S(6)} %div.39, f32[1024]{0:T(1024)S(1)} %broadcast_multiply_fusion.1, ...), kind=kLoop, calls=%fused_computation.20 | loop fusion | flops 25162752 | bytes 16814092 | tf_op jit(solution)/shard_map/reduce_sum | solution.py:66
  370.2 0.0 copy-start.1
  370.2 3.2 copy-done.1
  373.4 0.0 copy-done.2
  373.4 30.5 %multiply_subtract_fusion.1 = f32[1024,1024]{1,0:T(8,128)} fusion(f32[1024,1024]{1,0:T(8,128)S(1)} %copy-done.2, f32[1024]{0:T(1024)S(1)} %get-tuple-element.4, f32[2048,1024]{1,0:T(8,128)S(1)} %get-tuple-element.11, f32[2048,1024]{1,0:T(8,128)} %all-gather.3.cloned.1.call-done), kind=kOutput, calls=%fused_computation.12 | convolution fusion | flops 25771900928 | bytes 25169920 | tf_op jit(solution)/shard_map/dot_general | solution.py:58
  403.8 0.0 reduce-scatter.5.cloned.1.call-update
  403.9 0.0 reduce-scatter.3.cloned.1.call-start
  403.9 32.5 %multiply_subtract_fusion = f32[2048,1024]{1,0:T(8,128)} fusion(f32[2048,1024]{1,0:T(8,128)} %all-gather.3.cloned.1.call-done, f32[2048]{0:T(1024)S(1)} %get-tuple-element.5, f32[2048,1024]{1,0:T(8,128)} %copy-done.1, f32[1024,1024]{1,0:T(8,128)} %all-gather.5.cloned.1.call-done), kind=kOutput, calls=%fused_computation.7 | convolution fusion | flops 25773998080 | bytes 29368320 | tf_op jit(solution)/shard_map/dot_general | solution.py:48
  436.4 0.0 reduce-scatter.3.cloned.1.call-update
  436.5 49.4 %reduce-scatter.5.cloned.1.call-done = f32[128,1024]{1,0:T(8,128)} async-done(((f32[1024,1024]{1,0:T(8,128)}), f32[128,1024]{1,0:T(8,128)}) %reduce-scatter.5.cloned.1.call-update) | async-done | bytes 524304 | tf_op jit(solution)/shard_map/reduce_scatter | solution.py:65
  485.9 1.9 broadcast_divide_fusion
  487.8 97.1 %reduce-scatter.3.cloned.1.call-done = f32[128,1024]{1,0:T(8,128)} async-done(((f32[2048,1024]{1,0:T(8,128)}), f32[128,1024]{1,0:T(8,128)}) %reduce-scatter.3.cloned.1.call-update) | async-done | bytes 524304 | tf_op jit(solution)/shard_map/reduce_scatter | solution.py:51
  584.9 1.9 negate_divide_fusion
  (4 shorter events, 0.0 us)
Async XLA Ops:
  7.2 77.2 %all-gather.5.cloned.1.call-start = ((), (), s32[]{:S(2)}) async-start(), calls=%async_computation.3 | async-start | bytes 4718592 | tf_op jit(solution)/shard_map/all_gather | solution.py:25
  7.9 128.1 %all-gather.3.cloned.1.call-start = ((), (), s32[]{:S(2)}) async-start(), calls=%async_computation.2 | async-start | bytes 8912896 | tf_op jit(solution)/shard_map/all_gather | solution.py:26
  8.6 477.2 %reduce-scatter.5.cloned.1.call-start = ((), (), s32[]{:S(2)}) async-start(), calls=%async_computation.5 | async-start | bytes 4718592 | tf_op jit(solution)/shard_map/reduce_scatter | solution.py:65
  136.0 5.8 copy-start
  363.5 9.9 %copy-start.2 = (f32[1024,1024]{1,0:T(8,128)S(1)}, f32[1024,1024]{1,0:T(8,128)}, u32[]{:S(2)}) copy-start(f32[1024,1024]{1,0:T(8,128)} %all-gather.5.cloned.1.call-done) | copy-start | bytes 12582916
  370.2 3.2 copy-start.1
  403.9 181.0 %reduce-scatter.3.cloned.1.call-start = ((), (), s32[]{:S(2)}) async-start(), calls=%async_computation.4 | async-start | bytes 8912896 | tf_op jit(solution)/shard_map/reduce_scatter | solution.py:51
Sparse Core Ops, SparseCore 0:
  10.3 74.0 all-gather.4
  86.1 49.8 all-gather.2
  404.0 81.8 reduce-scatter.4
  488.3 96.5 reduce-scatter.2
where the time goes:
time: 594 us; the launch traced here: 593 us
  waiting for transfers between devices  272 us (46%)
  blocking collectives  178 us (30%)
  matrix products  96.8 us (16%)
  other arithmetic  23.9 us (4%)
  between operations  17.2 us (3%)
    reduce_scatter x1, waiting for transfers between devices, on_device(): lax.psum_scatter(jnp.sum(part_weight, axis=1)[:, None] * page_block - mix...  97.1 us
    all_gather x1, waiting for transfers between devices, on_device(): text_block = lax.all_gather(transcripts, 'row', axis=0, tiled=True)  75 us
    psum x1, blocking collectives, on_device(): total = lax.psum(jnp.sum(col_part), ('row', 'col'))  66.5 us
    psum x1, blocking collectives, on_device(): lax.psum((jnp.sum(centred * centred), jnp.sum(centred * on_diag)), ('row'...  62 us
    reduce_scatter x1, waiting for transfers between devices, on_device(): lax.psum_scatter(folded - jnp.sum(part_weight, axis=0)[:, None] * text_bl...  49.4 us
    all_gather x1, waiting for transfers between devices, on_device(): page_block = lax.all_gather(pages, 'col', axis=0, tiled=True)  49.1 us
    dot_general x1, matrix products, kernel_tile(): lax.dot_general(rows, cols, (((1,), (1,)), ((), ())), precision=lax.Preci...  33.8 us
    dot_general x1, matrix products, on_device(): jnp.dot(part_weight, text_block, precision=lax.Precision.HIGHEST, preferr...  32.5 us
  transfers between devices with their start and end apart: 4, of which 4 were waited for; matrix products, arithmetic and copies ran while one was open for 6% of the time, Pallas kernels for 0%

commit v1 on v0

v1 whole, which is shorter than its diff:
```python
import jax
import jax.numpy as jnp
from jax import lax
from jax.sharding import Mesh, PartitionSpec as P

AXES = ("z", "xh", "y", "xl", "core")
SIZES = (4, 2, 4, 2, 2)
PRECISION = lax.Precision.HIGH


def from_next(x, axis, step):
    n = lax.axis_size(axis)
    return lax.ppermute(x, axis, [(i, (i - step) % n) for i in range(n)])


def from_twin(x):
    return lax.ppermute(x, ("xh", "xl"), [(0, 3), (3, 0), (1, 2), (2, 1)])


def from_side(x):
    return from_next(x, "xl", 1)


def from_core(x):
    return from_next(x, "core", 1)


def gather_ring(own, ring, across):
    half = own.shape[0] // 2
    other = across(own)
    up, down = from_next(own, ring, 1), from_next(own, ring, -1)
    o_up, o_down = from_next(other, ring, 1), from_next(other, ring, -1)
    far = jnp.concatenate([from_next(up[:half], ring, 1), from_next(down[half:], ring, -1)])
    o_far = across(far)
    return [[own, other], [up, o_up], [far, o_far], [down, o_down]]


def reduce_ring(parts, ring, across):
    (own, other), (up, o_up), (far, o_far), (down, o_down) = parts
    half = own.shape[0] // 2
    other = other + from_next(o_up, ring, -1) + from_next(o_down, ring, 1)
    far = far + across(o_far)
    own = own + across(other)
    low = from_next(far[:half], ring, -1)
    high = from_next(far[half:], ring, 1)
    up = jnp.concatenate([up[:half] + low, up[half:]])
    down = jnp.concatenate([down[:half], down[half:] + high])
    return own + from_next(up, ring, -1) + from_next(down, ring, 1)


def ring_total(v, ring):
    lead = v.shape[0]
    step = lead // 4
    out = v
    for e in (1, 2, 3):
        out = out + jnp.roll(from_next(v, ring, e), e * step, axis=0)
    return out


def flip(v, stride):
    shape = v.shape
    w = v.reshape(-1, 2, stride, shape[-1])
    return jnp.concatenate([w[:, 1:], w[:, :1]], axis=1).reshape(shape)


def kernel_tile(rows, cols, inverse):
    cross = lax.dot_general(
        rows, cols, (((1,), (1,)), ((), ())), precision=PRECISION, preferred_element_type=jnp.float32
    )
    first = jnp.sum(rows * rows, axis=1)
    second = jnp.sum(cols * cols, axis=1)
    return jnp.exp(-(first[:, None] + second[None, :] - 2.0 * cross) * inverse)


def merge_ring(mean, spread, weight, ring):
    means = [mean] + [from_next(mean, ring, e) for e in (1, 2, 3)]
    spreads = [spread] + [from_next(spread, ring, e) for e in (1, 2, 3)]
    return merge(means, spreads, weight)


def merge(means, spreads, weight):
    mean = sum(means) / len(means)
    return mean, sum(spreads) + weight * sum((m - mean) ** 2 for m in means), weight * len(means)


def on_device(pages, transcripts, length_scale):
    share = pages.shape[0]
    count = share * 128
    spread_sq = length_scale[0] * length_scale[0]
    inverse = 0.5 / spread_sq
    z, xh, y, xl, core = (lax.axis_index(a) for a in AXES)
    page_parts = gather_ring(pages, "y", from_side)
    page_list = []
    page_ids = []
    for dy in range(4):
        for dx in range(2):
            b = page_parts[dy][dx]
            page_list += [b, from_core(b)]
            for dc in range(2):
                page_ids.append((z * 2 + xh) * 16 + ((y + dy) % 4) * 4 + (xl ^ dx) * 2 + (core ^ dc))
    text_parts = gather_ring(transcripts, "z", from_twin)
    text_list = []
    text_ids = []
    for dz in range(4):
        for dq in range(2):
            text_list.append(text_parts[dz][dq])
            text_ids.append((y * 4 + (xl ^ dq) * 2 + core) * 8 + ((z + dz) % 4) * 2 + (xh ^ dq))
    page_block = jnp.concatenate(page_list)
    text_block = jnp.concatenate(text_list)
    kern = kernel_tile(page_block, text_block, inverse)
    lane = lax.iota(jnp.int32, share)
    row_glob = (jnp.stack(page_ids)[:, None] * share + lane[None, :]).reshape(-1)
    col_glob = (jnp.stack(text_ids)[:, None] * share + lane[None, :]).reshape(-1)
    on_diag = row_glob[:, None] == col_glob[None, :]
    row_sums = jnp.sum(kern, axis=1).reshape(16, share)
    col_sums = jnp.sum(kern, axis=0).reshape(8, share)
    row_sums = row_sums + flip(from_core(row_sums), 1)
    row_sums = row_sums + flip(from_side(row_sums), 2)
    row_sums = ring_total(row_sums, "y")
    col_sums = col_sums + flip(from_twin(col_sums), 1)
    col_sums = ring_total(col_sums, "z")
    rows = row_sums.reshape(-1) / count
    cols = col_sums.reshape(-1) / count
    rest = kern - rows[:, None] - cols[None, :]
    mean = jnp.mean(rest)
    spread = jnp.sum((rest - mean) ** 2)
    trace = jnp.sum(jnp.where(on_diag, rest, 0.0))
    weight = float(kern.size)
    line = jnp.stack([mean, spread, trace])
    stat = jnp.zeros((8, 128), jnp.float32).at[0, :3].set(line)

    def join(stats, weight):
        n = len(stats)
        total = sum(stats)
        mean = total[0, 0] / n
        extra = weight * sum((s[0, 0] - mean) ** 2 for s in stats)
        return total.at[0, 0].set(mean).at[0, 1].add(extra), weight * n

    stat, weight = join([stat, from_core(stat)], weight)
    stat, weight = join([stat, from_side(stat)], weight)
    stat, weight = join([stat] + [from_next(stat, "y", e) for e in (1, 2, 3)], weight)
    stat, weight = join([stat, from_next(stat, "xh", 1)], weight)
    stat, weight = join([stat] + [from_next(stat, "z", e) for e in (1, 2, 3)], weight)
    grand = -stat[0, 0]
    frob_sq = stat[0, 1]
    align = stat[0, 2] + count * grand
    frob = jnp.sqrt(frob_sq)
    loss_scale = 4.0 * count
    weights = (
        loss_scale * align / (frob * frob_sq) * (rest + grand)
        - loss_scale / frob * (on_diag.astype(jnp.float32) - 1.0 / count)
    ) * kern
    mixed = jnp.dot(weights, text_block, precision=PRECISION, preferred_element_type=jnp.float32)
    page_part = jnp.sum(weights, axis=1)[:, None] * page_block - mixed
    page_part = page_part.reshape(4, 2, 2, share, -1)
    folded = lax.dot_general(
        weights, page_block, (((0,), (0,)), ((), ())), precision=PRECISION, preferred_element_type=jnp.float32
    )
    text_part = folded - jnp.sum(weights, axis=0)[:, None] * text_block
    text_part = text_part.reshape(4, 2, share, -1)
    page_sum = reduce_ring(
        [[page_part[dy, dx, 0] + from_core(page_part[dy, dx, 1]) for dx in range(2)] for dy in range(4)],
        "y",
        from_side,
    )
    text_sum = reduce_ring([[text_part[dz, dq] for dq in range(2)] for dz in range(4)], "z", from_twin)
    return (-page_sum / spread_sq, text_sum / spread_sq)


def solution(mesh):
    grid = Mesh(mesh.devices.reshape(SIZES), AXES)
    row, col = ("z", "xh"), ("y", "xl", "core")
    placed = (P(row + col, None), P(col + row, None), P())
    return jax.shard_map(
        on_device,
        mesh=grid,
        in_specs=placed,
        out_specs=(P(row + col, None), P(col + row, None)),
        check_vma=False,
    )
```

time: 594 us -> 324 us (0.55)
  waiting for transfers between devices: 272 us -> 90.9 us
  blocking collectives: 178 us -> 0 us
  starting transfers between devices: 0.16 us -> 62.6 us
  local copies, waits for them, and re-layouts: 4.83 us -> 54.9 us
  matrix products: 96.8 us -> 66.7 us
    psum x4 -> x0, blocking collectives: 178 us -> none  [the longest x1 66.5 us: on_device(): total = lax.psum(jnp.sum(col_part), ('row', 'col'))]
    reduce_scatter x2 -> x0, waiting for transfers between devices: 147 us -> none  [the longest x1 97.1 us: on_device(): lax.psum_scatter(jnp.sum(part_weight, axis=1)[:, None] * page_block - mix...]
    all_gather x2 -> x0, waiting for transfers between devices: 124 us -> none  [the longest x1 75 us: on_device(): text_block = lax.all_gather(transcripts, 'row', axis=0, tiled=True)]
    ppermute x0 -> x66, waiting for transfers between devices: none -> 90.9 us  [the longest x61 83.4 us: from_next(): return lax.ppermute(x, axis, [(i, (i - step) % n) for i in range(n)])]
    ppermute x0 -> x66, starting transfers between devices: none -> 62.6 us  [the longest x61 55.5 us: from_next(): return lax.ppermute(x, axis, [(i, (i - step) % n) for i in range(n)])]
    dot_general x3, matrix products: 96.8 us -> 66.7 us  [the longest x1 27.5 us: kernel_tile(): lax.dot_general(rows, cols, (((1,), (1,)), ((), ())), precision=PRECISION...]
    unnamed x6 -> x37, local copies, waits for them, and re-layouts: 4.83 us -> 21.6 us
    slice x0 -> x36, local copies, waits for them, and re-layouts: none -> 10.7 us  [the longest x13 6.66 us: join(): extra = weight * sum(((s[0, 0] - mean) ** 2 for s in stats))]
  transfers between devices with their start and end apart: 4 -> 66, of which waited for: 4 -> 32; matrix products, arithmetic and copies ran while one was open for 6% -> 15% of each run, Pallas kernels for 0% -> 0%
where the time goes in v1:
time: 324 us; the launch traced here: 322 us
  waiting for transfers between devices  90.9 us (28%)
  matrix products  66.7 us (21%)
  starting transfers between devices  62.6 us (19%)
  local copies, waits for them, and re-layouts  54.9 us (17%)
  other arithmetic  27 us (8%)
  between operations  20.1 us (6%)
    ppermute x61, waiting for transfers between devices, from_next(): return lax.ppermute(x, axis, [(i, (i - step) % n) for i in range(n)])  83.4 us
    ppermute x61, starting transfers between devices, from_next(): return lax.ppermute(x, axis, [(i, (i - step) % n) for i in range(n)])  55.5 us
    dot_general x1, matrix products, kernel_tile(): lax.dot_general(rows, cols, (((1,), (1,)), ((), ())), precision=PRECISION...  27.5 us
    dot_general x1, matrix products, on_device(): jnp.dot(weights, text_block, precision=PRECISION, preferred_element_type=...  21.9 us
    unnamed x37, local copies, waits for them, and re-layouts  21.6 us
    dot_general x1, matrix products, on_device(): lax.dot_general(weights, page_block, (((0,), (0,)), ((), ())), precision=...  17.3 us
    another operation x7, local copies, waits for them, and re-layouts  9.72 us
    ppermute x5, waiting for transfers between devices, from_twin(): return lax.ppermute(x, ('xh', 'xl'), [(0, 3), (3, 0), (1, 2), (2, 1)])  7.41 us
  transfers between devices with their start and end apart: 66, of which 32 were waited for; matrix products, arithmetic and copies ran while one was open for 15% of the time, Pallas kernels for 0%

profile of v1, /device:TPU:0, one launch (start us, length us, event | category | flops | bytes accessed | tf_op | source)
XLA Modules:
  0.0 322.1 jit_solution(2810358790519151847)
XLA Ops:
  2.3 3.0 collective-permute-start.3
  5.3 4.0 %collective-permute-start.17 = (f32[128,1024]{1,0:T(8,128)}, f32[128,1024]{1,0:T(8,128)S(1)}, u32[]{:S(2)}, u32[]{:S(2)}) collective-permute-start(f32[128,1024]{1,0:T(8,128)} %param.26), channel_id=1, source_target_pairs={{0,96},{32,0},{64,32},{96,64},{1,97},{33,1},{65,33},{97,65},{2,98}... | collective-permute-start | bytes 1572872 | tf_op jit(solution)/shard_map/ppermute | solution.py:13
  9.6 4.8 %collective-permute-done.1 = f32[128,1024]{1,0:T(8,128)S(1)} collective-permute-done((f32[128,1024]{1,0:T(8,128)}, f32[128,1024]{1,0:T(8,128)S(1)}, u32[]{:S(2)}, u32[]{:S(2)}) %collective-permute-start.1) | collective-permute-done | bytes 524320 | tf_op jit(solution)/shard_map/ppermute | solution.py:13
  14.4 1.8 collective-permute-start.8
  16.2 2.8 collective-permute-start.16
  19.0 1.9 constant_dynamic-update-slice_fusion.18
  22.6 1.9 constant_dynamic-update-slice_fusion.27
  26.2 4.1 %collective-permute-start.19 = (f32[64,1024]{1,0:T(8,128)S(1)}, f32[64,1024]{1,0:T(8,128)S(1)}, u32[]{:S(2)}, u32[]{:S(2)}) collective-permute-start(f32[64,1024]{1,0:T(8,128)S(1)} %slice.540), channel_id=1, source_target_pairs={{0,96},{32,0},{64,32},{96,64},{1,97},{33,1},{65,33},{97,65},{2,98}... | collective-permute-start | bytes 786440 | tf_op jit(solution)/shard_map/ppermute | solution.py:13
  31.7 1.9 constant_dynamic-update-slice_fusion.26
  34.5 2.0 collective-permute-done.19
  45.2 1.9 constant_dynamic-update-slice_fusion.12
  48.0 2.0 collective-permute-start.22
  50.7 9.3 %collective-permute-done.14 = f32[128,1024]{1,0:T(8,128)S(1)} collective-permute-done((f32[128,1024]{1,0:T(8,128)S(1)}, f32[128,1024]{1,0:T(8,128)S(1)}, u32[]{:S(2)}, u32[]{:S(2)}) %collective-permute-start.14) | collective-permute-done | bytes 524320 | tf_op jit(solution)/shard_map/ppermute | solution.py:13
  65.2 9.9 %collective-permute-done.11 = f32[128,1024]{1,0:T(8,128)S(1)} collective-permute-done((f32[128,1024]{1,0:T(8,128)S(1)}, f32[128,1024]{1,0:T(8,128)S(1)}, u32[]{:S(2)}, u32[]{:S(2)}) %collective-permute-start.11) | collective-permute-done | bytes 524320 | tf_op jit(solution)/shard_map/ppermute | solution.py:13
  76.1 2.5 multiply_reduce_fusion.2
  79.7 3.3 %copy-done.3 = f32[1024,1024]{1,0:T(8,128)S(1)} copy-done((f32[1024,1024]{1,0:T(8,128)S(1)}, f32[1024,1024]{1,0:T(8,128)}, u32[]{:S(2)}) %copy-start.3) | copy-done | bytes 4194328
  83.0 27.5 %fusion.40 = (f32[2048]{0:T(1024)S(1)}, f32[1024]{0:T(1024)S(1)}, f32[2048,1024]{1,0:T(8,128)S(1)}) fusion(f32[]{:T(128)S(6)} %div.49, f32[2048,1024]{1,0:T(8,128)S(1)} %constant_dynamic-update-slice_fusion.2, f32[1024,1024]{1,0:T(8,128)S(1)} %copy-done.3, f32[1024]{0:T(1024)S(1)} %multiply_reduce_fusion.2, f32[2048]{0:T(1024)S(1)} %multiply_reduce_fusion.1), kind=kOutput, calls=%fused_computation.129 | convolution fusion | flops 12899578880 | bytes 20996100 | tf_op jit(solution)/shard_map/dot_general | solution.py:67
  111.2 4.2 %collective-permute-done.29 = f32[8,128]{1,0:T(8,128)S(1)} collective-permute-done((f32[8,128]{1,0:T(8,128)S(1)}, f32[8,128]{1,0:T(8,128)S(1)}, u32[]{:S(2)}, u32[]{:S(2)}) %collective-permute-start.29) | collective-permute-done | bytes 4128 | tf_op jit(solution)/shard_map/ppermute | solution.py:17
  116.3 2.2 collective-permute-start.32
  124.3 2.7 collective-permute-start.26
  128.7 3.0 fusion.5
  132.4 6.6 %multiply_reduce_fusion = (f32[]{:T(128)}, f32[]{:T(128)}) fusion(f32[2048,1024]{1,0:T(8,128)} %copy-done, f32[]{:T(128)} %div.54, f32[1024]{0:T(1024)S(1)} %fusion.38, f32[2048]{0:T(1024)S(1)} %fusion.34, s32[1024]{0:T(1024)S(1)} %add_bitcast_fusion.1, s32[2048]{0:T(1024)S(1)} %add_bitcast_fusion), kind=kLoop, calls=%fused_computation.8 | loop fusion | flops 16777214 | bytes 8413196 | tf_op jit(solution)/shard_map/reduce_sum | solution.py:126
  144.6 1.8 dynamic-slice.78
  149.3 2.9 collective-permute-done.34
  155.2 1.8 dynamic-slice.79
  159.1 3.2 collective-permute-start.35
  163.8 3.6 %collective-permute-done.36 = f32[8,128]{1,0:T(8,128)S(1)} collective-permute-done((f32[8,128]{1,0:T(8,128)S(1)}, f32[8,128]{1,0:T(8,128)S(1)}, u32[]{:S(2)}, u32[]{:S(2)}) %collective-permute-start.36) | collective-permute-done | bytes 4128 | tf_op jit(solution)/shard_map/ppermute | solution.py:13
  173.4 1.8 dynamic-slice.80
  177.2 2.3 collective-permute-start.38
  180.0 2.4 collective-permute-done.38
  185.5 1.8 dynamic-slice.81
  190.5 2.0 collective-permute-start.40
  193.1 2.6 collective-permute-done.40
  202.7 1.8 dynamic-slice.82
  210.4 6.7 %fusion.39 = (f32[1024]{0:T(1024)S(1)}, f32[2048]{0:T(1024)S(1)}, f32[2048,1024]{1,0:T(8,128)S(1)}) fusion(f32[2048,1024]{1,0:T(8,128)} %copy-done, s32[1024]{0:T(1024)S(1)} %add_bitcast_fusion.1, s32[2048]{0:T(1024)S(1)} %add_bitcast_fusion, f32[]{:T(128)S(6)} %div.61, f32[]{:T(128)} %bitcast.51, f32[1024]{0:T(1024)S(1)} %fusion.38, f32[2048]{0:T(1024)S(1)} %fusion.34, ...), kind=kLoop, calls=%fused_computation.128 | loop fusion | flops 25162752 | bytes 16814092 | tf_op jit(solution)/shard_map/reduce_sum | solution.py:159
  217.2 21.9 %multiply_subtract_fusion = f32[2048,1024]{1,0:T(8,128)S(1)} fusion(f32[2048,1024]{1,0:T(8,128)} %copy-done.2, f32[2048]{0:T(1024)S(1)} %get-tuple-element.137, f32[2048,1024]{1,0:T(8,128)S(1)} %get-tuple-element.140, f32[1024,1024]{1,0:T(8,128)} %constant_dynamic-update-slice_fusion.19), kind=kOutput, calls=%fused_computation.7 | convolution fusion | flops 12889096192 | bytes 29368320 | tf_op jit(solution)/shard_map/dot_general | solution.py:153
  245.6 3.0 collective-permute-start.47
  248.6 17.3 %multiply_subtract_fusion.1 = f32[1024,1024]{1,0:T(8,128)} fusion(f32[1024,1024]{1,0:T(8,128)} %constant_dynamic-update-slice_fusion.19, f32[1024]{0:T(1024)S(1)} %get-tuple-element.136, f32[2048,1024]{1,0:T(8,128)S(1)} %get-tuple-element.140, f32[2048,1024]{1,0:T(8,128)S(1)} %bitcast.207), kind=kOutput, calls=%fused_computation.13 | convolution fusion | flops 12886999040 | bytes 25169920 | tf_op jit(solution)/shard_map/dot_general | solution.py:156
  267.7 3.2 collective-permute-start.59
  274.3 8.0 %collective-permute-done.58 = f32[128,1024]{1,0:T(8,128)S(1)} collective-permute-done((f32[128,1024]{1,0:T(8,128)S(1)}, f32[128,1024]{1,0:T(8,128)S(1)}, u32[]{:S(2)}, u32[]{:S(2)}) %collective-permute-start.58) | collective-permute-done | bytes 524320 | tf_op jit(solution)/shard_map/ppermute | solution.py:13
  282.3 2.7 collective-permute-done.61
  285.3 3.2 %collective-permute-start.64 = (f32[64,1024]{1,0:T(8,128)S(1)}, f32[64,1024]{1,0:T(8,128)S(1)}, u32[]{:S(2)}, u32[]{:S(2)}) collective-permute-start(f32[64,1024]{1,0:T(8,128)S(1)} %get-tuple-element.165), channel_id=1, source_target_pairs={{0,96},{32,0},{64,32},{96,64},{1,97},{33,1},{65,33},{97,65},{2,98}... | collective-permute-start | bytes 786440 | tf_op jit(solution)/shard_map/ppermute | solution.py:13
  289.7 5.0 %collective-permute-done.52 = f32[128,1024]{1,0:T(8,128)S(1)} collective-permute-done((f32[128,1024]{1,0:T(8,128)S(1)}, f32[128,1024]{1,0:T(8,128)S(1)}, u32[]{:S(2)}, u32[]{:S(2)}) %collective-permute-start.52) | collective-permute-done | bytes 524320 | tf_op jit(solution)/shard_map/ppermute | solution.py:13
  295.0 3.4 %collective-permute-start.56 = (f32[64,1024]{1,0:T(8,128)S(1)}, f32[64,1024]{1,0:T(8,128)S(1)}, u32[]{:S(2)}, u32[]{:S(2)}) collective-permute-start(f32[64,1024]{1,0:T(8,128)S(1)} %get-tuple-element.169), channel_id=1, source_target_pairs={{0,12},{4,0},{8,4},{12,8},{1,13},{5,1},{9,5},{13,9},{2,14},{6,2},{... | collective-permute-start | bytes 786440 | tf_op jit(solution)/shard_map/ppermute | solution.py:13
  298.7 3.9 %collective-permute-done.53 = f32[64,1024]{1,0:T(8,128)S(1)} collective-permute-done((f32[64,1024]{1,0:T(8,128)S(1)}, f32[64,1024]{1,0:T(8,128)S(1)}, u32[]{:S(2)}, u32[]{:S(2)}) %collective-permute-start.53) | collective-permute-done | bytes 262176 | tf_op jit(solution)/shard_map/ppermute | solution.py:13
  303.2 7.6 %collective-permute-done.63 = f32[128,1024]{1,0:T(8,128)S(1)} collective-permute-done((f32[128,1024]{1,0:T(8,128)S(1)}, f32[128,1024]{1,0:T(8,128)S(1)}, u32[]{:S(2)}, u32[]{:S(2)}) %collective-permute-start.63) | collective-permute-done | bytes 524320 | tf_op jit(solution)/shard_map/ppermute | solution.py:13
  311.1 2.1 collective-permute-done.65
  315.0 5.9 %collective-permute-done.57 = f32[128,1024]{1,0:T(8,128)S(1)} collective-permute-done((f32[128,1024]{1,0:T(8,128)S(1)}, f32[128,1024]{1,0:T(8,128)S(1)}, u32[]{:S(2)}, u32[]{:S(2)}) %collective-permute-start.57) | collective-permute-done | bytes 524320 | tf_op jit(solution)/shard_map/ppermute | solution.py:13
  (223 shorter events, 76.4 us)
Async XLA Ops:
  0.6 13.8 %collective-permute-start.1 = (f32[128,1024]{1,0:T(8,128)}, f32[128,1024]{1,0:T(8,128)S(1)}, u32[]{:S(2)}, u32[]{:S(2)}) collective-permute-start(f32[128,1024]{1,0:T(8,128)} %param.25), channel_id=1, source_target_pairs={{0,2},{2,0},{1,3},{3,1},{4,6},{6,4},{5,7},{7,5},{8,10},{10,8},{9,1... | collective-permute-start | bytes 1572872 | tf_op jit(solution)/shard_map/ppermute | solution.py:13
  2.3 14.0 %collective-permute-start = (f32[128,1024]{1,0:T(8,128)}, f32[128,1024]{1,0:T(8,128)S(1)}, u32[]{:S(2)}, u32[]{:S(2)}) collective-permute-start(f32[128,1024]{1,0:T(8,128)} %param.25), channel_id=1, source_target_pairs={{0,1},{1,0},{2,3},{3,2},{4,5},{5,4},{6,7},{7,6},{8,9},{9,8},{10,11... | collective-permute-start | bytes 1572872 | tf_op jit(solution)/shard_map/ppermute | solution.py:13
  2.3 23.9 %collective-permute-start.3 = (f32[128,1024]{1,0:T(8,128)}, f32[128,1024]{1,0:T(8,128)S(1)}, u32[]{:S(2)}, u32[]{:S(2)}) collective-permute-start(f32[128,1024]{1,0:T(8,128)} %param.25), channel_id=1, source_target_pairs={{0,12},{4,0},{8,4},{12,8},{1,13},{5,1},{9,5},{13,9},{2,14},{6,2},{... | collective-permute-start | bytes 1572872 | tf_op jit(solution)/shard_map/ppermute | solution.py:13
  5.3 15.9 %collective-permute-start.17 = (f32[128,1024]{1,0:T(8,128)}, f32[128,1024]{1,0:T(8,128)S(1)}, u32[]{:S(2)}, u32[]{:S(2)}) collective-permute-start(f32[128,1024]{1,0:T(8,128)} %param.26), channel_id=1, source_target_pairs={{0,96},{32,0},{64,32},{96,64},{1,97},{33,1},{65,33},{97,65},{2,98}... | collective-permute-start | bytes 1572872 | tf_op jit(solution)/shard_map/ppermute | solution.py:13
  9.3 15.8 %collective-permute-start.20 = (f32[128,1024]{1,0:T(8,128)}, f32[128,1024]{1,0:T(8,128)S(1)}, u32[]{:S(2)}, u32[]{:S(2)}) collective-permute-start(f32[128,1024]{1,0:T(8,128)} %param.26), channel_id=1, source_target_pairs={{0,32},{32,64},{64,96},{96,0},{1,33},{33,65},{65,97},{97,1},{2,34}... | collective-permute-start | bytes 1572872 | tf_op jit(solution)/shard_map/ppermute | solution.py:13
  14.4 15.8 %collective-permute-start.8 = (f32[128,1024]{1,0:T(8,128)}, f32[128,1024]{1,0:T(8,128)S(1)}, u32[]{:S(2)}, u32[]{:S(2)}) collective-permute-start(f32[128,1024]{1,0:T(8,128)} %param.25), channel_id=1, source_target_pairs={{0,4},{4,8},{8,12},{12,0},{1,5},{5,9},{9,13},{13,1},{2,6},{6,10},{... | collective-permute-start | bytes 1572872 | tf_op jit(solution)/shard_map/ppermute | solution.py:13
  16.2 15.5 %collective-permute-start.16 = (f32[128,1024]{1,0:T(8,128)}, f32[128,1024]{1,0:T(8,128)}, u32[]{:S(2)}, u32[]{:S(2)}) collective-permute-start(f32[128,1024]{1,0:T(8,128)} %param.26), channel_id=1, source_target_pairs={{0,18},{18,0},{2,16},{16,2},{1,19},{19,1},{3,17},{17,3},{4,22},{22... | collective-permute-start | bytes 1572872 | tf_op jit(solution)/shard_map/ppermute | solution.py:17
  21.2 19.0 %collective-permute-start.5 = (f32[128,1024]{1,0:T(8,128)S(1)}, f32[128,1024]{1,0:T(8,128)}, u32[]{:S(2)}, u32[]{:S(2)}) collective-permute-start(f32[128,1024]{1,0:T(8,128)S(1)} %collective-permute-done.1), channel_id=1, source_target_pairs={{0,12},{4,0},{8,4},{12,8},{1,13},{5,1},{9,5},{13,9},{2,14},{6,2},{... | collective-permute-start | bytes 1572872 | tf_op jit(solution)/shard_map/ppermute | solution.py:13
  25.2 15.2 %collective-permute-start.2 = (f32[128,1024]{1,0:T(8,128)S(1)}, f32[128,1024]{1,0:T(8,128)S(1)}, u32[]{:S(2)}, u32[]{:S(2)}) collective-permute-start(f32[128,1024]{1,0:T(8,128)S(1)} %collective-permute-done.1), channel_id=1, source_target_pairs={{0,1},{1,0},{2,3},{3,2},{4,5},{5,4},{6,7},{7,6},{8,9},{9,8},{10,11... | collective-permute-start | bytes 1572872 | tf_op jit(solution)/shard_map/ppermute | solution.py:13
  26.2 10.3 %collective-permute-start.19 = (f32[64,1024]{1,0:T(8,128)S(1)}, f32[64,1024]{1,0:T(8,128)S(1)}, u32[]{:S(2)}, u32[]{:S(2)}) collective-permute-start(f32[64,1024]{1,0:T(8,128)S(1)} %slice.540), channel_id=1, source_target_pairs={{0,96},{32,0},{64,32},{96,64},{1,97},{33,1},{65,33},{97,65},{2,98}... | collective-permute-start | bytes 786440 | tf_op jit(solution)/shard_map/ppermute | solution.py:13
  30.3 9.6 %collective-permute-start.21 = (f32[64,1024]{1,0:T(8,128)S(1)}, f32[64,1024]{1,0:T(8,128)S(1)}, u32[]{:S(2)}, u32[]{:S(2)}) collective-permute-start(f32[64,1024]{1,0:T(8,128)S(1)} %slice.541), channel_id=1, source_target_pairs={{0,32},{32,64},{64,96},{96,0},{1,33},{33,65},{65,97},{97,1},{2,34}... | collective-permute-start | bytes 786440 | tf_op jit(solution)/shard_map/ppermute | solution.py:13
  31.7 12.0 %collective-permute-start.4 = (f32[128,1024]{1,0:T(8,128)S(1)}, f32[128,1024]{1,0:T(8,128)S(1)}, u32[]{:S(2)}, u32[]{:S(2)}) collective-permute-start(f32[128,1024]{1,0:T(8,128)S(1)} %collective-permute-done.3), channel_id=1, source_target_pairs={{0,1},{1,0},{2,3},{3,2},{4,5},{5,4},{6,7},{7,6},{8,9},{9,8},{10,11... | collective-permute-start | bytes 1572872 | tf_op jit(solution)/shard_map/ppermute | solution.py:13
  36.5 11.5 %collective-permute-start.7 = (f32[64,1024]{1,0:T(8,128)S(1)}, f32[64,1024]{1,0:T(8,128)S(1)}, u32[]{:S(2)}, u32[]{:S(2)}) collective-permute-start(f32[64,1024]{1,0:T(8,128)S(1)} %slice.538), channel_id=1, source_target_pairs={{0,12},{4,0},{8,4},{12,8},{1,13},{5,1},{9,5},{13,9},{2,14},{6,2},{... | collective-permute-start | bytes 786440 | tf_op jit(solution)/shard_map/ppermute | solution.py:13
  39.9 10.8 %collective-permute-start.9 = (f32[64,1024]{1,0:T(8,128)S(1)}, f32[64,1024]{1,0:T(8,128)S(1)}, u32[]{:S(2)}, u32[]{:S(2)}) collective-permute-start(f32[64,1024]{1,0:T(8,128)S(1)} %slice.539), channel_id=1, source_target_pairs={{0,4},{4,8},{8,12},{12,0},{1,5},{5,9},{9,13},{13,1},{2,6},{6,10},{... | collective-permute-start | bytes 786440 | tf_op jit(solution)/shard_map/ppermute | solution.py:13
  40.3 6.8 %collective-permute-start.6 = (f32[128,1024]{1,0:T(8,128)}, f32[128,1024]{1,0:T(8,128)S(1)}, u32[]{:S(2)}, u32[]{:S(2)}) collective-permute-start(f32[128,1024]{1,0:T(8,128)} %collective-permute-done.5), channel_id=1, source_target_pairs={{0,1},{1,0},{2,3},{3,2},{4,5},{5,4},{6,7},{7,6},{8,9},{9,8},{10,11... | collective-permute-start | bytes 1572872 | tf_op jit(solution)/shard_map/ppermute | solution.py:13
  40.3 19.6 %collective-permute-start.14 = (f32[128,1024]{1,0:T(8,128)S(1)}, f32[128,1024]{1,0:T(8,128)S(1)}, u32[]{:S(2)}, u32[]{:S(2)}) collective-permute-start(f32[128,1024]{1,0:T(8,128)S(1)} %collective-permute-done.1), channel_id=1, source_target_pairs={{0,4},{4,8},{8,12},{12,0},{1,5},{5,9},{9,13},{13,1},{2,6},{6,10},{... | collective-permute-start | bytes 1572872 | tf_op jit(solution)/shard_map/ppermute | solution.py:13
  43.7 17.1 %collective-permute-start.18 = (f32[128,1024]{1,0:T(8,128)}, f32[128,1024]{1,0:T(8,128)S(1)}, u32[]{:S(2)}, u32[]{:S(2)}) collective-permute-start(f32[128,1024]{1,0:T(8,128)} %collective-permute-done.16), channel_id=1, source_target_pairs={{0,96},{32,0},{64,32},{96,64},{1,97},{33,1},{65,33},{97,65},{2,98}... | collective-permute-start | bytes 1572872 | tf_op jit(solution)/shard_map/ppermute | solution.py:13
  47.1 31.8 %collective-permute-start.13 = (f32[128,1024]{1,0:T(8,128)S(1)}, f32[128,1024]{1,0:T(8,128)S(1)}, u32[]{:S(2)}, u32[]{:S(2)}) collective-permute-start(f32[128,1024]{1,0:T(8,128)S(1)} %collective-permute-done.8), channel_id=1, source_target_pairs={{0,1},{1,0},{2,3},{3,2},{4,5},{5,4},{6,7},{7,6},{8,9},{9,8},{10,11... | collective-permute-start | bytes 1572872 | tf_op jit(solution)/shard_map/ppermute | solution.py:13
  48.0 15.5 %collective-permute-start.22 = (f32[128,1024]{1,0:T(8,128)S(1)}, f32[128,1024]{1,0:T(8,128)S(1)}, u32[]{:S(2)}, u32[]{:S(2)}) collective-permute-start(f32[128,1024]{1,0:T(8,128)S(1)} %pad_maximum_fusion), channel_id=1, source_target_pairs={{0,18},{18,0},{2,16},{16,2},{1,19},{19,1},{3,17},{17,3},{4,22},{22... | collective-permute-start | bytes 1572872 | tf_op jit(solution)/shard_map/ppermute | solution.py:17
  50.7 24.6 %collective-permute-start.23 = (f32[128,1024]{1,0:T(8,128)}, f32[128,1024]{1,0:T(8,128)S(1)}, u32[]{:S(2)}, u32[]{:S(2)}) collective-permute-start(f32[128,1024]{1,0:T(8,128)} %collective-permute-done.16), channel_id=1, source_target_pairs={{0,32},{32,64},{64,96},{96,0},{1,33},{33,65},{65,97},{97,1},{2,34}... | collective-permute-start | bytes 1572872 | tf_op jit(solution)/shard_map/ppermute | solution.py:13
  60.0 19.1 %collective-permute-start.15 = (f32[128,1024]{1,0:T(8,128)S(1)}, f32[128,1024]{1,0:T(8,128)S(1)}, u32[]{:S(2)}, u32[]{:S(2)}) collective-permute-start(f32[128,1024]{1,0:T(8,128)S(1)} %collective-permute-done.14), channel_id=1, source_target_pairs={{0,1},{1,0},{2,3},{3,2},{4,5},{5,4},{6,7},{7,6},{8,9},{9,8},{10,11... | collective-permute-start | bytes 1572872 | tf_op jit(solution)/shard_map/ppermute | solution.py:13
  60.7 14.3 %collective-permute-start.11 = (f32[128,1024]{1,0:T(8,128)S(1)}, f32[128,1024]{1,0:T(8,128)S(1)}, u32[]{:S(2)}, u32[]{:S(2)}) collective-permute-start(f32[128,1024]{1,0:T(8,128)S(1)} %get-tuple-element.172), channel_id=1, source_target_pairs={{0,2},{2,0},{1,3},{3,1},{4,6},{6,4},{5,7},{7,5},{8,10},{10,8},{9,1... | collective-permute-start | bytes 1572872 | tf_op jit(solution)/shard_map/ppermute | solution.py:13
  63.5 15.2 %collective-permute-start.10 = (f32[128,1024]{1,0:T(8,128)S(1)}, f32[128,1024]{1,0:T(8,128)S(1)}, u32[]{:S(2)}, u32[]{:S(2)}) collective-permute-start(f32[128,1024]{1,0:T(8,128)S(1)} %get-tuple-element.172), channel_id=1, source_target_pairs={{0,1},{1,0},{2,3},{3,2},{4,5},{5,4},{6,7},{7,6},{8,9},{9,8},{10,11... | collective-permute-start | bytes 1572872 | tf_op jit(solution)/shard_map/ppermute | solution.py:13
  110.7 8.8 %collective-permute-start.24 = (f32[16,128]{1,0:T(8,128)S(1)}, f32[16,128]{1,0:T(8,128)S(1)}, u32[]{:S(2)}, u32[]{:S(2)}) collective-permute-start(f32[16,128]{1,0:T(8,128)S(1)} %bitcast.221), channel_id=1, source_target_pairs={{0,1},{1,0},{2,3},{3,2},{4,5},{5,4},{6,7},{7,6},{8,9},{9,8},{10,11... | collective-permute-start | bytes 24584 | tf_op jit(solution)/shard_map/ppermute | solution.py:13
  115.5 5.2 %collective-permute-start.31 = (f32[8,128]{1,0:T(8,128)S(1)}, f32[8,128]{1,0:T(8,128)S(1)}, u32[]{:S(2)}, u32[]{:S(2)}) collective-permute-start(f32[8,128]{1,0:T(8,128)S(1)} %bitcast_add_fusion), channel_id=1, source_target_pairs={{0,64},{32,96},{64,0},{96,32},{1,65},{33,97},{65,1},{97,33},{2,66}... | collective-permute-start | bytes 12296 | tf_op jit(solution)/shard_map/ppermute | solution.py:13
  123.3 5.2 %collective-permute-start.27 = (f32[16,128]{1,0:T(8,128)S(1)}, f32[16,128]{1,0:T(8,128)S(1)}, u32[]{:S(2)}, u32[]{:S(2)}) collective-permute-start(f32[16,128]{1,0:T(8,128)S(1)} %fusion.58), channel_id=1, source_target_pairs={{0,8},{4,12},{8,0},{12,4},{1,9},{5,13},{9,1},{13,5},{2,10},{6,14},... | collective-permute-start | bytes 24584 | tf_op jit(solution)/shard_map/ppermute | solution.py:13
  177.2 5.2 %collective-permute-start.38 = (f32[8,128]{1,0:T(8,128)S(1)}, f32[8,128]{1,0:T(8,128)S(1)}, u32[]{:S(2)}, u32[]{:S(2)}) collective-permute-start(f32[8,128]{1,0:T(8,128)S(1)} %scatter-add.20), channel_id=1, source_target_pairs={{0,16},{16,0},{1,17},{17,1},{2,18},{18,2},{3,19},{19,3},{4,20},{20... | collective-permute-start | bytes 12296 | tf_op jit(solution)/shard_map/ppermute | solution.py:13
  241.2 26.4 %collective-permute-start.49 = (f32[128,1024]{1,0:T(8,128)}, f32[128,1024]{1,0:T(8,128)S(1)}, u32[]{:S(2)}, u32[]{:S(2)}) collective-permute-start(f32[128,1024]{1,0:T(8,128)} %get-tuple-element.145), channel_id=1, source_target_pairs={{0,1},{1,0},{2,3},{3,2},{4,5},{5,4},{6,7},{7,6},{8,9},{9,8},{10,11... | collective-permute-start | bytes 1572872 | tf_op jit(solution)/shard_map/ppermute | solution.py:13
  241.7 26.0 %collective-permute-start.51 = (f32[128,1024]{1,0:T(8,128)}, f32[128,1024]{1,0:T(8,128)S(1)}, u32[]{:S(2)}, u32[]{:S(2)}) collective-permute-start(f32[128,1024]{1,0:T(8,128)} %get-tuple-element.143), channel_id=1, source_target_pairs={{0,1},{1,0},{2,3},{3,2},{4,5},{5,4},{6,7},{7,6},{8,9},{9,8},{10,11... | collective-permute-start | bytes 1572872 | tf_op jit(solution)/shard_map/ppermute | solution.py:13
  242.6 28.3 %collective-permute-start.55 = (f32[128,1024]{1,0:T(8,128)}, f32[128,1024]{1,0:T(8,128)S(1)}, u32[]{:S(2)}, u32[]{:S(2)}) collective-permute-start(f32[128,1024]{1,0:T(8,128)} %get-tuple-element.142), channel_id=1, source_target_pairs={{0,1},{1,0},{2,3},{3,2},{4,5},{5,4},{6,7},{7,6},{8,9},{9,8},{10,11... | collective-permute-start | bytes 1572872 | tf_op jit(solution)/shard_map/ppermute | solution.py:13
  245.2 27.9 %collective-permute-start.45 = (f32[128,1024]{1,0:T(8,128)}, f32[128,1024]{1,0:T(8,128)S(1)}, u32[]{:S(2)}, u32[]{:S(2)}) collective-permute-start(f32[128,1024]{1,0:T(8,128)} %get-tuple-element.153), channel_id=1, source_target_pairs={{0,4},{4,8},{8,12},{12,0},{1,5},{5,9},{9,13},{13,1},{2,6},{6,10},{... | collective-permute-start | bytes 1572872 | tf_op jit(solution)/shard_map/ppermute | solution.py:13
  245.6 27.7 %collective-permute-start.47 = (f32[128,1024]{1,0:T(8,128)}, f32[128,1024]{1,0:T(8,128)S(1)}, u32[]{:S(2)}, u32[]{:S(2)}) collective-permute-start(f32[128,1024]{1,0:T(8,128)} %get-tuple-element.154), channel_id=1, source_target_pairs={{0,12},{4,0},{8,4},{12,8},{1,13},{5,1},{9,5},{13,9},{2,14},{6,2},{... | collective-permute-start | bytes 1572872 | tf_op jit(solution)/shard_map/ppermute | solution.py:13
  267.6 14.7 %collective-permute-start.58 = (f32[128,1024]{1,0:T(8,128)S(1)}, f32[128,1024]{1,0:T(8,128)S(1)}, u32[]{:S(2)}, u32[]{:S(2)}) collective-permute-start(f32[128,1024]{1,0:T(8,128)S(1)} %get-tuple-element.157), channel_id=1, source_target_pairs={{0,32},{32,64},{64,96},{96,0},{1,33},{33,65},{65,97},{97,1},{2,34}... | collective-permute-start | bytes 1572872 | tf_op jit(solution)/shard_map/ppermute | solution.py:13
  267.7 14.6 %collective-permute-start.59 = (f32[128,1024]{1,0:T(8,128)S(1)}, f32[128,1024]{1,0:T(8,128)S(1)}, u32[]{:S(2)}, u32[]{:S(2)}) collective-permute-start(f32[128,1024]{1,0:T(8,128)S(1)} %get-tuple-element.159), channel_id=1, source_target_pairs={{0,96},{32,0},{64,32},{96,64},{1,97},{33,1},{65,33},{97,65},{2,98}... | collective-permute-start | bytes 1572872 | tf_op jit(solution)/shard_map/ppermute | solution.py:13
  270.9 14.1 %collective-permute-start.61 = (f32[128,1024]{1,0:T(8,128)S(1)}, f32[128,1024]{1,0:T(8,128)S(1)}, u32[]{:S(2)}, u32[]{:S(2)}) collective-permute-start(f32[128,1024]{1,0:T(8,128)S(1)} %get-tuple-element.158), channel_id=1, source_target_pairs={{0,18},{18,0},{2,16},{16,2},{1,19},{19,1},{3,17},{17,3},{4,22},{22... | collective-permute-start | bytes 1572872 | tf_op jit(solution)/shard_map/ppermute | solution.py:17
  273.1 15.4 %collective-permute-start.50 = (f32[128,1024]{1,0:T(8,128)}, f32[128,1024]{1,0:T(8,128)S(1)}, u32[]{:S(2)}, u32[]{:S(2)}) collective-permute-start(f32[128,1024]{1,0:T(8,128)} %get-tuple-element.144), channel_id=1, source_target_pairs={{0,1},{1,0},{2,3},{3,2},{4,5},{5,4},{6,7},{7,6},{8,9},{9,8},{10,11... | collective-permute-start | bytes 1572872 | tf_op jit(solution)/shard_map/ppermute | solution.py:13
  273.2 41.0 %collective-permute-start.42 = (f32[128,1024]{1,0:T(8,128)S(1)}, f32[128,1024]{1,0:T(8,128)S(1)}, u32[]{:S(2)}, u32[]{:S(2)}) collective-permute-start(f32[128,1024]{1,0:T(8,128)S(1)} %get-tuple-element.141), channel_id=1, source_target_pairs={{0,1},{1,0},{2,3},{3,2},{4,5},{5,4},{6,7},{7,6},{8,9},{9,8},{10,11... | collective-permute-start | bytes 1572872 | tf_op jit(solution)/shard_map/ppermute | solution.py:13
  282.3 12.5 %collective-permute-start.52 = (f32[128,1024]{1,0:T(8,128)S(1)}, f32[128,1024]{1,0:T(8,128)S(1)}, u32[]{:S(2)}, u32[]{:S(2)}) collective-permute-start(f32[128,1024]{1,0:T(8,128)S(1)} %get-tuple-element.151), channel_id=1, source_target_pairs={{0,2},{2,0},{1,3},{3,1},{4,6},{6,4},{5,7},{7,5},{8,10},{10,8},{9,1... | collective-permute-start | bytes 1572872 | tf_op jit(solution)/shard_map/ppermute | solution.py:13
  285.3 9.7 %collective-permute-start.62 = (f32[64,1024]{1,0:T(8,128)S(1)}, f32[64,1024]{1,0:T(8,128)S(1)}, u32[]{:S(2)}, u32[]{:S(2)}) collective-permute-start(f32[64,1024]{1,0:T(8,128)S(1)} %get-tuple-element.164), channel_id=1, source_target_pairs={{0,32},{32,64},{64,96},{96,0},{1,33},{33,65},{65,97},{97,1},{2,34}... | collective-permute-start | bytes 786440 | tf_op jit(solution)/shard_map/ppermute | solution.py:13
  285.3 13.1 %collective-permute-start.64 = (f32[64,1024]{1,0:T(8,128)S(1)}, f32[64,1024]{1,0:T(8,128)S(1)}, u32[]{:S(2)}, u32[]{:S(2)}) collective-permute-start(f32[64,1024]{1,0:T(8,128)S(1)} %get-tuple-element.165), channel_id=1, source_target_pairs={{0,96},{32,0},{64,32},{96,64},{1,97},{33,1},{65,33},{97,65},{2,98}... | collective-permute-start | bytes 786440 | tf_op jit(solution)/shard_map/ppermute | solution.py:13
  288.6 14.5 %collective-permute-start.60 = (f32[128,1024]{1,0:T(8,128)S(1)}, f32[128,1024]{1,0:T(8,128)S(1)}, u32[]{:S(2)}, u32[]{:S(2)}) collective-permute-start(f32[128,1024]{1,0:T(8,128)S(1)} %get-tuple-element.155), channel_id=1, source_target_pairs={{0,18},{18,0},{2,16},{16,2},{1,19},{19,1},{3,17},{17,3},{4,22},{22... | collective-permute-start | bytes 1572872 | tf_op jit(solution)/shard_map/ppermute | solution.py:17
  294.9 7.7 %collective-permute-start.53 = (f32[64,1024]{1,0:T(8,128)S(1)}, f32[64,1024]{1,0:T(8,128)S(1)}, u32[]{:S(2)}, u32[]{:S(2)}) collective-permute-start(f32[64,1024]{1,0:T(8,128)S(1)} %get-tuple-element.168), channel_id=1, source_target_pairs={{0,4},{4,8},{8,12},{12,0},{1,5},{5,9},{9,13},{13,1},{2,6},{6,10},{... | collective-permute-start | bytes 786440 | tf_op jit(solution)/shard_map/ppermute | solution.py:13
  295.0 7.6 %collective-permute-start.56 = (f32[64,1024]{1,0:T(8,128)S(1)}, f32[64,1024]{1,0:T(8,128)S(1)}, u32[]{:S(2)}, u32[]{:S(2)}) collective-permute-start(f32[64,1024]{1,0:T(8,128)S(1)} %get-tuple-element.169), channel_id=1, source_target_pairs={{0,12},{4,0},{8,4},{12,8},{1,13},{5,1},{9,5},{13,9},{2,14},{6,2},{... | collective-permute-start | bytes 786440 | tf_op jit(solution)/shard_map/ppermute | solution.py:13
  298.5 12.3 %collective-permute-start.63 = (f32[128,1024]{1,0:T(8,128)S(1)}, f32[128,1024]{1,0:T(8,128)S(1)}, u32[]{:S(2)}, u32[]{:S(2)}) collective-permute-start(f32[128,1024]{1,0:T(8,128)S(1)} %pad_maximum_fusion.3), channel_id=1, source_target_pairs={{0,32},{32,64},{64,96},{96,0},{1,33},{33,65},{65,97},{97,1},{2,34}... | collective-permute-start | bytes 1572872 | tf_op jit(solution)/shard_map/ppermute | solution.py:13
  302.6 10.7 %collective-permute-start.65 = (f32[128,1024]{1,0:T(8,128)S(1)}, f32[128,1024]{1,0:T(8,128)S(1)}, u32[]{:S(2)}, u32[]{:S(2)}) collective-permute-start(f32[128,1024]{1,0:T(8,128)S(1)} %pad_maximum_fusion.4), channel_id=1, source_target_pairs={{0,96},{32,0},{64,32},{96,64},{1,97},{33,1},{65,33},{97,65},{2,98}... | collective-permute-start | bytes 1572872 | tf_op jit(solution)/shard_map/ppermute | solution.py:13
  302.6 11.7 %collective-permute-start.48 = (f32[128,1024]{1,0:T(8,128)S(1)}, f32[128,1024]{1,0:T(8,128)S(1)}, u32[]{:S(2)}, u32[]{:S(2)}) collective-permute-start(f32[128,1024]{1,0:T(8,128)S(1)} %get-tuple-element.149), channel_id=1, source_target_pairs={{0,2},{2,0},{1,3},{3,1},{4,6},{6,4},{5,7},{7,5},{8,10},{10,8},{9,1... | collective-permute-start | bytes 1572872 | tf_op jit(solution)/shard_map/ppermute | solution.py:13
  303.1 11.9 %collective-permute-start.54 = (f32[128,1024]{1,0:T(8,128)S(1)}, f32[128,1024]{1,0:T(8,128)S(1)}, u32[]{:S(2)}, u32[]{:S(2)}) collective-permute-start(f32[128,1024]{1,0:T(8,128)S(1)} %pad_maximum_fusion.1), channel_id=1, source_target_pairs={{0,4},{4,8},{8,12},{12,0},{1,5},{5,9},{9,13},{13,1},{2,6},{6,10},{... | collective-permute-start | bytes 1572872 | tf_op jit(solution)/shard_map/ppermute | solution.py:13
  310.8 10.1 %collective-permute-start.57 = (f32[128,1024]{1,0:T(8,128)S(1)}, f32[128,1024]{1,0:T(8,128)S(1)}, u32[]{:S(2)}, u32[]{:S(2)}) collective-permute-start(f32[128,1024]{1,0:T(8,128)S(1)} %pad_maximum_fusion.2), channel_id=1, source_target_pairs={{0,12},{4,0},{8,4},{12,8},{1,13},{5,1},{9,5},{13,9},{2,14},{6,2},{... | collective-permute-start | bytes 1572872 | tf_op jit(solution)/shard_map/ppermute | solution.py:13
  (25 other events, 233.6 us)

commit v2 on v0

v2 whole, which is shorter than its diff:
```python
import functools

import jax
import jax.numpy as jnp
from jax import lax
from jax.experimental import pallas as pl
from jax.experimental.pallas import tpu as pltpu
from jax.sharding import Mesh, PartitionSpec as P

AXES = ("z", "xh", "y", "xl", "core")
SIZES = (4, 2, 4, 2, 2)
COUNT = 16384
HEIGHT, WIDTH, DEPTH, SHARE = 2048, 1024, 1024, 128
F32, BF16 = jnp.float32, jnp.bfloat16
WHOLE = pl.BlockSpec(memory_space=pltpu.VMEM)
SCALAR = pl.BlockSpec(memory_space=pltpu.SMEM)
NT = (((1,), (1,)), ((), ()))
NN = (((1,), (0,)), ((), ()))
TN = (((0,), (0,)), ((), ()))


def from_next(x, axis, step):
    n = lax.axis_size(axis)
    return lax.ppermute(x, axis, [(i, (i - step) % n) for i in range(n)])


def from_twin(x):
    return lax.ppermute(x, ("xh", "xl"), [(0, 3), (3, 0), (1, 2), (2, 1)])


def from_side(x):
    return from_next(x, "xl", 1)


def from_core(x):
    return from_next(x, "core", 1)


def together(*values):
    return lax.optimization_barrier(values)


def gather(texts):
    half = texts.shape[0] // 2
    side, up, down = together(from_twin(texts), from_next(texts, "z", 1), from_next(texts, "z", -1))
    low, high = together(from_next(up[:half], "z", 1), from_next(down[half:], "z", -1))
    far = jnp.concatenate([low, high])
    side2, far2 = together(side, far)
    return [
        texts, up, far, down,
        side, from_next(side2, "z", 1), from_twin(far2), from_next(side2, "z", -1),
    ]


class Ring:
    def __init__(self, axis, across):
        self.axis, self.across = axis, across

    def first(self, o_up, o_down, o_far):
        self.got = (from_next(o_up, self.axis, -1), from_next(o_down, self.axis, 1), self.across(o_far))

    def second(self, far, other):
        low, high, o_far = self.got
        far = far + o_far
        half = far.shape[0] // 2
        self.halves = (from_next(far[:half], self.axis, -1), from_next(far[half:], self.axis, 1))
        self.other = self.across(other + low + high)

    def third(self, own, up, down):
        half = own.shape[0] // 2
        low, high = self.halves
        up = jnp.concatenate([up[:half] + low, up[half:]])
        down = jnp.concatenate([down[:half], down[half:] + high])
        return own + from_next(up, self.axis, -1) + from_next(down, self.axis, 1) + self.other


def split(x):
    high = x.astype(BF16)
    return high, (x - high.astype(F32)).astype(BF16)


def fold(x):
    return functools.reduce(jnp.add, [x[:, i : i + 128] for i in range(0, x.shape[1], 128)])


def as_lanes(x):
    return jnp.sum(jnp.transpose(fold(x)), axis=0, keepdims=True)


def as_column(line):
    return jnp.transpose(jnp.broadcast_to(line, (128, 128)))


def dot3(ah, al, bh, bl, dims):
    d = functools.partial(lax.dot_general, dimension_numbers=dims, preferred_element_type=F32)
    return d(ah, bh) + (d(ah, bl) + d(al, bh))


CHUNK = 512
CHUNKS = HEIGHT // CHUNK
HBM = pl.BlockSpec(memory_space=pltpu.HBM)


def text_split_kernel(*refs):
    texts = refs[:8]
    tnorm, th_out, tl_out, th, tl, sem = refs[8:]
    for b in range(8):
        t = texts[b][...]
        cut = pl.ds(b * 128, 128)
        th[cut, :], tl[cut, :] = split(t)
        tnorm[:, b * 128 : b * 128 + 128] = as_lanes(t * t)
    high = pltpu.make_async_copy(th, th_out, sem.at[0])
    low = pltpu.make_async_copy(tl, tl_out, sem.at[1])
    high.start()
    low.start()
    high.wait()
    low.wait()


def text_split(texts):
    return pl.pallas_call(
        text_split_kernel,
        out_shape=[jax.ShapeDtypeStruct((1, WIDTH), F32)] + [pltpu.HBM((WIDTH, DEPTH), BF16)] * 2,
        in_specs=[WHOLE] * 8,
        out_specs=[WHOLE] + [HBM] * 2,
        scratch_shapes=[pltpu.VMEM((WIDTH, DEPTH), BF16)] * 2 + [pltpu.SemaphoreType.DMA((2,))],
        compiler_params=pltpu.CompilerParams(vmem_limit_bytes=14 * 2**20),
        cost_estimate=pl.CostEstimate(flops=2**24, bytes_accessed=8 * 2**20, transcendentals=0),
        name="text_split",
    )(*texts)


def cross_kernel(
    inverse_ref, row_ids, col_ids, pages, th_in, tl_in, tnorm,
    kern, ph, pl_, rows, cols,
    page_in, held, high, low, th, tl, col_acc, ident, in_sem, out_sem, text_sem,
):
    inverse = inverse_ref[0]

    def page_copy(c):
        return pltpu.make_async_copy(pages.at[pl.ds(c * CHUNK, CHUNK), :], page_in.at[c % 2], in_sem.at[c])

    def out_copies(c):
        cut = pl.ds(c * CHUNK, CHUNK)
        return (
            pltpu.make_async_copy(high.at[c % 2], ph.at[cut, :], out_sem.at[0, c]),
            pltpu.make_async_copy(low.at[c % 2], pl_.at[cut, :], out_sem.at[1, c]),
            pltpu.make_async_copy(held.at[cut, :], kern.at[cut, :], out_sem.at[2, c]),
        )

    text_copies = (
        pltpu.make_async_copy(th_in, th, text_sem.at[0]),
        pltpu.make_async_copy(tl_in, tl, text_sem.at[1]),
    )
    page_copy(0).start()
    for copy in text_copies:
        copy.start()
    page_copy(1).start()
    col_acc[...] = jnp.zeros_like(col_acc)
    rows[...] = jnp.zeros_like(rows)
    cols[...] = jnp.zeros_like(cols)
    for c in range(CHUNKS):
        page_copy(c).wait()
        h_copy, l_copy, k_copy = out_copies(c)
        if c >= 2:
            for copy in out_copies(c - 2)[:2]:
                copy.wait()
        p = page_in[c % 2]
        high[c % 2], low[c % 2] = split(p)
        pnorm = jnp.sum(p * p, axis=1, keepdims=True)
        h_copy.start()
        l_copy.start()
        if c + 2 < CHUNKS:
            page_copy(c + 2).start()
        if c == 0:
            for copy in text_copies:
                copy.wait()
        cross = dot3(high[c % 2], low[c % 2], th[...], tl[...], NT)
        k = jnp.exp((2.0 * cross - pnorm - tnorm[...]) * inverse)
        held[c * CHUNK : c * CHUNK + CHUNK, :] = k
        k_copy.start()
        col_acc[...] += jnp.sum(k.reshape(CHUNK // 8, 8, WIDTH), axis=0)
        for i in range(0, CHUNK, 128):
            line = (c * CHUNK + i) // 128
            rows[line : line + 1, :] = as_lanes(k[i : i + 128])

    total = jnp.sum(col_acc[...], axis=0, keepdims=True)
    for b in range(8):
        cols[pl.ds(col_ids[b] & 7, 1), :] = total[:, b * 128 : b * 128 + 128]
        ident[:, b * 128 : b * 128 + 128] = lax.broadcasted_iota(jnp.int32, (1, 128), 1) + col_ids[b] * 128
    tile_mean = jnp.sum(total) / (float(HEIGHT) * WIDTH)
    shift = total / float(HEIGHT) - tile_mean

    def stat(b, carry):
        inner, trace = carry
        k = held[pl.ds(pl.multiple_of(b * 128, 128), 128), :]
        mean = as_column(rows[pl.ds(b, 1), :] / float(WIDTH))[:, :1]
        own = k - mean - shift
        here = (lax.broadcasted_iota(jnp.int32, (128, 1), 0) + row_ids[b] * 128) == ident[...]
        diag = jnp.where(here, k, 0.0)
        inner = inner + jnp.sum(fold(own * own).reshape(16, 8, 128), axis=0)
        trace = trace + jnp.sum(fold(diag).reshape(16, 8, 128), axis=0)
        return inner, trace

    zero = jnp.zeros((8, 128), F32)
    inner, trace = lax.fori_loop(0, 16, stat, (zero, zero))
    rows[16:17, :] = jnp.sum(inner, axis=0, keepdims=True)
    rows[17:18, :] = jnp.sum(trace, axis=0, keepdims=True)
    for c in range(CHUNKS):
        for copy in out_copies(c)[0 if c >= CHUNKS - 2 else 2 :]:
            copy.wait()


def cross(inverse, row_ids, col_ids, pages, th, tl, tnorm):
    return pl.pallas_call(
        cross_kernel,
        out_shape=[
            pltpu.HBM((HEIGHT, WIDTH), F32),
            pltpu.HBM((HEIGHT, DEPTH), BF16),
            pltpu.HBM((HEIGHT, DEPTH), BF16),
            jax.ShapeDtypeStruct((24, 128), F32),
            jax.ShapeDtypeStruct((16, 128), F32),
        ],
        in_specs=[SCALAR] * 3 + [HBM] * 3 + [WHOLE],
        out_specs=[HBM] * 3 + [WHOLE] * 2,
        scratch_shapes=[
            pltpu.VMEM((2, CHUNK, DEPTH), F32),
            pltpu.VMEM((HEIGHT, WIDTH), F32),
            pltpu.VMEM((2, CHUNK, DEPTH), BF16),
            pltpu.VMEM((2, CHUNK, DEPTH), BF16),
            pltpu.VMEM((WIDTH, DEPTH), BF16),
            pltpu.VMEM((WIDTH, DEPTH), BF16),
            pltpu.VMEM((8, WIDTH), F32),
            pltpu.VMEM((1, WIDTH), jnp.int32),
            pltpu.SemaphoreType.DMA((CHUNKS,)),
            pltpu.SemaphoreType.DMA((3, CHUNKS)),
            pltpu.SemaphoreType.DMA((2,)),
        ],
        compiler_params=pltpu.CompilerParams(vmem_limit_bytes=36 * 2**20),
        cost_estimate=pl.CostEstimate(flops=6 * 2**31, bytes_accessed=8 * 2**20, transcendentals=2**21),
        name="cross",
    )(inverse, row_ids, col_ids, afar(pages), afar(th), afar(tl), tnorm)


def afar(x):
    return pltpu.with_memory_space_constraint(x, pltpu.HBM)


def near(x):
    return pltpu.with_memory_space_constraint(x, pltpu.VMEM)


def page_blocks(places, outs, wh, wl, load, ph, pl_, th, tl, size):
    for first in range(0, len(outs), size):
        cuts = [pl.ds(pl.multiple_of(p * 128, 128), 128) for p in places[first : first + size]]
        high = jnp.concatenate([wh[c, :] for c in cuts])
        low = jnp.concatenate([wl[c, :] for c in cuts])
        mixed = dot3(high, low, th[...], tl[...], NN)
        for i, c in enumerate(cuts):
            p = ph[c, :].astype(F32) + pl_[c, :].astype(F32)
            outs[first + i][...] = load[c, :1] * p - mixed[i * 128 : i * 128 + 128]


FIRST = (5, 7, 6, 2, 4, 13, 15, 14, 10, 12)
SECOND = (1, 3, 0, 9, 11, 8)
STEP = 256


def weight_kernel(*refs):
    facts, row_ids, col_ids, order, kern, ph_in, pl_in, th_in, tl_in, rows, cols = refs[:11]
    outs = refs[11:21]
    wh, wl, load, heavy, ph, pl_, th, tl = refs[21:29]
    mean_t, ident, held, k_sem, in_sem = refs[29:]
    k_copies = [
        pltpu.make_async_copy(kern.at[pl.ds(b, STEP), :], held.at[pl.ds(b, STEP), :], k_sem.at[b // STEP])
        for b in range(0, HEIGHT, STEP)
    ]
    copies = [
        pltpu.make_async_copy(src, dst, in_sem.at[i])
        for i, (src, dst) in enumerate(((th_in, th), (tl_in, tl), (ph_in, ph), (pl_in, pl_)))
    ]
    for copy in k_copies + copies:
        copy.start()
    per_row = 1.0 / COUNT
    slope, base, spike = facts[0:1, :1], facts[1:2, :1], facts[2:3, :1]
    for b in range(8):
        mean_t[:, b * 128 : b * 128 + 128] = cols[pl.ds(col_ids[b] & 7, 1), :] * per_row
        ident[:, b * 128 : b * 128 + 128] = lax.broadcasted_iota(jnp.int32, (1, 128), 1) + col_ids[b] * 128
    heavy[...] = jnp.zeros_like(heavy)
    for b in range(0, HEIGHT, STEP):
        cut = pl.ds(b, STEP)
        k_copies[b // STEP].wait()
        k = held[cut, :]
        blocks = range(b // 128, (b + STEP) // 128)
        r = jnp.concatenate([as_column(rows[i : i + 1, :] * per_row) for i in blocks])[:, :1]
        g = jnp.concatenate([lax.broadcasted_iota(jnp.int32, (128, 1), 0) + row_ids[i] * 128 for i in blocks])
        w = (slope * (k - r - mean_t[...]) + jnp.where(g == ident[...], base - spike, base)) * k
        wh[cut, :], wl[cut, :] = split(w)
        heavy[...] += jnp.sum(w.reshape(STEP // 8, 8, WIDTH), axis=0)
        load[cut, :] = jnp.broadcast_to(jnp.sum(w, axis=1, keepdims=True), (STEP, 128))
    for copy in copies:
        copy.wait()
    page_blocks([order[p] for p in FIRST], outs, wh, wl, load, ph, pl_, th, tl, 5)


def weigh(facts, row_ids, col_ids, order, kern, ph, pl_, th, tl, rows, cols):
    return pl.pallas_call(
        weight_kernel,
        out_shape=[pltpu.VMEM((SHARE, DEPTH), F32)] * 10
        + [pltpu.VMEM((HEIGHT, WIDTH), BF16), pltpu.VMEM((HEIGHT, WIDTH), BF16)]
        + [pltpu.VMEM((HEIGHT, 128), F32), jax.ShapeDtypeStruct((8, WIDTH), F32)]
        + [pltpu.VMEM((HEIGHT, DEPTH), BF16)] * 2
        + [pltpu.VMEM((WIDTH, DEPTH), BF16)] * 2,
        in_specs=[WHOLE] + [SCALAR] * 3 + [HBM] * 5 + [WHOLE] * 2,
        out_specs=[WHOLE] * 18,
        scratch_shapes=[
            pltpu.VMEM((1, WIDTH), F32),
            pltpu.VMEM((1, WIDTH), jnp.int32),
            pltpu.VMEM((HEIGHT, WIDTH), F32),
            pltpu.SemaphoreType.DMA((HEIGHT // STEP,)),
            pltpu.SemaphoreType.DMA((4,)),
        ],
        compiler_params=pltpu.CompilerParams(vmem_limit_bytes=22 * 2**20),
        cost_estimate=pl.CostEstimate(flops=10000, bytes_accessed=100000, transcendentals=0),
        name="weigh",
    )(facts, row_ids, col_ids, order, *map(afar, (kern, ph, pl_, th, tl)), rows, cols)


def page_kernel(*refs):
    order, wh, wl, load, ph, pl_, th, tl = refs[:8]
    page_blocks([order[p] for p in SECOND], refs[8:], wh, wl, load, ph, pl_, th, tl, 3)


def page_part(order, wh, wl, load, ph, pl_, th, tl):
    return pl.pallas_call(
        page_kernel,
        out_shape=[pltpu.VMEM((SHARE, DEPTH), F32)] * 6,
        in_specs=[SCALAR] + [WHOLE] * 7,
        out_specs=[WHOLE] * 6,
        compiler_params=pltpu.CompilerParams(vmem_limit_bytes=14 * 2**20),
        cost_estimate=pl.CostEstimate(flops=10000, bytes_accessed=100000, transcendentals=0),
        name="page_part",
    )(order, *map(near, (wh, wl, load, ph, pl_, th, tl)))


def text_kernel(start, heavy, wh, wl, ph, pl_, th, tl, *outs):
    load = jnp.sum(heavy[...], axis=0, keepdims=True)
    for j in range(start, start + 512, 256):
        folded = dot3(wh[:, j : j + 256], wl[:, j : j + 256], ph[...], pl_[...], TN)
        for i in range(2):
            q = j + i * 128
            t = th[q : q + 128, :].astype(F32) + tl[q : q + 128, :].astype(F32)
            column = as_column(load[:, q : q + 128])[:, :1]
            outs[(q - start) // 128][...] = folded[i * 128 : i * 128 + 128] - column * t


def text_part(start, heavy, wh, wl, ph, pl_, th, tl):
    return pl.pallas_call(
        functools.partial(text_kernel, start),
        out_shape=[pltpu.VMEM((SHARE, DEPTH), F32)] * 4,
        in_specs=[WHOLE] * 7,
        out_specs=[WHOLE] * 4,
        compiler_params=pltpu.CompilerParams(vmem_limit_bytes=14 * 2**20),
        cost_estimate=pl.CostEstimate(flops=10000, bytes_accessed=100000, transcendentals=0),
        name="text_part",
    )(heavy, *map(near, (wh, wl, ph, pl_, th, tl)))


def line_sum(x):
    return jnp.sum(x, axis=0, keepdims=True)


def without_mean(x):
    return x - jnp.mean(x)


def row_merge(size, r, r_got, r_out):
    d = r[:16] - r_got[:16]
    r_out[...] = r[...] + r_got[...]
    r_out[16:17] += line_sum(d * d) / (2.0 * size * WIDTH)


def column_merge(size, c, c_got, c_out):
    d = without_mean(c[:8] - c_got[:8])
    c_out[...] = c[...] + c_got[...]
    c_out[8:9] += line_sum(d * d) / (2.0 * size * HEIGHT)


def block_merge(size, u, u_got, u_out):
    d = u[1:2] - u_got[1:2]
    u_out[...] = u[...] + u_got[...]
    u_out[2:3] += d * d / (2.0 * size)


def row_facts(r, s_out):
    s_out[...] = jnp.zeros_like(s_out)
    s_out[0:2] = r[16:18]
    s_out[2:3] = line_sum(r[:16])


def block_facts(c, u_out):
    u_out[...] = jnp.zeros_like(u_out)
    u_out[0:1] = c[8:9]
    u_out[1:2] = jnp.broadcast_to(jnp.sum(c[:8]).reshape(1, 1), (1, 128))


def plain_merge(s, s_got, s_out):
    s_out[...] = s[...] + s_got[...]


def last_merge(s, u, facts):
    def whole(line):
        return jnp.broadcast_to(jnp.sum(line).reshape(1, 1), (1, 128))

    total = whole(s[2:3])
    frob_sq = whole(s[0:1] + u[0:1]) - u[2:3] / (COUNT * float(WIDTH))
    align = whole(s[1:2]) - total / COUNT
    grand = total / (float(COUNT) * COUNT)
    spike = 4.0 * COUNT / jnp.sqrt(frob_sq)
    slope = spike * (align / frob_sq)
    facts[...] = jnp.zeros_like(facts)
    facts[0:1] = slope
    facts[1:2] = slope * grand + spike / COUNT
    facts[2:3] = spike


def small(body, rows, *args):
    return pl.pallas_call(
        body,
        out_shape=jax.ShapeDtypeStruct((rows, 128), F32),
        in_specs=[WHOLE] * len(args),
        out_specs=WHOLE,
        compiler_params=pltpu.CompilerParams(vmem_limit_bytes=2**20),
        cost_estimate=pl.CostEstimate(flops=10000, bytes_accessed=100000, transcendentals=0),
        name="small",
    )(*args)


def from_pair(x, axis, bit):
    return lax.ppermute(x, axis, [(i, i ^ bit) for i in range(lax.axis_size(axis))])


def merged(body, size, x, got):
    return small(functools.partial(body, size), x.shape[0], x, got)


def statistics(r, c):
    r = merged(row_merge, 1, r, from_core(r))
    r_got, c_got = together(from_side(r), from_twin(c))
    r, c = merged(row_merge, 2, r, r_got), merged(column_merge, 1, c, c_got)
    r_got, c_got = together(from_pair(r, "y", 1), from_pair(c, "z", 1))
    r, c = merged(row_merge, 4, r, r_got), merged(column_merge, 2, c, c_got)
    r_got, c_got = together(from_pair(r, "y", 2), from_pair(c, "z", 2))
    r, c = merged(row_merge, 8, r, r_got), merged(column_merge, 4, c, c_got)
    s, u = small(row_facts, 8, r), small(block_facts, 8, c)
    u = merged(block_merge, 1, u, from_core(u))
    s_got, u_got = together(from_twin(s), from_side(u))
    s, u = small(plain_merge, 8, s, s_got), merged(block_merge, 2, u, u_got)
    s_got, u_got = together(from_pair(s, "z", 1), from_pair(u, "y", 1))
    s, u = small(plain_merge, 8, s, s_got), merged(block_merge, 4, u, u_got)
    s_got, u_got = together(from_pair(s, "z", 2), from_pair(u, "y", 2))
    s, u = small(plain_merge, 8, s, s_got), merged(block_merge, 8, u, u_got)
    return r, c, small(last_merge, 8, s, u)


def on_device(pages, transcripts, length_scale):
    spread_sq = length_scale[0] * length_scale[0]
    inverse = 0.5 / spread_sq
    z, xh, y, xl, core = (lax.axis_index(a) for a in AXES)
    blocks = lax.all_gather(pages, ("y", "xl", "core"), axis=0, tiled=True)
    texts = gather(transcripts)
    row_ids = (z * 2 + xh) * 16 + lax.iota(jnp.int32, 16)
    col_ids = jnp.stack(
        [
            (y * 4 + (xl ^ dq) * 2 + core) * 8 + ((z + dz) % 4) * 2 + (xh ^ dq)
            for dq in range(2)
            for dz in range(4)
        ]
    )
    order = jnp.stack(
        [
            ((y + dy) % 4) * 4 + (xl ^ dx) * 2 + (core ^ dc)
            for dc in range(2)
            for dx in range(2)
            for dy in range(4)
        ]
    )
    tnorm, th, tl = text_split(texts)
    kern, ph, pl_, r, c = cross(inverse.reshape(1), row_ids, col_ids, blocks, th, tl, tnorm)
    r, c, facts = statistics(r, c)
    *early, wh, wl, load, heavy, ph, pl_, th, tl = weigh(
        facts, row_ids, col_ids, order, kern, ph, pl_, th, tl, r, c
    )
    pages_ring, texts_ring = Ring("y", from_side), Ring("z", from_twin)
    o_up, o_down, o_far, far, other, heavy = together(
        *[early[i] + from_core(early[i + 5]) for i in range(5)], heavy
    )
    pages_ring.first(o_up, o_down, o_far)
    late = text_part(512, heavy, wh, wl, ph, pl_, th, tl)
    texts_ring.first(late[1], late[3], late[2])
    soon = text_part(0, together(heavy, *late)[0], wh, wl, ph, pl_, th, tl)
    *soon, order, g0, g1, g2 = together(*soon, order, *pages_ring.got)
    pages_ring.got = (g0, g1, g2)
    pages_ring.second(far, other)
    got = page_part(order, wh, wl, load, ph, pl_, th, tl)
    *got, g0, g1, g2, h0, h1, other = together(*got, *texts_ring.got, *pages_ring.halves, pages_ring.other)
    texts_ring.got, pages_ring.halves, pages_ring.other = (g0, g1, g2), (h0, h1), other
    up, down, own = together(*[got[i] + from_core(got[i + 3]) for i in range(3)])
    page_sum = pages_ring.third(own, up, down)
    texts_ring.second(soon[2], late[0])
    text_sum = texts_ring.third(soon[0], soon[1], soon[3])
    return (-page_sum / spread_sq, text_sum / spread_sq)


def solution(mesh):
    grid = Mesh(mesh.devices.reshape(SIZES), AXES)
    row, col = ("z", "xh"), ("y", "xl", "core")
    placed = (P(row + col, None), P(col + row, None), P())
    return jax.shard_map(
        on_device,
        mesh=grid,
        in_specs=placed,
        out_specs=(P(row + col, None), P(col + row, None)),
        check_vma=False,
    )
```

time: 594 us -> 217 us (0.37)
  waiting for transfers between devices: 272 us -> 71.8 us
  blocking collectives: 178 us -> 0 us
  matrix products: 96.8 us -> 0 us
  Pallas kernels: 0 us -> 62.7 us
  starting transfers between devices: 0.16 us -> 59.9 us
  other arithmetic: 23.9 us -> 3.22 us
    psum x4 -> x0, blocking collectives: 178 us -> none  [the longest x1 66.5 us: on_device(): total = lax.psum(jnp.sum(col_part), ('row', 'col'))]
    reduce_scatter x2 -> x0, waiting for transfers between devices: 147 us -> none  [the longest x1 97.1 us: on_device(): lax.psum_scatter(jnp.sum(part_weight, axis=1)[:, None] * page_block - mix...]
    all_gather x2 -> x1, waiting for transfers between devices: 124 us -> 9.03 us  [on_device(): blocks = lax.all_gather(pages, ('y', 'xl', 'core'), axis=0, tiled=True)]
    dot_general x3 -> x0, matrix products: 96.8 us -> none  [the longest x1 33.8 us: kernel_tile(): lax.dot_general(rows, cols, (((1,), (1,)), ((), ())), precision=lax.Preci...]
    pallas_call x0 -> x23, Pallas kernels: none -> 62.7 us  [the longest x1 22.5 us: cross(): pl.pallas_call(cross_kernel, out_shape=[pltpu.HBM((HEIGHT, WIDTH), F32),...]
    ppermute x0 -> x46, waiting for transfers between devices: none -> 62.1 us  [the longest x32 33.1 us: from_next(): return lax.ppermute(x, axis, [(i, (i - step) % n) for i in range(n)])]
    ppermute x0 -> x46, starting transfers between devices: none -> 59.9 us  [the longest x32 32.5 us: from_next(): return lax.ppermute(x, axis, [(i, (i - step) % n) for i in range(n)])]
    reduce_sum x4 -> x0, other arithmetic: 20.1 us -> none  [the longest x1 6.78 us: on_device(): jnp.sum(centred * on_diag)]
  transfers between devices with their start and end apart: 4 -> 47, of which waited for: 4 -> 29; matrix products, arithmetic and copies ran while one was open for 6% -> 1% of each run, Pallas kernels for 0% -> 11%
where the time goes in v2:
time: 217 us; the launch traced here: 214 us
  waiting for transfers between devices  71.8 us (33%)
  Pallas kernels  62.7 us (29%)
  starting transfers between devices  59.9 us (28%)
  between operations  15.3 us (7%)
  other arithmetic  3.22 us (1%)
    ppermute x32, waiting for transfers between devices, from_next(): return lax.ppermute(x, axis, [(i, (i - step) % n) for i in range(n)])  33.1 us
    ppermute x32, starting transfers between devices, from_next(): return lax.ppermute(x, axis, [(i, (i - step) % n) for i in range(n)])  32.5 us
    pallas_call x1, Pallas kernels, cross(): pl.pallas_call(cross_kernel, out_shape=[pltpu.HBM((HEIGHT, WIDTH), F32),...  22.5 us
    ppermute x6, waiting for transfers between devices, from_twin(): return lax.ppermute(x, ('xh', 'xl'), [(0, 3), (3, 0), (1, 2), (2, 1)])  20.9 us
    pallas_call x1, Pallas kernels, weigh(): pl.pallas_call(weight_kernel, out_shape=[pltpu.VMEM((SHARE, DEPTH), F32)]...  16.2 us
    ppermute x8, starting transfers between devices, from_pair(): lax.ppermute(x, axis, [(i, i ^ bit) for i in range(lax.axis_size(axis))])  15.6 us
    pallas_call x2, Pallas kernels, text_part(): pl.pallas_call(functools.partial(text_kernel, start), out_shape=[pltpu.VM...  13.6 us
    ppermute x6, starting transfers between devices, from_twin(): return lax.ppermute(x, ('xh', 'xl'), [(0, 3), (3, 0), (1, 2), (2, 1)])  11.7 us
  transfers between devices with their start and end apart: 47, of which 29 were waited for; matrix products, arithmetic and copies ran while one was open for 1% of the time, Pallas kernels for 11%

profile of v2, /device:TPU:0, one launch (start us, length us, event | category | flops | bytes accessed | tf_op | source)
XLA Modules:
  0.0 214.3 jit_solution(9644741295416821759)
XLA Ops:
  7.9 4.2 %collective-permute-start.1 = (f32[128,1024]{1,0:T(8,128)}, f32[128,1024]{1,0:T(8,128)S(1)}, u32[]{:S(2)}, u32[]{:S(2)}) collective-permute-start(f32[128,1024]{1,0:T(8,128)} %refs_0_.1), channel_id=1, source_target_pairs={{0,96},{32,0},{64,32},{96,64},{1,97},{33,1},{65,33},{97,65},{2,98}... | collective-permute-start | bytes 1572872 | tf_op jit(solution)/shard_map/ppermute | solution.py:24
  12.1 2.8 %collective-permute-start = (f32[128,1024]{1,0:T(8,128)}, f32[128,1024]{1,0:T(8,128)S(1)}, u32[]{:S(2)}, u32[]{:S(2)}) collective-permute-start(f32[128,1024]{1,0:T(8,128)} %refs_0_.1), channel_id=1, source_target_pairs={{0,18},{18,0},{2,16},{16,2},{1,19},{19,1},{3,17},{17,3},{4,22},{22... | collective-permute-start | bytes 1572872 | tf_op jit(solution)/shard_map/ppermute | solution.py:28
  14.8 8.7 %collective-permute-done.1.refs_1_ = f32[128,1024]{1,0:T(8,128)S(1)} collective-permute-done((f32[128,1024]{1,0:T(8,128)}, f32[128,1024]{1,0:T(8,128)S(1)}, u32[]{:S(2)}, u32[]{:S(2)}) %collective-permute-start.1) | collective-permute-done | bytes 524320 | tf_op jit(solution)/shard_map/ppermute | solution.py:24
  23.6 3.3 %collective-permute-done.refs_4_ = f32[128,1024]{1,0:T(8,128)S(1)} collective-permute-done((f32[128,1024]{1,0:T(8,128)}, f32[128,1024]{1,0:T(8,128)S(1)}, u32[]{:S(2)}, u32[]{:S(2)}) %collective-permute-start) | collective-permute-done | bytes 524320 | tf_op jit(solution)/shard_map/ppermute | solution.py:28
  26.9 2.5 %collective-permute-done.2.refs_3_ = f32[128,1024]{1,0:T(8,128)S(1)} collective-permute-done((f32[128,1024]{1,0:T(8,128)}, f32[128,1024]{1,0:T(8,128)S(1)}, u32[]{:S(2)}, u32[]{:S(2)}) %collective-permute-start.2) | collective-permute-done | bytes 524320 | tf_op jit(solution)/shard_map/ppermute | solution.py:24
  29.5 3.2 %collective-permute-start.3 = (f32[64,1024]{1,0:T(8,128)S(1)}, f32[64,1024]{1,0:T(8,128)S(1)}, u32[]{:S(2)}, u32[]{:S(2)}) collective-permute-start(f32[64,1024]{1,0:T(8,128)S(1)} %slice.42), channel_id=1, source_target_pairs={{0,96},{32,0},{64,32},{96,64},{1,97},{33,1},{65,33},{97,65},{2,98}... | collective-permute-start | bytes 786440 | tf_op jit(solution)/shard_map/ppermute | solution.py:24
  32.7 4.5 %collective-permute-done.4 = f32[64,1024]{1,0:T(8,128)S(1)} collective-permute-done((f32[64,1024]{1,0:T(8,128)S(1)}, f32[64,1024]{1,0:T(8,128)S(1)}, u32[]{:S(2)}, u32[]{:S(2)}) %collective-permute-start.4) | collective-permute-done | bytes 262176 | tf_op jit(solution)/shard_map/ppermute | solution.py:24
  38.0 3.4 %collective-permute-start.5 = (f32[128,1024]{1,0:T(8,128)S(1)}, f32[128,1024]{1,0:T(8,128)}, u32[]{:S(2)}, u32[]{:S(2)}) collective-permute-start(f32[128,1024]{1,0:T(8,128)S(1)} %collective-permute-done.refs_4_), channel_id=1, source_target_pairs={{0,96},{32,0},{64,32},{96,64},{1,97},{33,1},{65,33},{97,65},{2,98}... | collective-permute-start | bytes 1572872 | tf_op jit(solution)/shard_map/ppermute | solution.py:24
  42.2 7.7 %collective-permute-done.6.refs_6_ = f32[128,1024]{1,0:T(8,128)S(1)} collective-permute-done((f32[128,1024]{1,0:T(8,128)S(1)}, f32[128,1024]{1,0:T(8,128)S(1)}, u32[]{:S(2)}, u32[]{:S(2)}) %collective-permute-start.6) | collective-permute-done | bytes 524320 | tf_op jit(solution)/shard_map/ppermute | solution.py:28
  51.3 4.0 %text_split.1 = (f32[1,1024]{1,0:T(1,128)S(1)}, bf16[1024,1024]{1,0:T(8,128)(2,1)}, bf16[1024,1024]{1,0:T(8,128)(2,1)}) custom-call(f32[128,1024]{1,0:T(8,128)S(1)} %copy-done, f32[128,1024]{1,0:T(8,128)S(1)} %collective-permute-done.1.refs_1_, f32[128,1024]{1,0:T(8,128)S(1)} %constant_dynamic-update-slice_fusion.refs_2_, ...), custom_call_target="tpu_custom_call" | custom-call | flops 16777216 | bytes 8388608 | tf_op jit(solution)/shard_map/text_split/pallas_call | solution.py:121
  55.3 9.0 %all-gather.2.cloned.1.call-done.pages = f32[2048,1024]{1,0:T(8,128)} async-done(((f32[128,1024]{1,0:T(8,128)}), f32[2048,1024]{1,0:T(8,128)}) %all-gather.2.cloned.1.call-update) | async-done | bytes 8388624 | tf_op jit(solution)/shard_map/all_gather | solution.py:470
  64.3 22.5 %cross.1 = (f32[2048,1024]{1,0:T(8,128)}, bf16[2048,1024]{1,0:T(8,128)(2,1)}, bf16[2048,1024]{1,0:T(8,128)(2,1)}, f32[24,128]{1,0:T(8,128)S(1)}, f32[16,128]{1,0:T(8,128)S(1)}) custom-call(f32[1]{0:T(128)} %bitcast.1.inverse_ref, s32[16]{0:T(128)S(1)} %iota_add_fusion.row_ids.refs_1_, s32[8]{0:T(128)S(1)} %stack.86.col_ids.refs_2_, ...), custom_call_target="tpu_custom_call" | custom-call | flops 12884901888 | bytes 8388608 | tf_op jit(solution)/shard_map/cross/pallas_call | solution.py:215
  88.1 1.5 collective-permute-start.9
  89.5 2.1 %collective-permute-start.10 = (f32[16,128]{1,0:T(8,128)S(1)}, f32[16,128]{1,0:T(8,128)S(1)}, u32[]{:S(2)}, u32[]{:S(2)}) collective-permute-start(f32[16,128]{1,0:T(8,128)S(1)} %get-tuple-element.102.c), channel_id=1, source_target_pairs={{0,18},{18,0},{2,16},{16,2},{1,19},{19,1},{3,17},{17,3},{4,22},{22... | collective-permute-start | bytes 24584 | tf_op jit(solution)/shard_map/ppermute | solution.py:28
  91.7 2.7 %collective-permute-done.10.c_got = f32[16,128]{1,0:T(8,128)S(1)} collective-permute-done((f32[16,128]{1,0:T(8,128)S(1)}, f32[16,128]{1,0:T(8,128)S(1)}, u32[]{:S(2)}, u32[]{:S(2)}) %collective-permute-start.10) | collective-permute-done | bytes 8224 | tf_op jit(solution)/shard_map/ppermute | solution.py:28
  94.4 1.6 collective-permute-start.11
  96.1 1.6 collective-permute-start.12
  97.7 2.1 collective-permute-done.12.c_got
  99.9 2.2 %collective-permute-start.13 = (f32[24,128]{1,0:T(8,128)S(1)}, f32[24,128]{1,0:T(8,128)S(1)}, u32[]{:S(2)}, u32[]{:S(2)}) collective-permute-start(f32[24,128]{1,0:T(8,128)S(1)} %small.20.r), channel_id=1, source_target_pairs={{0,8},{4,12},{8,0},{12,4},{1,9},{5,13},{9,1},{13,5},{2,10},{6,14},... | collective-permute-start | bytes 36872 | tf_op jit(solution)/shard_map/ppermute | solution.py:440
  102.2 3.2 %collective-permute-start.14 = (f32[16,128]{1,0:T(8,128)S(1)}, f32[16,128]{1,0:T(8,128)S(1)}, u32[]{:S(2)}, u32[]{:S(2)}) collective-permute-start(f32[16,128]{1,0:T(8,128)S(1)} %small.21.c), channel_id=1, source_target_pairs={{0,64},{32,96},{64,0},{96,32},{1,65},{33,97},{65,1},{97,33},{2,66}... | collective-permute-start | bytes 24584 | tf_op jit(solution)/shard_map/ppermute | solution.py:440
  105.4 2.0 collective-permute-done.14.c_got
  107.8 2.5 %collective-permute-start.15 = (f32[8,128]{1,0:T(8,128)S(1)}, f32[8,128]{1,0:T(8,128)S(1)}, u32[]{:S(2)}, u32[]{:S(2)}) collective-permute-start(f32[8,128]{1,0:T(8,128)S(1)} %small.23.s), channel_id=1, source_target_pairs={{0,18},{18,0},{2,16},{16,2},{1,19},{19,1},{3,17},{17,3},{4,22},{22... | collective-permute-start | bytes 12296 | tf_op jit(solution)/shard_map/ppermute | solution.py:28
  110.4 2.3 %collective-permute-done.15.s_got = f32[8,128]{1,0:T(8,128)S(1)} collective-permute-done((f32[8,128]{1,0:T(8,128)S(1)}, f32[8,128]{1,0:T(8,128)S(1)}, u32[]{:S(2)}, u32[]{:S(2)}) %collective-permute-start.15) | collective-permute-done | bytes 4128 | tf_op jit(solution)/shard_map/ppermute | solution.py:28
  112.7 1.3 collective-permute-done.17.u_got
  114.3 1.6 collective-permute-start.18
  115.8 1.8 collective-permute-done.19.u_got
  117.9 2.0 collective-permute-start.21
  119.9 3.2 %collective-permute-start.20 = (f32[8,128]{1,0:T(8,128)S(1)}, f32[8,128]{1,0:T(8,128)S(1)}, u32[]{:S(2)}, u32[]{:S(2)}) collective-permute-start(f32[8,128]{1,0:T(8,128)S(1)} %small.29.s), channel_id=1, source_target_pairs={{0,64},{32,96},{64,0},{96,32},{1,65},{33,97},{65,1},{97,33},{2,66}... | collective-permute-start | bytes 12296 | tf_op jit(solution)/shard_map/ppermute | solution.py:440
  123.1 2.0 collective-permute-done.20.s_got
  125.3 16.2 %weigh.1 = (f32[128,1024]{1,0:T(8,128)S(1)}, f32[128,1024]{1,0:T(8,128)S(1)}, f32[128,1024]{1,0:T(8,128)S(1)}, f32[128,1024]{1,0:T(8,128)S(1)}, f32[128,1024]{1,...) custom-call(f32[8,128]{1,0:T(8,128)S(1)} %small.33.refs_0_, ...), custom_call_target="tpu_custom_call" | custom-call | flops 10000 | bytes 100000 | tf_op jit(solution)/shard_map/weigh/pallas_call | solution.py:307
  146.9 3.0 %collective-permute-start.28 = (f32[128,1024]{1,0:T(8,128)S(1)}, f32[128,1024]{1,0:T(8,128)S(1)}, u32[]{:S(2)}, u32[]{:S(2)}) collective-permute-start(f32[128,1024]{1,0:T(8,128)S(1)} %add.366), channel_id=1, source_target_pairs={{0,12},{4,0},{8,4},{12,8},{1,13},{5,1},{9,5},{13,9},{2,14},{6,2},{... | collective-permute-start | bytes 1572872 | tf_op jit(solution)/shard_map/ppermute | solution.py:24
  149.9 6.8 %text_part.2 = (f32[128,1024]{1,0:T(8,128)S(1)}, f32[128,1024]{1,0:T(8,128)S(1)}, f32[128,1024]{1,0:T(8,128)S(1)}, f32[128,1024]{1,0:T(8,128)S(1)}) custom-call(f32[8,1024]{1,0:T(8,128)S(1)} %get-tuple-element.140.heavy, bf16[2048,1024]{1,0:T(8,128)(2,1)S(1)} %get-tuple-element.130.wh.refs_1_, bf16[2048,1024]{1,0:T(8,128)(2,1)S(1)} %get-tuple-element.131.wl.refs_2_, ...), custom_call_target="tpu_custom_call" | custom-call | flops 10000 | bytes 100000 | tf_op jit(solution)/shard_map/text_part/pallas_call | solution.py:358
  156.7 1.6 collective-permute-start.30
  158.3 1.4 collective-permute-start.32
  159.7 6.8 %text_part.3 = (f32[128,1024]{1,0:T(8,128)S(1)}, f32[128,1024]{1,0:T(8,128)S(1)}, f32[128,1024]{1,0:T(8,128)S(1)}, f32[128,1024]{1,0:T(8,128)S(1)}) custom-call(f32[8,1024]{1,0:T(8,128)S(1)} %get-tuple-element.140.heavy, bf16[2048,1024]{1,0:T(8,128)(2,1)S(1)} %get-tuple-element.130.wh.refs_1_, bf16[2048,1024]{1,0:T(8,128)(2,1)S(1)} %get-tuple-element.131.wl.refs_2_, ...), custom_call_target="tpu_custom_call" | custom-call | flops 10000 | bytes 100000 | tf_op jit(solution)/shard_map/text_part/pallas_call | solution.py:358
  166.5 1.8 collective-permute-start.31
  168.4 1.5 collective-permute-start.35
  170.0 1.3 collective-permute-start.34
  172.1 5.6 %page_part.1 = (f32[128,1024]{1,0:T(8,128)S(1)}, f32[128,1024]{1,0:T(8,128)S(1)}, f32[128,1024]{1,0:T(8,128)S(1)}, f32[128,1024]{1,0:T(8,128)S(1)}, f32[128,1024]{1,0:T(8,128)S(1)}, /*index=5*/f32[128,1024]{1,0:T(8,128)S(1)}) custom-call(s32[16]{0:T(128)S(1)} %stack.103.refs_3_.refs_0_, bf16[2048,1024]{1,0:T(8,128)(2,1)S(1)} %get-tuple-element.130.wh.refs_1_, ...), custom_call_target="tpu_custom_call" | custom-call | flops 10000 | bytes 100000 | tf_op jit(solution)/shard_map/page_part/pallas_call | solution.py:335
  177.8 1.7 collective-permute-done.31
  179.5 1.7 collective-permute-done.35
  181.6 3.0 %collective-permute-start.43 = (f32[64,1024]{1,0:T(8,128)S(1)}, f32[64,1024]{1,0:T(8,128)S(1)}, u32[]{:S(2)}, u32[]{:S(2)}) collective-permute-start(f32[64,1024]{1,0:T(8,128)S(1)} %get-tuple-element.183), channel_id=1, source_target_pairs={{0,96},{32,0},{64,32},{96,64},{1,97},{33,1},{65,33},{97,65},{2,98}... | collective-permute-start | bytes 786440 | tf_op jit(solution)/shard_map/ppermute | solution.py:24
  185.2 3.7 %collective-permute-done.41 = f32[64,1024]{1,0:T(8,128)S(1)} collective-permute-done((f32[64,1024]{1,0:T(8,128)S(1)}, f32[64,1024]{1,0:T(8,128)S(1)}, u32[]{:S(2)}, u32[]{:S(2)}) %collective-permute-start.41) | collective-permute-done | bytes 262176 | tf_op jit(solution)/shard_map/ppermute | solution.py:24
  188.9 2.3 %collective-permute-start.45 = (f32[128,1024]{1,0:T(8,128)S(1)}, f32[128,1024]{1,0:T(8,128)S(1)}, u32[]{:S(2)}, u32[]{:S(2)}) collective-permute-start(f32[128,1024]{1,0:T(8,128)S(1)} %add_add_fusion), channel_id=1, source_target_pairs={{0,18},{18,0},{2,16},{16,2},{1,19},{19,1},{3,17},{17,3},{4,22},{22... | collective-permute-start | bytes 1572872 | tf_op jit(solution)/shard_map/ppermute | solution.py:28
  194.0 1.3 collective-permute-start.40
  196.2 4.9 %collective-permute-done.45 = f32[128,1024]{1,0:T(8,128)S(1)} collective-permute-done((f32[128,1024]{1,0:T(8,128)S(1)}, f32[128,1024]{1,0:T(8,128)S(1)}, u32[]{:S(2)}, u32[]{:S(2)}) %collective-permute-start.45) | collective-permute-done | bytes 524320 | tf_op jit(solution)/shard_map/ppermute | solution.py:28
  201.9 1.9 collective-permute-done.42
  204.8 1.5 collective-permute-done.39
  (101 shorter events, 19.7 us)
Async XLA Ops:
  7.2 57.1 %all-gather.2.cloned.1.call-start = ((), (), s32[]{:S(2)}) async-start(), calls=%async_computation | async-start | bytes 8912896 | tf_op jit(solution)/shard_map/all_gather | solution.py:470
  7.9 15.7 %collective-permute-start.1 = (f32[128,1024]{1,0:T(8,128)}, f32[128,1024]{1,0:T(8,128)S(1)}, u32[]{:S(2)}, u32[]{:S(2)}) collective-permute-start(f32[128,1024]{1,0:T(8,128)} %refs_0_.1), channel_id=1, source_target_pairs={{0,96},{32,0},{64,32},{96,64},{1,97},{33,1},{65,33},{97,65},{2,98}... | collective-permute-start | bytes 1572872 | tf_op jit(solution)/shard_map/ppermute | solution.py:24
  12.1 14.8 %collective-permute-start = (f32[128,1024]{1,0:T(8,128)}, f32[128,1024]{1,0:T(8,128)S(1)}, u32[]{:S(2)}, u32[]{:S(2)}) collective-permute-start(f32[128,1024]{1,0:T(8,128)} %refs_0_.1), channel_id=1, source_target_pairs={{0,18},{18,0},{2,16},{16,2},{1,19},{19,1},{3,17},{17,3},{4,22},{22... | collective-permute-start | bytes 1572872 | tf_op jit(solution)/shard_map/ppermute | solution.py:28
  14.8 14.5 %collective-permute-start.2 = (f32[128,1024]{1,0:T(8,128)}, f32[128,1024]{1,0:T(8,128)S(1)}, u32[]{:S(2)}, u32[]{:S(2)}) collective-permute-start(f32[128,1024]{1,0:T(8,128)} %refs_0_.1), channel_id=1, source_target_pairs={{0,32},{32,64},{64,96},{96,0},{1,33},{33,65},{65,97},{97,1},{2,34}... | collective-permute-start | bytes 1572872 | tf_op jit(solution)/shard_map/ppermute | solution.py:24
  29.4 7.8 %collective-permute-start.4 = (f32[64,1024]{1,0:T(8,128)S(1)}, f32[64,1024]{1,0:T(8,128)S(1)}, u32[]{:S(2)}, u32[]{:S(2)}) collective-permute-start(f32[64,1024]{1,0:T(8,128)S(1)} %slice.43), channel_id=1, source_target_pairs={{0,32},{32,64},{64,96},{96,0},{1,33},{33,65},{65,97},{97,1},{2,34}... | collective-permute-start | bytes 786440 | tf_op jit(solution)/shard_map/ppermute | solution.py:24
  29.5 7.8 %collective-permute-start.3 = (f32[64,1024]{1,0:T(8,128)S(1)}, f32[64,1024]{1,0:T(8,128)S(1)}, u32[]{:S(2)}, u32[]{:S(2)}) collective-permute-start(f32[64,1024]{1,0:T(8,128)S(1)} %slice.42), channel_id=1, source_target_pairs={{0,96},{32,0},{64,32},{96,64},{1,97},{33,1},{65,33},{97,65},{2,98}... | collective-permute-start | bytes 786440 | tf_op jit(solution)/shard_map/ppermute | solution.py:24
  37.3 12.5 %collective-permute-start.6 = (f32[128,1024]{1,0:T(8,128)S(1)}, f32[128,1024]{1,0:T(8,128)S(1)}, u32[]{:S(2)}, u32[]{:S(2)}) collective-permute-start(f32[128,1024]{1,0:T(8,128)S(1)} %constant_dynamic-update-slice_fusion.refs_2_), channel_id=1, source_target_pairs={{0,18},{18,0},{2,16},{16,2},{1,19},{19,1},{3,17},{17,3},{4,22},{22... | collective-permute-start | bytes 1572872 | tf_op jit(solution)/shard_map/ppermute | solution.py:28
  38.0 12.3 %collective-permute-start.7 = (f32[128,1024]{1,0:T(8,128)S(1)}, f32[128,1024]{1,0:T(8,128)S(1)}, u32[]{:S(2)}, u32[]{:S(2)}) collective-permute-start(f32[128,1024]{1,0:T(8,128)S(1)} %collective-permute-done.refs_4_), channel_id=1, source_target_pairs={{0,32},{32,64},{64,96},{96,0},{1,33},{33,65},{65,97},{97,1},{2,34}... | collective-permute-start | bytes 1572872 | tf_op jit(solution)/shard_map/ppermute | solution.py:24
  38.0 12.3 %collective-permute-start.5 = (f32[128,1024]{1,0:T(8,128)S(1)}, f32[128,1024]{1,0:T(8,128)}, u32[]{:S(2)}, u32[]{:S(2)}) collective-permute-start(f32[128,1024]{1,0:T(8,128)S(1)} %collective-permute-done.refs_4_), channel_id=1, source_target_pairs={{0,96},{32,0},{64,32},{96,64},{1,97},{33,1},{65,33},{97,65},{2,98}... | collective-permute-start | bytes 1572872 | tf_op jit(solution)/shard_map/ppermute | solution.py:24
  50.3 1.0 copy-start
  86.8 1.3 collective-permute-start.8
  88.1 6.3 %collective-permute-start.9 = (f32[24,128]{1,0:T(8,128)S(1)}, f32[24,128]{1,0:T(8,128)S(1)}, u32[]{:S(2)}, u32[]{:S(2)}) collective-permute-start(f32[24,128]{1,0:T(8,128)S(1)} %small.17.r), channel_id=1, source_target_pairs={{0,2},{2,0},{1,3},{3,1},{4,6},{6,4},{5,7},{7,5},{8,10},{10,8},{9,1... | collective-permute-start | bytes 36872 | tf_op jit(solution)/shard_map/ppermute | solution.py:24
  89.5 4.9 %collective-permute-start.10 = (f32[16,128]{1,0:T(8,128)S(1)}, f32[16,128]{1,0:T(8,128)S(1)}, u32[]{:S(2)}, u32[]{:S(2)}) collective-permute-start(f32[16,128]{1,0:T(8,128)S(1)} %get-tuple-element.102.c), channel_id=1, source_target_pairs={{0,18},{18,0},{2,16},{16,2},{1,19},{19,1},{3,17},{17,3},{4,22},{22... | collective-permute-start | bytes 24584 | tf_op jit(solution)/shard_map/ppermute | solution.py:28
  94.4 5.4 %collective-permute-start.11 = (f32[24,128]{1,0:T(8,128)S(1)}, f32[24,128]{1,0:T(8,128)S(1)}, u32[]{:S(2)}, u32[]{:S(2)}) collective-permute-start(f32[24,128]{1,0:T(8,128)S(1)} %small.18.r), channel_id=1, source_target_pairs={{0,4},{4,0},{8,12},{12,8},{1,5},{5,1},{9,13},{13,9},{2,6},{6,2},{1... | collective-permute-start | bytes 36872 | tf_op jit(solution)/shard_map/ppermute | solution.py:440
  96.1 3.7 %collective-permute-start.12 = (f32[16,128]{1,0:T(8,128)S(1)}, f32[16,128]{1,0:T(8,128)S(1)}, u32[]{:S(2)}, u32[]{:S(2)}) collective-permute-start(f32[16,128]{1,0:T(8,128)S(1)} %small.19.c), channel_id=1, source_target_pairs={{0,32},{32,0},{64,96},{96,64},{1,33},{33,1},{65,97},{97,65},{2,34}... | collective-permute-start | bytes 24584 | tf_op jit(solution)/shard_map/ppermute | solution.py:440
  99.9 7.6 %collective-permute-start.13 = (f32[24,128]{1,0:T(8,128)S(1)}, f32[24,128]{1,0:T(8,128)S(1)}, u32[]{:S(2)}, u32[]{:S(2)}) collective-permute-start(f32[24,128]{1,0:T(8,128)S(1)} %small.20.r), channel_id=1, source_target_pairs={{0,8},{4,12},{8,0},{12,4},{1,9},{5,13},{9,1},{13,5},{2,10},{6,14},... | collective-permute-start | bytes 36872 | tf_op jit(solution)/shard_map/ppermute | solution.py:440
  102.2 5.2 %collective-permute-start.14 = (f32[16,128]{1,0:T(8,128)S(1)}, f32[16,128]{1,0:T(8,128)S(1)}, u32[]{:S(2)}, u32[]{:S(2)}) collective-permute-start(f32[16,128]{1,0:T(8,128)S(1)} %small.21.c), channel_id=1, source_target_pairs={{0,64},{32,96},{64,0},{96,32},{1,65},{33,97},{65,1},{97,33},{2,66}... | collective-permute-start | bytes 24584 | tf_op jit(solution)/shard_map/ppermute | solution.py:440
  107.7 2.6 %collective-permute-start.16 = (f32[8,128]{1,0:T(8,128)S(1)}, f32[8,128]{1,0:T(8,128)S(1)}, u32[]{:S(2)}, u32[]{:S(2)}) collective-permute-start(f32[8,128]{1,0:T(8,128)S(1)} %small.25.u), channel_id=1, source_target_pairs={{0,1},{1,0},{2,3},{3,2},{4,5},{5,4},{6,7},{7,6},{8,9},{9,8},{10,11... | collective-permute-start | bytes 12296 | tf_op jit(solution)/shard_map/ppermute | solution.py:24
  107.8 4.9 %collective-permute-start.15 = (f32[8,128]{1,0:T(8,128)S(1)}, f32[8,128]{1,0:T(8,128)S(1)}, u32[]{:S(2)}, u32[]{:S(2)}) collective-permute-start(f32[8,128]{1,0:T(8,128)S(1)} %small.23.s), channel_id=1, source_target_pairs={{0,18},{18,0},{2,16},{16,2},{1,19},{19,1},{3,17},{17,3},{4,22},{22... | collective-permute-start | bytes 12296 | tf_op jit(solution)/shard_map/ppermute | solution.py:28
  110.3 3.7 %collective-permute-start.17 = (f32[8,128]{1,0:T(8,128)S(1)}, f32[8,128]{1,0:T(8,128)S(1)}, u32[]{:S(2)}, u32[]{:S(2)}) collective-permute-start(f32[8,128]{1,0:T(8,128)S(1)} %small.26.u), channel_id=1, source_target_pairs={{0,2},{2,0},{1,3},{3,1},{4,6},{6,4},{5,7},{7,5},{8,10},{10,8},{9,1... | collective-permute-start | bytes 12296 | tf_op jit(solution)/shard_map/ppermute | solution.py:24
  114.0 3.6 %collective-permute-start.19 = (f32[8,128]{1,0:T(8,128)S(1)}, f32[8,128]{1,0:T(8,128)S(1)}, u32[]{:S(2)}, u32[]{:S(2)}) collective-permute-start(f32[8,128]{1,0:T(8,128)S(1)} %small.28.u), channel_id=1, source_target_pairs={{0,4},{4,0},{8,12},{12,8},{1,5},{5,1},{9,13},{13,9},{2,6},{6,2},{1... | collective-permute-start | bytes 12296 | tf_op jit(solution)/shard_map/ppermute | solution.py:440
  114.3 3.6 %collective-permute-start.18 = (f32[8,128]{1,0:T(8,128)S(1)}, f32[8,128]{1,0:T(8,128)S(1)}, u32[]{:S(2)}, u32[]{:S(2)}) collective-permute-start(f32[8,128]{1,0:T(8,128)S(1)} %small.27.s), channel_id=1, source_target_pairs={{0,32},{32,0},{64,96},{96,64},{1,33},{33,1},{65,97},{97,65},{2,34}... | collective-permute-start | bytes 12296 | tf_op jit(solution)/shard_map/ppermute | solution.py:440
  117.9 5.2 %collective-permute-start.21 = (f32[8,128]{1,0:T(8,128)S(1)}, f32[8,128]{1,0:T(8,128)S(1)}, u32[]{:S(2)}, u32[]{:S(2)}) collective-permute-start(f32[8,128]{1,0:T(8,128)S(1)} %small.30.u), channel_id=1, source_target_pairs={{0,8},{4,12},{8,0},{12,4},{1,9},{5,13},{9,1},{13,5},{2,10},{6,14},... | collective-permute-start | bytes 12296 | tf_op jit(solution)/shard_map/ppermute | solution.py:440
  119.9 5.1 %collective-permute-start.20 = (f32[8,128]{1,0:T(8,128)S(1)}, f32[8,128]{1,0:T(8,128)S(1)}, u32[]{:S(2)}, u32[]{:S(2)}) collective-permute-start(f32[8,128]{1,0:T(8,128)S(1)} %small.29.s), channel_id=1, source_target_pairs={{0,64},{32,96},{64,0},{96,32},{1,65},{33,97},{65,1},{97,33},{2,66}... | collective-permute-start | bytes 12296 | tf_op jit(solution)/shard_map/ppermute | solution.py:440
  141.5 2.0 collective-permute-start.22
  141.6 2.6 %collective-permute-start.23 = (f32[128,1024]{1,0:T(8,128)S(1)}, f32[128,1024]{1,0:T(8,128)S(1)}, u32[]{:S(2)}, u32[]{:S(2)}) collective-permute-start(f32[128,1024]{1,0:T(8,128)S(1)} %get-tuple-element.121), channel_id=1, source_target_pairs={{0,1},{1,0},{2,3},{3,2},{4,5},{5,4},{6,7},{7,6},{8,9},{9,8},{10,11... | collective-permute-start | bytes 1572872 | tf_op jit(solution)/shard_map/ppermute | solution.py:24
  142.1 2.9 %collective-permute-start.24 = (f32[128,1024]{1,0:T(8,128)S(1)}, f32[128,1024]{1,0:T(8,128)S(1)}, u32[]{:S(2)}, u32[]{:S(2)}) collective-permute-start(f32[128,1024]{1,0:T(8,128)S(1)} %get-tuple-element.123), channel_id=1, source_target_pairs={{0,1},{1,0},{2,3},{3,2},{4,5},{5,4},{6,7},{7,6},{8,9},{9,8},{10,11... | collective-permute-start | bytes 1572872 | tf_op jit(solution)/shard_map/ppermute | solution.py:24
  142.2 3.6 %collective-permute-start.25 = (f32[128,1024]{1,0:T(8,128)S(1)}, f32[128,1024]{1,0:T(8,128)S(1)}, u32[]{:S(2)}, u32[]{:S(2)}) collective-permute-start(f32[128,1024]{1,0:T(8,128)S(1)} %get-tuple-element.125), channel_id=1, source_target_pairs={{0,1},{1,0},{2,3},{3,2},{4,5},{5,4},{6,7},{7,6},{8,9},{9,8},{10,11... | collective-permute-start | bytes 1572872 | tf_op jit(solution)/shard_map/ppermute | solution.py:24
  142.6 3.9 %collective-permute-start.26 = (f32[128,1024]{1,0:T(8,128)S(1)}, f32[128,1024]{1,0:T(8,128)S(1)}, u32[]{:S(2)}, u32[]{:S(2)}) collective-permute-start(f32[128,1024]{1,0:T(8,128)S(1)} %get-tuple-element.127), channel_id=1, source_target_pairs={{0,1},{1,0},{2,3},{3,2},{4,5},{5,4},{6,7},{7,6},{8,9},{9,8},{10,11... | collective-permute-start | bytes 1572872 | tf_op jit(solution)/shard_map/ppermute | solution.py:24
  146.6 20.0 %collective-permute-start.27 = (f32[128,1024]{1,0:T(8,128)S(1)}, f32[128,1024]{1,0:T(8,128)S(1)}, u32[]{:S(2)}, u32[]{:S(2)}) collective-permute-start(f32[128,1024]{1,0:T(8,128)S(1)} %add.365), channel_id=1, source_target_pairs={{0,4},{4,8},{8,12},{12,0},{1,5},{5,9},{9,13},{13,1},{2,6},{6,10},{... | collective-permute-start | bytes 1572872 | tf_op jit(solution)/shard_map/ppermute | solution.py:24
  146.9 21.4 %collective-permute-start.28 = (f32[128,1024]{1,0:T(8,128)S(1)}, f32[128,1024]{1,0:T(8,128)S(1)}, u32[]{:S(2)}, u32[]{:S(2)}) collective-permute-start(f32[128,1024]{1,0:T(8,128)S(1)} %add.366), channel_id=1, source_target_pairs={{0,12},{4,0},{8,4},{12,8},{1,13},{5,1},{9,5},{13,9},{2,14},{6,2},{... | collective-permute-start | bytes 1572872 | tf_op jit(solution)/shard_map/ppermute | solution.py:24
  149.9 18.4 %collective-permute-start.29 = (f32[128,1024]{1,0:T(8,128)S(1)}, f32[128,1024]{1,0:T(8,128)S(1)}, u32[]{:S(2)}, u32[]{:S(2)}) collective-permute-start(f32[128,1024]{1,0:T(8,128)S(1)} %add.367), channel_id=1, source_target_pairs={{0,2},{2,0},{1,3},{3,1},{4,6},{6,4},{5,7},{7,5},{8,10},{10,8},{9,1... | collective-permute-start | bytes 1572872 | tf_op jit(solution)/shard_map/ppermute | solution.py:24
  156.7 14.7 %collective-permute-start.30 = (f32[128,1024]{1,0:T(8,128)S(1)}, f32[128,1024]{1,0:T(8,128)S(1)}, u32[]{:S(2)}, u32[]{:S(2)}) collective-permute-start(f32[128,1024]{1,0:T(8,128)S(1)} %get-tuple-element.137), channel_id=1, source_target_pairs={{0,32},{32,64},{64,96},{96,0},{1,33},{33,65},{65,97},{97,1},{2,34}... | collective-permute-start | bytes 1572872 | tf_op jit(solution)/shard_map/ppermute | solution.py:24
  158.3 19.5 %collective-permute-start.32 = (f32[128,1024]{1,0:T(8,128)S(1)}, f32[128,1024]{1,0:T(8,128)S(1)}, u32[]{:S(2)}, u32[]{:S(2)}) collective-permute-start(f32[128,1024]{1,0:T(8,128)S(1)} %get-tuple-element.138), channel_id=1, source_target_pairs={{0,18},{18,0},{2,16},{16,2},{1,19},{19,1},{3,17},{17,3},{4,22},{22... | collective-permute-start | bytes 1572872 | tf_op jit(solution)/shard_map/ppermute | solution.py:28
  166.5 12.9 %collective-permute-start.31 = (f32[128,1024]{1,0:T(8,128)S(1)}, f32[128,1024]{1,0:T(8,128)S(1)}, u32[]{:S(2)}, u32[]{:S(2)}) collective-permute-start(f32[128,1024]{1,0:T(8,128)S(1)} %get-tuple-element.139), channel_id=1, source_target_pairs={{0,96},{32,0},{64,32},{96,64},{1,97},{33,1},{65,33},{97,65},{2,98}... | collective-permute-start | bytes 1572872 | tf_op jit(solution)/shard_map/ppermute | solution.py:24
  168.4 12.8 %collective-permute-start.35 = (f32[128,1024]{1,0:T(8,128)S(1)}, f32[128,1024]{1,0:T(8,128)S(1)}, u32[]{:S(2)}, u32[]{:S(2)}) collective-permute-start(f32[128,1024]{1,0:T(8,128)S(1)} %add_add_fusion.1), channel_id=1, source_target_pairs={{0,2},{2,0},{1,3},{3,1},{4,6},{6,4},{5,7},{7,5},{8,10},{10,8},{9,1... | collective-permute-start | bytes 1572872 | tf_op jit(solution)/shard_map/ppermute | solution.py:24
  170.0 9.4 %collective-permute-start.34 = (f32[64,1024]{1,0:T(8,128)S(1)}, f32[64,1024]{1,0:T(8,128)S(1)}, u32[]{:S(2)}, u32[]{:S(2)}) collective-permute-start(f32[64,1024]{1,0:T(8,128)S(1)} %get-tuple-element.190), channel_id=1, source_target_pairs={{0,12},{4,0},{8,4},{12,8},{1,13},{5,1},{9,5},{13,9},{2,14},{6,2},{... | collective-permute-start | bytes 786440 | tf_op jit(solution)/shard_map/ppermute | solution.py:24
  171.4 8.1 %collective-permute-start.33 = (f32[64,1024]{1,0:T(8,128)S(1)}, f32[64,1024]{1,0:T(8,128)S(1)}, u32[]{:S(2)}, u32[]{:S(2)}) collective-permute-start(f32[64,1024]{1,0:T(8,128)S(1)} %get-tuple-element.191), channel_id=1, source_target_pairs={{0,4},{4,8},{8,12},{12,0},{1,5},{5,9},{9,13},{13,1},{2,6},{6,10},{... | collective-permute-start | bytes 786440 | tf_op jit(solution)/shard_map/ppermute | solution.py:24
  181.3 7.7 %collective-permute-start.41 = (f32[64,1024]{1,0:T(8,128)S(1)}, f32[64,1024]{1,0:T(8,128)S(1)}, u32[]{:S(2)}, u32[]{:S(2)}) collective-permute-start(f32[64,1024]{1,0:T(8,128)S(1)} %get-tuple-element.182), channel_id=1, source_target_pairs={{0,32},{32,64},{64,96},{96,0},{1,33},{33,65},{65,97},{97,1},{2,34}... | collective-permute-start | bytes 786440 | tf_op jit(solution)/shard_map/ppermute | solution.py:24
  181.6 9.6 %collective-permute-start.43 = (f32[64,1024]{1,0:T(8,128)S(1)}, f32[64,1024]{1,0:T(8,128)S(1)}, u32[]{:S(2)}, u32[]{:S(2)}) collective-permute-start(f32[64,1024]{1,0:T(8,128)S(1)} %get-tuple-element.183), channel_id=1, source_target_pairs={{0,96},{32,0},{64,32},{96,64},{1,97},{33,1},{65,33},{97,65},{2,98}... | collective-permute-start | bytes 786440 | tf_op jit(solution)/shard_map/ppermute | solution.py:24
  184.6 7.9 %collective-permute-start.36 = (f32[128,1024]{1,0:T(8,128)S(1)}, f32[128,1024]{1,0:T(8,128)S(1)}, u32[]{:S(2)}, u32[]{:S(2)}) collective-permute-start(f32[128,1024]{1,0:T(8,128)S(1)} %get-tuple-element.162), channel_id=1, source_target_pairs={{0,1},{1,0},{2,3},{3,2},{4,5},{5,4},{6,7},{7,6},{8,9},{9,8},{10,11... | collective-permute-start | bytes 1572872 | tf_op jit(solution)/shard_map/ppermute | solution.py:24
  184.6 9.1 %collective-permute-start.37 = (f32[128,1024]{1,0:T(8,128)S(1)}, f32[128,1024]{1,0:T(8,128)S(1)}, u32[]{:S(2)}, u32[]{:S(2)}) collective-permute-start(f32[128,1024]{1,0:T(8,128)S(1)} %get-tuple-element.164), channel_id=1, source_target_pairs={{0,1},{1,0},{2,3},{3,2},{4,5},{5,4},{6,7},{7,6},{8,9},{9,8},{10,11... | collective-permute-start | bytes 1572872 | tf_op jit(solution)/shard_map/ppermute | solution.py:24
  185.1 8.7 %collective-permute-start.38 = (f32[128,1024]{1,0:T(8,128)S(1)}, f32[128,1024]{1,0:T(8,128)S(1)}, u32[]{:S(2)}, u32[]{:S(2)}) collective-permute-start(f32[128,1024]{1,0:T(8,128)S(1)} %get-tuple-element.166), channel_id=1, source_target_pairs={{0,1},{1,0},{2,3},{3,2},{4,5},{5,4},{6,7},{7,6},{8,9},{9,8},{10,11... | collective-permute-start | bytes 1572872 | tf_op jit(solution)/shard_map/ppermute | solution.py:24
  188.9 12.2 %collective-permute-start.45 = (f32[128,1024]{1,0:T(8,128)S(1)}, f32[128,1024]{1,0:T(8,128)S(1)}, u32[]{:S(2)}, u32[]{:S(2)}) collective-permute-start(f32[128,1024]{1,0:T(8,128)S(1)} %add_add_fusion), channel_id=1, source_target_pairs={{0,18},{18,0},{2,16},{16,2},{1,19},{19,1},{3,17},{17,3},{4,22},{22... | collective-permute-start | bytes 1572872 | tf_op jit(solution)/shard_map/ppermute | solution.py:28
  191.4 10.5 %collective-permute-start.44 = (f32[128,1024]{1,0:T(8,128)S(1)}, f32[128,1024]{1,0:T(8,128)S(1)}, u32[]{:S(2)}, u32[]{:S(2)}) collective-permute-start(f32[128,1024]{1,0:T(8,128)S(1)} %pad_maximum_fusion.3), channel_id=1, source_target_pairs={{0,96},{32,0},{64,32},{96,64},{1,97},{33,1},{65,33},{97,65},{2,98}... | collective-permute-start | bytes 1572872 | tf_op jit(solution)/shard_map/ppermute | solution.py:24
  192.5 11.3 %collective-permute-start.42 = (f32[128,1024]{1,0:T(8,128)S(1)}, f32[128,1024]{1,0:T(8,128)S(1)}, u32[]{:S(2)}, u32[]{:S(2)}) collective-permute-start(f32[128,1024]{1,0:T(8,128)S(1)} %pad_maximum_fusion.2), channel_id=1, source_target_pairs={{0,32},{32,64},{64,96},{96,0},{1,33},{33,65},{65,97},{97,1},{2,34}... | collective-permute-start | bytes 1572872 | tf_op jit(solution)/shard_map/ppermute | solution.py:24
  194.0 10.7 %collective-permute-start.40 = (f32[128,1024]{1,0:T(8,128)S(1)}, f32[128,1024]{1,0:T(8,128)S(1)}, u32[]{:S(2)}, u32[]{:S(2)}) collective-permute-start(f32[128,1024]{1,0:T(8,128)S(1)} %pad_maximum_fusion.1), channel_id=1, source_target_pairs={{0,12},{4,0},{8,4},{12,8},{1,13},{5,1},{9,5},{13,9},{2,14},{6,2},{... | collective-permute-start | bytes 1572872 | tf_op jit(solution)/shard_map/ppermute | solution.py:24
  195.4 10.9 %collective-permute-start.39 = (f32[128,1024]{1,0:T(8,128)S(1)}, f32[128,1024]{1,0:T(8,128)S(1)}, u32[]{:S(2)}, u32[]{:S(2)}) collective-permute-start(f32[128,1024]{1,0:T(8,128)S(1)} %pad_maximum_fusion), channel_id=1, source_target_pairs={{0,4},{4,8},{8,12},{12,0},{1,5},{5,9},{9,13},{13,1},{2,6},{6,10},{... | collective-permute-start | bytes 1572872 | tf_op jit(solution)/shard_map/ppermute | solution.py:24
Sparse Core Ops, SparseCore 0:
  9.7 54.5 all-gather.1

commit v3 on v2

--- a/solution.py
+++ b/solution.py
@@ -89,6 +89,10 @@
 
 def as_column(line):
     return jnp.transpose(jnp.broadcast_to(line, (128, 128)))
+
+
+def line_sum(x):
+    return jnp.sum(x, axis=0, keepdims=True)
 
 
 def dot3(ah, al, bh, bl, dims):
@@ -133,7 +137,7 @@
 def cross_kernel(
     inverse_ref, row_ids, col_ids, pages, th_in, tl_in, tnorm,
     kern, ph, pl_, rows, cols,
-    page_in, held, high, low, th, tl, col_acc, ident, in_sem, out_sem, text_sem,
+    page_in, held, high, low, th, tl, col_acc, in_sem, out_sem, text_sem,
 ):
     inverse = inverse_ref[0]
 
@@ -148,6 +152,10 @@
             pltpu.make_async_copy(held.at[cut, :], kern.at[cut, :], out_sem.at[2, c]),
         )
 
+    text_copies = (
+        pltpu.make_async_copy(th_in, th, text_sem.at[0]),
+        pltpu.make_async_copy(tl_in, tl, text_sem.at[1]),
+    )
     text_copies = (
         pltpu.make_async_copy(th_in, th, text_sem.at[0]),
         pltpu.make_async_copy(tl_in, tl, text_sem.at[1]),
@@ -187,25 +195,26 @@
     total = jnp.sum(col_acc[...], axis=0, keepdims=True)
     for b in range(8):
         cols[pl.ds(col_ids[b] & 7, 1), :] = total[:, b * 128 : b * 128 + 128]
-        ident[:, b * 128 : b * 128 + 128] = lax.broadcasted_iota(jnp.int32, (1, 128), 1) + col_ids[b] * 128
     tile_mean = jnp.sum(total) / (float(HEIGHT) * WIDTH)
     shift = total / float(HEIGHT) - tile_mean
 
-    def stat(b, carry):
-        inner, trace = carry
+    def stat(b, inner):
         k = held[pl.ds(pl.multiple_of(b * 128, 128), 128), :]
         mean = as_column(rows[pl.ds(b, 1), :] / float(WIDTH))[:, :1]
         own = k - mean - shift
-        here = (lax.broadcasted_iota(jnp.int32, (128, 1), 0) + row_ids[b] * 128) == ident[...]
-        diag = jnp.where(here, k, 0.0)
-        inner = inner + jnp.sum(fold(own * own).reshape(16, 8, 128), axis=0)
-        trace = trace + jnp.sum(fold(diag).reshape(16, 8, 128), axis=0)
-        return inner, trace
-
-    zero = jnp.zeros((8, 128), F32)
-    inner, trace = lax.fori_loop(0, 16, stat, (zero, zero))
+        return inner + jnp.sum(fold(own * own).reshape(16, 8, 128), axis=0)
+
+    inner = lax.fori_loop(0, 16, stat, jnp.zeros((8, 128), F32))
     rows[16:17, :] = jnp.sum(inner, axis=0, keepdims=True)
-    rows[17:18, :] = jnp.sum(trace, axis=0, keepdims=True)
+    diagonal = lax.broadcasted_iota(jnp.int32, (128, 128), 0) == lax.broadcasted_iota(jnp.int32, (128, 128), 1)
+    for b in range(8):
+        place = col_ids[b] - row_ids[0]
+
+        @pl.when((place >= 0) & (place < 16))
+        def _():
+            k = held[pl.ds(pl.multiple_of(place * 128, 128), 128), b * 128 : b * 128 + 128]
+            rows[17:18, :] += line_sum(jnp.where(diagonal, k, 0.0))
+
     for c in range(CHUNKS):
         for copy in out_copies(c)[0 if c >= CHUNKS - 2 else 2 :]:
             copy.wait()
@@ -231,7 +240,6 @@
             pltpu.VMEM((WIDTH, DEPTH), BF16),
             pltpu.VMEM((WIDTH, DEPTH), BF16),
             pltpu.VMEM((8, WIDTH), F32),
-            pltpu.VMEM((1, WIDTH), jnp.int32),
             pltpu.SemaphoreType.DMA((CHUNKS,)),
             pltpu.SemaphoreType.DMA((3, CHUNKS)),
             pltpu.SemaphoreType.DMA((2,)),
@@ -250,9 +258,13 @@
     return pltpu.with_memory_space_constraint(x, pltpu.VMEM)
 
 
+def block_at(place):
+    return pl.ds(pl.multiple_of(place * 128, 128), 128)
+
+
 def page_blocks(places, outs, wh, wl, load, ph, pl_, th, tl, size):
     for first in range(0, len(outs), size):
-        cuts = [pl.ds(pl.multiple_of(p * 128, 128), 128) for p in places[first : first + size]]
+        cuts = [block_at(p) for p in places[first : first + size]]
         high = jnp.concatenate([wh[c, :] for c in cuts])
         low = jnp.concatenate([wl[c, :] for c in cuts])
         mixed = dot3(high, low, th[...], tl[...], NN)
@@ -263,23 +275,21 @@
 
 FIRST = (5, 7, 6, 2, 4, 13, 15, 14, 10, 12)
 SECOND = (1, 3, 0, 9, 11, 8)
-STEP = 256
+RUN = 5
 
 
 def weight_kernel(*refs):
     facts, row_ids, col_ids, order, kern, ph_in, pl_in, th_in, tl_in, rows, cols = refs[:11]
     outs = refs[11:21]
     wh, wl, load, heavy, ph, pl_, th, tl = refs[21:29]
-    mean_t, ident, held, k_sem, in_sem = refs[29:]
+    mean_t, ident, held, high, low, k_sem, in_sem = refs[29:]
+    places = [order[p] for p in FIRST + SECOND]
     k_copies = [
-        pltpu.make_async_copy(kern.at[pl.ds(b, STEP), :], held.at[pl.ds(b, STEP), :], k_sem.at[b // STEP])
-        for b in range(0, HEIGHT, STEP)
+        pltpu.make_async_copy(kern.at[block_at(p), :], held.at[i], k_sem.at[i]) for i, p in enumerate(places)
     ]
-    copies = [
-        pltpu.make_async_copy(src, dst, in_sem.at[i])
-        for i, (src, dst) in enumerate(((th_in, th), (tl_in, tl), (ph_in, ph), (pl_in, pl_)))
-    ]
-    for copy in k_copies + copies:
+    t_copies = [pltpu.make_async_copy(th_in, th, in_sem.at[0]), pltpu.make_async_copy(tl_in, tl, in_sem.at[1])]
+    p_copies = [pltpu.make_async_copy(ph_in, ph, in_sem.at[2]), pltpu.make_async_copy(pl_in, pl_, in_sem.at[3])]
+    for copy in k_copies[:RUN] + t_copies + k_copies[RUN : 2 * RUN] + p_copies + k_copies[2 * RUN :]:
         copy.start()
     per_row = 1.0 / COUNT
     slope, base, spike = facts[0:1, :1], facts[1:2, :1], facts[2:3, :1]
@@ -287,20 +297,50 @@
         mean_t[:, b * 128 : b * 128 + 128] = cols[pl.ds(col_ids[b] & 7, 1), :] * per_row
         ident[:, b * 128 : b * 128 + 128] = lax.broadcasted_iota(jnp.int32, (1, 128), 1) + col_ids[b] * 128
     heavy[...] = jnp.zeros_like(heavy)
-    for b in range(0, HEIGHT, STEP):
-        cut = pl.ds(b, STEP)
-        k_copies[b // STEP].wait()
-        k = held[cut, :]
-        blocks = range(b // 128, (b + STEP) // 128)
-        r = jnp.concatenate([as_column(rows[i : i + 1, :] * per_row) for i in blocks])[:, :1]
-        g = jnp.concatenate([lax.broadcasted_iota(jnp.int32, (128, 1), 0) + row_ids[i] * 128 for i in blocks])
+
+    def weights(i):
+        p = places[i]
+        k = held[i]
+        r = as_column(rows[pl.ds(p, 1), :] * per_row)[:, :1]
+        g = lax.broadcasted_iota(jnp.int32, (128, 1), 0) + row_ids[p] * 128
         w = (slope * (k - r - mean_t[...]) + jnp.where(g == ident[...], base - spike, base)) * k
-        wh[cut, :], wl[cut, :] = split(w)
-        heavy[...] += jnp.sum(w.reshape(STEP // 8, 8, WIDTH), axis=0)
-        load[cut, :] = jnp.broadcast_to(jnp.sum(w, axis=1, keepdims=True), (STEP, 128))
-    for copy in copies:
+        h, l = split(w)
+        if i < 2 * RUN:
+            high[i // RUN, i % RUN * 128 : i % RUN * 128 + 128] = h
+            low[i // RUN, i % RUN * 128 : i % RUN * 128 + 128] = l
+        cut = block_at(p)
+        wh[cut, :] = h
+        wl[cut, :] = l
+        heavy[...] += jnp.sum(w.reshape(16, 8, WIDTH), axis=0)
+        load[cut, :] = jnp.broadcast_to(jnp.sum(w, axis=1, keepdims=True), (128, 128))
+
+    def product(run):
+        mixed = dot3(high[run], low[run], th[...], tl[...], NN)
+        for i in range(RUN):
+            outs[run * RUN + i][...] = mixed[i * 128 : i * 128 + 128]
+
+    def finish(run):
+        for i in range(run * RUN, run * RUN + RUN):
+            cut = block_at(places[i])
+            p = ph[cut, :].astype(F32) + pl_[cut, :].astype(F32)
+            outs[i][...] = load[cut, :1] * p - outs[i][...]
+
+    for copy in k_copies[:RUN]:
         copy.wait()
-    page_blocks([order[p] for p in FIRST], outs, wh, wl, load, ph, pl_, th, tl, 5)
+    for i in range(RUN):
+        weights(i)
+    for copy in t_copies + k_copies[RUN : 2 * RUN]:
+        copy.wait()
+    product(0)
+    for i in range(RUN, 2 * RUN):
+        weights(i)
+    for copy in p_copies + k_copies[2 * RUN :]:
+        copy.wait()
+    product(1)
+    for i in range(2 * RUN, 16):
+        weights(i)
+    finish(0)
+    finish(1)
 
 
 def weigh(facts, row_ids, col_ids, order, kern, ph, pl_, th, tl, rows, cols):
@@ -316,11 +356,13 @@
         scratch_shapes=[
             pltpu.VMEM((1, WIDTH), F32),
             pltpu.VMEM((1, WIDTH), jnp.int32),
-            pltpu.VMEM((HEIGHT, WIDTH), F32),
-            pltpu.SemaphoreType.DMA((HEIGHT // STEP,)),
+            pltpu.VMEM((16, 128, WIDTH), F32),
+            pltpu.VMEM((2, RUN * 128, WIDTH), BF16),
+            pltpu.VMEM((2, RUN * 128, WIDTH), BF16),
+            pltpu.SemaphoreType.DMA((16,)),
             pltpu.SemaphoreType.DMA((4,)),
         ],
-        compiler_params=pltpu.CompilerParams(vmem_limit_bytes=22 * 2**20),
+        compiler_params=pltpu.CompilerParams(vmem_limit_bytes=24 * 2**20),
         cost_estimate=pl.CostEstimate(flops=10000, bytes_accessed=100000, transcendentals=0),
         name="weigh",
     )(facts, row_ids, col_ids, order, *map(afar, (kern, ph, pl_, th, tl)), rows, cols)
@@ -366,10 +408,6 @@
     )(heavy, *map(near, (wh, wl, ph, pl_, th, tl)))
 
 
-def line_sum(x):
-    return jnp.sum(x, axis=0, keepdims=True)
-
-
 def without_mean(x):
     return x - jnp.mean(x)
 
@@ -450,7 +488,7 @@
     r, c = merged(row_merge, 2, r, r_got), merged(column_merge, 1, c, c_got)
     r_got, c_got = together(from_pair(r, "y", 1), from_pair(c, "z", 1))
     r, c = merged(row_merge, 4, r, r_got), merged(column_merge, 2, c, c_got)
-    r_got, c_got = together(from_pair(r, "y", 2), from_pair(c, "z", 2))
+    r_got, c_got = together(from_pair(r, "y", 3), from_pair(c, "z", 3))
     r, c = merged(row_merge, 8, r, r_got), merged(column_merge, 4, c, c_got)
     s, u = small(row_facts, 8, r), small(block_facts, 8, c)
     u = merged(block_merge, 1, u, from_core(u))
@@ -458,7 +496,7 @@
     s, u = small(plain_merge, 8, s, s_got), merged(block_merge, 2, u, u_got)
     s_got, u_got = together(from_pair(s, "z", 1), from_pair(u, "y", 1))
     s, u = small(plain_merge, 8, s, s_got), merged(block_merge, 4, u, u_got)
-    s_got, u_got = together(from_pair(s, "z", 2), from_pair(u, "y", 2))
+    s_got, u_got = together(from_pair(s, "z", 3), from_pair(u, "y", 3))
     s, u = small(plain_merge, 8, s, s_got), merged(block_merge, 8, u, u_got)
     return r, c, small(last_merge, 8, s, u)
 
@@ -492,13 +530,13 @@
         facts, row_ids, col_ids, order, kern, ph, pl_, th, tl, r, c
     )
     pages_ring, texts_ring = Ring("y", from_side), Ring("z", from_twin)
-    o_up, o_down, o_far, far, other, heavy = together(
-        *[early[i] + from_core(early[i + 5]) for i in range(5)], heavy
-    )
+    o_up, o_down, o_far, far, other = [early[i] + from_core(early[i + 5]) for i in range(5)]
+    o_up, o_down, o_far, heavy = together(o_up, o_down, o_far, heavy)
     pages_ring.first(o_up, o_down, o_far)
     late = text_part(512, heavy, wh, wl, ph, pl_, th, tl)
     texts_ring.first(late[1], late[3], late[2])
-    soon = text_part(0, together(heavy, *late)[0], wh, wl, ph, pl_, th, tl)
+    far, other, heavy, *late = together(far, other, heavy, *late)
+    soon = text_part(0, heavy, wh, wl, ph, pl_, th, tl)
     *soon, order, g0, g1, g2 = together(*soon, order, *pages_ring.got)
     pages_ring.got = (g0, g1, g2)
     pages_ring.second(far, other)

time: 217 us -> 213 us (0.982)
  starting transfers between devices: 59.9 us -> 56.9 us
    ppermute x8, starting transfers between devices: 15.6 us -> 12.9 us  [from_pair(): lax.ppermute(x, axis, [(i, i ^ bit) for i in range(lax.axis_size(axis))])]
  transfers between devices with their start and end apart: 47 -> 47, of which waited for: 29 -> 28; matrix products, arithmetic and copies ran while one was open for 1% -> 1% of each run, Pallas kernels for 11% -> 11%
where the time goes in v3:
time: 213 us; the launch traced here: 210 us
  waiting for transfers between devices  71.3 us (33%)
  Pallas kernels  61.7 us (29%)
  starting transfers between devices  56.9 us (27%)
  between operations  15.4 us (7%)
  other arithmetic  3.14 us (1%)
    ppermute x32, starting transfers between devices, from_next(): return lax.ppermute(x, axis, [(i, (i - step) % n) for i in range(n)])  32.8 us
    ppermute x32, waiting for transfers between devices, from_next(): return lax.ppermute(x, axis, [(i, (i - step) % n) for i in range(n)])  31.4 us
    pallas_call x1, Pallas kernels, cross(): pl.pallas_call(cross_kernel, out_shape=[pltpu.HBM((HEIGHT, WIDTH), F32),...  22.4 us
    ppermute x6, waiting for transfers between devices, from_twin(): return lax.ppermute(x, ('xh', 'xl'), [(0, 3), (3, 0), (1, 2), (2, 1)])  21.1 us
    pallas_call x1, Pallas kernels, weigh(): pl.pallas_call(weight_kernel, out_shape=[pltpu.VMEM((SHARE, DEPTH), F32)]...  15.3 us
    pallas_call x2, Pallas kernels, text_part(): pl.pallas_call(functools.partial(text_kernel, start), out_shape=[pltpu.VM...  13.6 us
    ppermute x8, starting transfers between devices, from_pair(): lax.ppermute(x, axis, [(i, i ^ bit) for i in range(lax.axis_size(axis))])  12.9 us
    ppermute x6, starting transfers between devices, from_twin(): return lax.ppermute(x, ('xh', 'xl'), [(0, 3), (3, 0), (1, 2), (2, 1)])  11.1 us
  transfers between devices with their start and end apart: 47, of which 28 were waited for; matrix products, arithmetic and copies ran while one was open for 1% of the time, Pallas kernels for 11%

profile of v3, /device:TPU:0, one launch (start us, length us, event | category | flops | bytes accessed | tf_op | source)
XLA Modules:
  0.0 209.8 jit_solution(18251300999832681076)
XLA Ops:
  7.9 4.2 %collective-permute-start.1 = (f32[128,1024]{1,0:T(8,128)}, f32[128,1024]{1,0:T(8,128)S(1)}, u32[]{:S(2)}, u32[]{:S(2)}) collective-permute-start(f32[128,1024]{1,0:T(8,128)} %refs_0_.1), channel_id=1, source_target_pairs={{0,96},{32,0},{64,32},{96,64},{1,97},{33,1},{65,33},{97,65},{2,98}... | collective-permute-start | bytes 1572872 | tf_op jit(solution)/shard_map/ppermute | solution.py:24
  12.1 2.8 %collective-permute-start = (f32[128,1024]{1,0:T(8,128)}, f32[128,1024]{1,0:T(8,128)S(1)}, u32[]{:S(2)}, u32[]{:S(2)}) collective-permute-start(f32[128,1024]{1,0:T(8,128)} %refs_0_.1), channel_id=1, source_target_pairs={{0,18},{18,0},{2,16},{16,2},{1,19},{19,1},{3,17},{17,3},{4,22},{22... | collective-permute-start | bytes 1572872 | tf_op jit(solution)/shard_map/ppermute | solution.py:28
  14.8 8.7 %collective-permute-done.1.refs_1_ = f32[128,1024]{1,0:T(8,128)S(1)} collective-permute-done((f32[128,1024]{1,0:T(8,128)}, f32[128,1024]{1,0:T(8,128)S(1)}, u32[]{:S(2)}, u32[]{:S(2)}) %collective-permute-start.1) | collective-permute-done | bytes 524320 | tf_op jit(solution)/shard_map/ppermute | solution.py:24
  23.6 3.3 %collective-permute-done.refs_4_ = f32[128,1024]{1,0:T(8,128)S(1)} collective-permute-done((f32[128,1024]{1,0:T(8,128)}, f32[128,1024]{1,0:T(8,128)S(1)}, u32[]{:S(2)}, u32[]{:S(2)}) %collective-permute-start) | collective-permute-done | bytes 524320 | tf_op jit(solution)/shard_map/ppermute | solution.py:28
  26.9 2.5 %collective-permute-done.2.refs_3_ = f32[128,1024]{1,0:T(8,128)S(1)} collective-permute-done((f32[128,1024]{1,0:T(8,128)}, f32[128,1024]{1,0:T(8,128)S(1)}, u32[]{:S(2)}, u32[]{:S(2)}) %collective-permute-start.2) | collective-permute-done | bytes 524320 | tf_op jit(solution)/shard_map/ppermute | solution.py:24
  29.5 3.2 %collective-permute-start.3 = (f32[64,1024]{1,0:T(8,128)S(1)}, f32[64,1024]{1,0:T(8,128)S(1)}, u32[]{:S(2)}, u32[]{:S(2)}) collective-permute-start(f32[64,1024]{1,0:T(8,128)S(1)} %slice.42), channel_id=1, source_target_pairs={{0,96},{32,0},{64,32},{96,64},{1,97},{33,1},{65,33},{97,65},{2,98}... | collective-permute-start | bytes 786440 | tf_op jit(solution)/shard_map/ppermute | solution.py:24
  32.7 4.5 %collective-permute-done.4 = f32[64,1024]{1,0:T(8,128)S(1)} collective-permute-done((f32[64,1024]{1,0:T(8,128)S(1)}, f32[64,1024]{1,0:T(8,128)S(1)}, u32[]{:S(2)}, u32[]{:S(2)}) %collective-permute-start.4) | collective-permute-done | bytes 262176 | tf_op jit(solution)/shard_map/ppermute | solution.py:24
  38.0 3.4 %collective-permute-start.5 = (f32[128,1024]{1,0:T(8,128)S(1)}, f32[128,1024]{1,0:T(8,128)}, u32[]{:S(2)}, u32[]{:S(2)}) collective-permute-start(f32[128,1024]{1,0:T(8,128)S(1)} %collective-permute-done.refs_4_), channel_id=1, source_target_pairs={{0,96},{32,0},{64,32},{96,64},{1,97},{33,1},{65,33},{97,65},{2,98}... | collective-permute-start | bytes 1572872 | tf_op jit(solution)/shard_map/ppermute | solution.py:24
  42.2 7.7 %collective-permute-done.6.refs_6_ = f32[128,1024]{1,0:T(8,128)S(1)} collective-permute-done((f32[128,1024]{1,0:T(8,128)S(1)}, f32[128,1024]{1,0:T(8,128)S(1)}, u32[]{:S(2)}, u32[]{:S(2)}) %collective-permute-start.6) | collective-permute-done | bytes 524320 | tf_op jit(solution)/shard_map/ppermute | solution.py:28
  50.3 1.0 copy-done
  51.3 4.0 %text_split.1 = (f32[1,1024]{1,0:T(1,128)S(1)}, bf16[1024,1024]{1,0:T(8,128)(2,1)}, bf16[1024,1024]{1,0:T(8,128)(2,1)}) custom-call(f32[128,1024]{1,0:T(8,128)S(1)} %copy-done, f32[128,1024]{1,0:T(8,128)S(1)} %collective-permute-done.1.refs_1_, f32[128,1024]{1,0:T(8,128)S(1)} %constant_dynamic-update-slice_fusion.refs_2_, ...), custom_call_target="tpu_custom_call" | custom-call | flops 16777216 | bytes 8388608 | tf_op jit(solution)/shard_map/text_split/pallas_call | solution.py:125
  55.3 9.0 %all-gather.2.cloned.1.call-done.pages = f32[2048,1024]{1,0:T(8,128)} async-done(((f32[128,1024]{1,0:T(8,128)}), f32[2048,1024]{1,0:T(8,128)}) %all-gather.2.cloned.1.call-update) | async-done | bytes 8388624 | tf_op jit(solution)/shard_map/all_gather | solution.py:508
  64.3 22.4 %cross.1 = (f32[2048,1024]{1,0:T(8,128)}, bf16[2048,1024]{1,0:T(8,128)(2,1)}, bf16[2048,1024]{1,0:T(8,128)(2,1)}, f32[24,128]{1,0:T(8,128)S(1)}, f32[16,128]{1,0:T(8,128)S(1)}) custom-call(f32[1]{0:T(128)} %bitcast.1.inverse_ref, s32[16]{0:T(128)S(1)} %iota_add_fusion.row_ids.refs_1_, s32[8]{0:T(128)S(1)} %stack.86.col_ids.refs_2_, ...), custom_call_target="tpu_custom_call" | custom-call | flops 12884901888 | bytes 8388608 | tf_op jit(solution)/shard_map/cross/pallas_call | solution.py:224
  88.0 1.5 collective-permute-start.9
  89.5 2.2 %collective-permute-start.10 = (f32[16,128]{1,0:T(8,128)S(1)}, f32[16,128]{1,0:T(8,128)S(1)}, u32[]{:S(2)}, u32[]{:S(2)}) collective-permute-start(f32[16,128]{1,0:T(8,128)S(1)} %get-tuple-element.103.c), channel_id=1, source_target_pairs={{0,18},{18,0},{2,16},{16,2},{1,19},{19,1},{3,17},{17,3},{4,22},{22... | collective-permute-start | bytes 24584 | tf_op jit(solution)/shard_map/ppermute | solution.py:28
  91.7 2.7 %collective-permute-done.10.c_got = f32[16,128]{1,0:T(8,128)S(1)} collective-permute-done((f32[16,128]{1,0:T(8,128)S(1)}, f32[16,128]{1,0:T(8,128)S(1)}, u32[]{:S(2)}, u32[]{:S(2)}) %collective-permute-start.10) | collective-permute-done | bytes 8224 | tf_op jit(solution)/shard_map/ppermute | solution.py:28
  94.4 1.5 collective-permute-start.11
  96.0 1.7 collective-permute-start.12
  97.7 2.0 collective-permute-done.12.c_got
  99.7 1.9 collective-permute-start.13
  101.8 3.0 %collective-permute-start.14 = (f32[16,128]{1,0:T(8,128)S(1)}, f32[16,128]{1,0:T(8,128)S(1)}, u32[]{:S(2)}, u32[]{:S(2)}) collective-permute-start(f32[16,128]{1,0:T(8,128)S(1)} %small.21.c), channel_id=1, source_target_pairs={{0,96},{32,64},{64,32},{96,0},{1,97},{33,65},{65,33},{97,1},{2,98}... | collective-permute-start | bytes 24584 | tf_op jit(solution)/shard_map/ppermute | solution.py:478
  104.8 1.9 collective-permute-done.14.c_got
  107.1 2.2 %collective-permute-start.15 = (f32[8,128]{1,0:T(8,128)S(1)}, f32[8,128]{1,0:T(8,128)S(1)}, u32[]{:S(2)}, u32[]{:S(2)}) collective-permute-start(f32[8,128]{1,0:T(8,128)S(1)} %small.23.s), channel_id=1, source_target_pairs={{0,18},{18,0},{2,16},{16,2},{1,19},{19,1},{3,17},{17,3},{4,22},{22... | collective-permute-start | bytes 12296 | tf_op jit(solution)/shard_map/ppermute | solution.py:28
  109.4 2.6 %collective-permute-done.15.s_got = f32[8,128]{1,0:T(8,128)S(1)} collective-permute-done((f32[8,128]{1,0:T(8,128)S(1)}, f32[8,128]{1,0:T(8,128)S(1)}, u32[]{:S(2)}, u32[]{:S(2)}) %collective-permute-start.15) | collective-permute-done | bytes 4128 | tf_op jit(solution)/shard_map/ppermute | solution.py:28
  112.0 1.0 collective-permute-done.17.u_got
  113.9 2.7 %collective-permute-done.19.u_got = f32[8,128]{1,0:T(8,128)S(1)} collective-permute-done((f32[8,128]{1,0:T(8,128)S(1)}, f32[8,128]{1,0:T(8,128)S(1)}, u32[]{:S(2)}, u32[]{:S(2)}) %collective-permute-start.19) | collective-permute-done | bytes 4128 | tf_op jit(solution)/shard_map/ppermute | solution.py:478
  118.2 2.9 %collective-permute-start.20 = (f32[8,128]{1,0:T(8,128)S(1)}, f32[8,128]{1,0:T(8,128)S(1)}, u32[]{:S(2)}, u32[]{:S(2)}) collective-permute-start(f32[8,128]{1,0:T(8,128)S(1)} %small.29.s), channel_id=1, source_target_pairs={{0,96},{32,64},{64,32},{96,0},{1,97},{33,65},{65,33},{97,1},{2,98}... | collective-permute-start | bytes 12296 | tf_op jit(solution)/shard_map/ppermute | solution.py:478
  122.0 1.0 collective-permute-done.20.s_got
  123.3 15.3 %weigh.1 = (f32[128,1024]{1,0:T(8,128)S(1)}, f32[128,1024]{1,0:T(8,128)S(1)}, f32[128,1024]{1,0:T(8,128)S(1)}, f32[128,1024]{1,0:T(8,128)S(1)}, f32[128,1024]{1,...) custom-call(f32[8,128]{1,0:T(8,128)S(1)} %small.33.refs_0_, ...), custom_call_target="tpu_custom_call" | custom-call | flops 10000 | bytes 100000 | tf_op jit(solution)/shard_map/weigh/pallas_call | solution.py:347
  142.1 1.4 collective-permute-start.27
  143.5 1.9 collective-permute-start.28
  145.6 6.8 %text_part.2 = (f32[128,1024]{1,0:T(8,128)S(1)}, f32[128,1024]{1,0:T(8,128)S(1)}, f32[128,1024]{1,0:T(8,128)S(1)}, f32[128,1024]{1,0:T(8,128)S(1)}) custom-call(f32[8,1024]{1,0:T(8,128)S(1)} %get-tuple-element.141.heavy, bf16[2048,1024]{1,0:T(8,128)(2,1)S(1)} %get-tuple-element.131.wh.refs_1_, bf16[2048,1024]{1,0:T(8,128)(2,1)S(1)} %get-tuple-element.132.wl.refs_2_, ...), custom_call_target="tpu_custom_call" | custom-call | flops 10000 | bytes 100000 | tf_op jit(solution)/shard_map/text_part/pallas_call | solution.py:400
  152.6 1.3 collective-permute-start.32
  153.9 6.8 %text_part.3 = (f32[128,1024]{1,0:T(8,128)S(1)}, f32[128,1024]{1,0:T(8,128)S(1)}, f32[128,1024]{1,0:T(8,128)S(1)}, f32[128,1024]{1,0:T(8,128)S(1)}) custom-call(f32[8,1024]{1,0:T(8,128)S(1)} %get-tuple-element.141.heavy, bf16[2048,1024]{1,0:T(8,128)(2,1)S(1)} %get-tuple-element.131.wh.refs_1_, bf16[2048,1024]{1,0:T(8,128)(2,1)S(1)} %get-tuple-element.132.wl.refs_2_, ...), custom_call_target="tpu_custom_call" | custom-call | flops 10000 | bytes 100000 | tf_op jit(solution)/shard_map/text_part/pallas_call | solution.py:400
  160.8 3.3 %collective-permute-start.31 = (f32[128,1024]{1,0:T(8,128)S(1)}, f32[128,1024]{1,0:T(8,128)S(1)}, u32[]{:S(2)}, u32[]{:S(2)}) collective-permute-start(f32[128,1024]{1,0:T(8,128)S(1)} %get-tuple-element.140), channel_id=1, source_target_pairs={{0,96},{32,0},{64,32},{96,64},{1,97},{33,1},{65,33},{97,65},{2,98}... | collective-permute-start | bytes 1572872 | tf_op jit(solution)/shard_map/ppermute | solution.py:24
  164.2 1.7 collective-permute-start.35
  166.0 1.1 collective-permute-start.34
  167.1 1.0 collective-permute-start.33
  168.1 5.7 %page_part.1 = (f32[128,1024]{1,0:T(8,128)S(1)}, f32[128,1024]{1,0:T(8,128)S(1)}, f32[128,1024]{1,0:T(8,128)S(1)}, f32[128,1024]{1,0:T(8,128)S(1)}, f32[128,1024]{1,0:T(8,128)S(1)}, /*index=5*/f32[128,1024]{1,0:T(8,128)S(1)}) custom-call(s32[16]{0:T(128)S(1)} %stack.103.refs_3_.refs_0_, bf16[2048,1024]{1,0:T(8,128)(2,1)S(1)} %get-tuple-element.131.wh.refs_1_, ...), custom_call_target="tpu_custom_call" | custom-call | flops 10000 | bytes 100000 | tf_op jit(solution)/shard_map/page_part/pallas_call | solution.py:377
  175.2 1.8 collective-permute-done.35
  177.3 3.2 %collective-permute-start.43 = (f32[64,1024]{1,0:T(8,128)S(1)}, f32[64,1024]{1,0:T(8,128)S(1)}, u32[]{:S(2)}, u32[]{:S(2)}) collective-permute-start(f32[64,1024]{1,0:T(8,128)S(1)} %get-tuple-element.185), channel_id=1, source_target_pairs={{0,96},{32,0},{64,32},{96,64},{1,97},{33,1},{65,33},{97,65},{2,98}... | collective-permute-start | bytes 786440 | tf_op jit(solution)/shard_map/ppermute | solution.py:24
  181.1 3.7 %collective-permute-done.41 = f32[64,1024]{1,0:T(8,128)S(1)} collective-permute-done((f32[64,1024]{1,0:T(8,128)S(1)}, f32[64,1024]{1,0:T(8,128)S(1)}, u32[]{:S(2)}, u32[]{:S(2)}) %collective-permute-start.41) | collective-permute-done | bytes 262176 | tf_op jit(solution)/shard_map/ppermute | solution.py:24
  184.8 2.0 collective-permute-start.45
  187.1 1.3 collective-permute-start.44
  189.7 1.2 collective-permute-start.40
  191.9 4.8 %collective-permute-done.45 = f32[128,1024]{1,0:T(8,128)S(1)} collective-permute-done((f32[128,1024]{1,0:T(8,128)S(1)}, f32[128,1024]{1,0:T(8,128)S(1)}, u32[]{:S(2)}, u32[]{:S(2)}) %collective-permute-start.45) | collective-permute-done | bytes 524320 | tf_op jit(solution)/shard_map/ppermute | solution.py:28
  197.6 2.0 collective-permute-done.42
  200.6 1.3 collective-permute-done.39
  (101 shorter events, 19.2 us)
Async XLA Ops:
  7.2 57.1 %all-gather.2.cloned.1.call-start = ((), (), s32[]{:S(2)}) async-start(), calls=%async_computation | async-start | bytes 8912896 | tf_op jit(solution)/shard_map/all_gather | solution.py:508
  7.9 15.7 %collective-permute-start.1 = (f32[128,1024]{1,0:T(8,128)}, f32[128,1024]{1,0:T(8,128)S(1)}, u32[]{:S(2)}, u32[]{:S(2)}) collective-permute-start(f32[128,1024]{1,0:T(8,128)} %refs_0_.1), channel_id=1, source_target_pairs={{0,96},{32,0},{64,32},{96,64},{1,97},{33,1},{65,33},{97,65},{2,98}... | collective-permute-start | bytes 1572872 | tf_op jit(solution)/shard_map/ppermute | solution.py:24
  12.1 14.8 %collective-permute-start = (f32[128,1024]{1,0:T(8,128)}, f32[128,1024]{1,0:T(8,128)S(1)}, u32[]{:S(2)}, u32[]{:S(2)}) collective-permute-start(f32[128,1024]{1,0:T(8,128)} %refs_0_.1), channel_id=1, source_target_pairs={{0,18},{18,0},{2,16},{16,2},{1,19},{19,1},{3,17},{17,3},{4,22},{22... | collective-permute-start | bytes 1572872 | tf_op jit(solution)/shard_map/ppermute | solution.py:28
  14.8 14.5 %collective-permute-start.2 = (f32[128,1024]{1,0:T(8,128)}, f32[128,1024]{1,0:T(8,128)S(1)}, u32[]{:S(2)}, u32[]{:S(2)}) collective-permute-start(f32[128,1024]{1,0:T(8,128)} %refs_0_.1), channel_id=1, source_target_pairs={{0,32},{32,64},{64,96},{96,0},{1,33},{33,65},{65,97},{97,1},{2,34}... | collective-permute-start | bytes 1572872 | tf_op jit(solution)/shard_map/ppermute | solution.py:24
  29.4 7.8 %collective-permute-start.4 = (f32[64,1024]{1,0:T(8,128)S(1)}, f32[64,1024]{1,0:T(8,128)S(1)}, u32[]{:S(2)}, u32[]{:S(2)}) collective-permute-start(f32[64,1024]{1,0:T(8,128)S(1)} %slice.43), channel_id=1, source_target_pairs={{0,32},{32,64},{64,96},{96,0},{1,33},{33,65},{65,97},{97,1},{2,34}... | collective-permute-start | bytes 786440 | tf_op jit(solution)/shard_map/ppermute | solution.py:24
  29.5 7.8 %collective-permute-start.3 = (f32[64,1024]{1,0:T(8,128)S(1)}, f32[64,1024]{1,0:T(8,128)S(1)}, u32[]{:S(2)}, u32[]{:S(2)}) collective-permute-start(f32[64,1024]{1,0:T(8,128)S(1)} %slice.42), channel_id=1, source_target_pairs={{0,96},{32,0},{64,32},{96,64},{1,97},{33,1},{65,33},{97,65},{2,98}... | collective-permute-start | bytes 786440 | tf_op jit(solution)/shard_map/ppermute | solution.py:24
  37.3 12.5 %collective-permute-start.6 = (f32[128,1024]{1,0:T(8,128)S(1)}, f32[128,1024]{1,0:T(8,128)S(1)}, u32[]{:S(2)}, u32[]{:S(2)}) collective-permute-start(f32[128,1024]{1,0:T(8,128)S(1)} %constant_dynamic-update-slice_fusion.refs_2_), channel_id=1, source_target_pairs={{0,18},{18,0},{2,16},{16,2},{1,19},{19,1},{3,17},{17,3},{4,22},{22... | collective-permute-start | bytes 1572872 | tf_op jit(solution)/shard_map/ppermute | solution.py:28
  38.0 12.3 %collective-permute-start.7 = (f32[128,1024]{1,0:T(8,128)S(1)}, f32[128,1024]{1,0:T(8,128)S(1)}, u32[]{:S(2)}, u32[]{:S(2)}) collective-permute-start(f32[128,1024]{1,0:T(8,128)S(1)} %collective-permute-done.refs_4_), channel_id=1, source_target_pairs={{0,32},{32,64},{64,96},{96,0},{1,33},{33,65},{65,97},{97,1},{2,34}... | collective-permute-start | bytes 1572872 | tf_op jit(solution)/shard_map/ppermute | solution.py:24
  38.0 12.3 %collective-permute-start.5 = (f32[128,1024]{1,0:T(8,128)S(1)}, f32[128,1024]{1,0:T(8,128)}, u32[]{:S(2)}, u32[]{:S(2)}) collective-permute-start(f32[128,1024]{1,0:T(8,128)S(1)} %collective-permute-done.refs_4_), channel_id=1, source_target_pairs={{0,96},{32,0},{64,32},{96,64},{1,97},{33,1},{65,33},{97,65},{2,98}... | collective-permute-start | bytes 1572872 | tf_op jit(solution)/shard_map/ppermute | solution.py:24
  50.3 1.0 copy-start
  86.7 1.3 collective-permute-start.8
  88.0 6.3 %collective-permute-start.9 = (f32[24,128]{1,0:T(8,128)S(1)}, f32[24,128]{1,0:T(8,128)S(1)}, u32[]{:S(2)}, u32[]{:S(2)}) collective-permute-start(f32[24,128]{1,0:T(8,128)S(1)} %small.17.r), channel_id=1, source_target_pairs={{0,2},{2,0},{1,3},{3,1},{4,6},{6,4},{5,7},{7,5},{8,10},{10,8},{9,1... | collective-permute-start | bytes 36872 | tf_op jit(solution)/shard_map/ppermute | solution.py:24
  89.5 4.9 %collective-permute-start.10 = (f32[16,128]{1,0:T(8,128)S(1)}, f32[16,128]{1,0:T(8,128)S(1)}, u32[]{:S(2)}, u32[]{:S(2)}) collective-permute-start(f32[16,128]{1,0:T(8,128)S(1)} %get-tuple-element.103.c), channel_id=1, source_target_pairs={{0,18},{18,0},{2,16},{16,2},{1,19},{19,1},{3,17},{17,3},{4,22},{22... | collective-permute-start | bytes 24584 | tf_op jit(solution)/shard_map/ppermute | solution.py:28
  94.4 5.3 %collective-permute-start.11 = (f32[24,128]{1,0:T(8,128)S(1)}, f32[24,128]{1,0:T(8,128)S(1)}, u32[]{:S(2)}, u32[]{:S(2)}) collective-permute-start(f32[24,128]{1,0:T(8,128)S(1)} %small.18.r), channel_id=1, source_target_pairs={{0,4},{4,0},{8,12},{12,8},{1,5},{5,1},{9,13},{13,9},{2,6},{6,2},{1... | collective-permute-start | bytes 36872 | tf_op jit(solution)/shard_map/ppermute | solution.py:478
  96.0 3.7 %collective-permute-start.12 = (f32[16,128]{1,0:T(8,128)S(1)}, f32[16,128]{1,0:T(8,128)S(1)}, u32[]{:S(2)}, u32[]{:S(2)}) collective-permute-start(f32[16,128]{1,0:T(8,128)S(1)} %small.19.c), channel_id=1, source_target_pairs={{0,32},{32,0},{64,96},{96,64},{1,33},{33,1},{65,97},{97,65},{2,34}... | collective-permute-start | bytes 24584 | tf_op jit(solution)/shard_map/ppermute | solution.py:478
  99.7 7.0 %collective-permute-start.13 = (f32[24,128]{1,0:T(8,128)S(1)}, f32[24,128]{1,0:T(8,128)S(1)}, u32[]{:S(2)}, u32[]{:S(2)}) collective-permute-start(f32[24,128]{1,0:T(8,128)S(1)} %small.20.r), channel_id=1, source_target_pairs={{0,12},{4,8},{8,4},{12,0},{1,13},{5,9},{9,5},{13,1},{2,14},{6,10},... | collective-permute-start | bytes 36872 | tf_op jit(solution)/shard_map/ppermute | solution.py:478
  101.8 4.9 %collective-permute-start.14 = (f32[16,128]{1,0:T(8,128)S(1)}, f32[16,128]{1,0:T(8,128)S(1)}, u32[]{:S(2)}, u32[]{:S(2)}) collective-permute-start(f32[16,128]{1,0:T(8,128)S(1)} %small.21.c), channel_id=1, source_target_pairs={{0,96},{32,64},{64,32},{96,0},{1,97},{33,65},{65,33},{97,1},{2,98}... | collective-permute-start | bytes 24584 | tf_op jit(solution)/shard_map/ppermute | solution.py:478
  107.0 2.4 %collective-permute-start.16 = (f32[8,128]{1,0:T(8,128)S(1)}, f32[8,128]{1,0:T(8,128)S(1)}, u32[]{:S(2)}, u32[]{:S(2)}) collective-permute-start(f32[8,128]{1,0:T(8,128)S(1)} %small.25.u), channel_id=1, source_target_pairs={{0,1},{1,0},{2,3},{3,2},{4,5},{5,4},{6,7},{7,6},{8,9},{9,8},{10,11... | collective-permute-start | bytes 12296 | tf_op jit(solution)/shard_map/ppermute | solution.py:24
  107.1 4.9 %collective-permute-start.15 = (f32[8,128]{1,0:T(8,128)S(1)}, f32[8,128]{1,0:T(8,128)S(1)}, u32[]{:S(2)}, u32[]{:S(2)}) collective-permute-start(f32[8,128]{1,0:T(8,128)S(1)} %small.23.s), channel_id=1, source_target_pairs={{0,18},{18,0},{2,16},{16,2},{1,19},{19,1},{3,17},{17,3},{4,22},{22... | collective-permute-start | bytes 12296 | tf_op jit(solution)/shard_map/ppermute | solution.py:28
  109.3 3.7 %collective-permute-start.17 = (f32[8,128]{1,0:T(8,128)S(1)}, f32[8,128]{1,0:T(8,128)S(1)}, u32[]{:S(2)}, u32[]{:S(2)}) collective-permute-start(f32[8,128]{1,0:T(8,128)S(1)} %small.26.u), channel_id=1, source_target_pairs={{0,2},{2,0},{1,3},{3,1},{4,6},{6,4},{5,7},{7,5},{8,10},{10,8},{9,1... | collective-permute-start | bytes 12296 | tf_op jit(solution)/shard_map/ppermute | solution.py:24
  113.0 3.6 %collective-permute-start.19 = (f32[8,128]{1,0:T(8,128)S(1)}, f32[8,128]{1,0:T(8,128)S(1)}, u32[]{:S(2)}, u32[]{:S(2)}) collective-permute-start(f32[8,128]{1,0:T(8,128)S(1)} %small.28.u), channel_id=1, source_target_pairs={{0,4},{4,0},{8,12},{12,8},{1,5},{5,1},{9,13},{13,9},{2,6},{6,2},{1... | collective-permute-start | bytes 12296 | tf_op jit(solution)/shard_map/ppermute | solution.py:478
  113.6 3.6 %collective-permute-start.18 = (f32[8,128]{1,0:T(8,128)S(1)}, f32[8,128]{1,0:T(8,128)S(1)}, u32[]{:S(2)}, u32[]{:S(2)}) collective-permute-start(f32[8,128]{1,0:T(8,128)S(1)} %small.27.s), channel_id=1, source_target_pairs={{0,32},{32,0},{64,96},{96,64},{1,33},{33,1},{65,97},{97,65},{2,34}... | collective-permute-start | bytes 12296 | tf_op jit(solution)/shard_map/ppermute | solution.py:478
  117.2 4.8 %collective-permute-start.21 = (f32[8,128]{1,0:T(8,128)S(1)}, f32[8,128]{1,0:T(8,128)S(1)}, u32[]{:S(2)}, u32[]{:S(2)}) collective-permute-start(f32[8,128]{1,0:T(8,128)S(1)} %small.30.u), channel_id=1, source_target_pairs={{0,12},{4,8},{8,4},{12,0},{1,13},{5,9},{9,5},{13,1},{2,14},{6,10},... | collective-permute-start | bytes 12296 | tf_op jit(solution)/shard_map/ppermute | solution.py:478
  118.2 4.8 %collective-permute-start.20 = (f32[8,128]{1,0:T(8,128)S(1)}, f32[8,128]{1,0:T(8,128)S(1)}, u32[]{:S(2)}, u32[]{:S(2)}) collective-permute-start(f32[8,128]{1,0:T(8,128)S(1)} %small.29.s), channel_id=1, source_target_pairs={{0,96},{32,64},{64,32},{96,0},{1,97},{33,65},{65,33},{97,1},{2,98}... | collective-permute-start | bytes 12296 | tf_op jit(solution)/shard_map/ppermute | solution.py:478
  138.6 2.0 collective-permute-start.24
  138.7 2.6 %collective-permute-start.25 = (f32[128,1024]{1,0:T(8,128)S(1)}, f32[128,1024]{1,0:T(8,128)S(1)}, u32[]{:S(2)}, u32[]{:S(2)}) collective-permute-start(f32[128,1024]{1,0:T(8,128)S(1)} %get-tuple-element.126), channel_id=1, source_target_pairs={{0,1},{1,0},{2,3},{3,2},{4,5},{5,4},{6,7},{7,6},{8,9},{9,8},{10,11... | collective-permute-start | bytes 1572872 | tf_op jit(solution)/shard_map/ppermute | solution.py:24
  139.2 2.9 %collective-permute-start.26 = (f32[128,1024]{1,0:T(8,128)S(1)}, f32[128,1024]{1,0:T(8,128)S(1)}, u32[]{:S(2)}, u32[]{:S(2)}) collective-permute-start(f32[128,1024]{1,0:T(8,128)S(1)} %get-tuple-element.128), channel_id=1, source_target_pairs={{0,1},{1,0},{2,3},{3,2},{4,5},{5,4},{6,7},{7,6},{8,9},{9,8},{10,11... | collective-permute-start | bytes 1572872 | tf_op jit(solution)/shard_map/ppermute | solution.py:24
  139.2 13.2 %collective-permute-start.22 = (f32[128,1024]{1,0:T(8,128)S(1)}, f32[128,1024]{1,0:T(8,128)S(1)}, u32[]{:S(2)}, u32[]{:S(2)}) collective-permute-start(f32[128,1024]{1,0:T(8,128)S(1)} %get-tuple-element.120), channel_id=1, source_target_pairs={{0,1},{1,0},{2,3},{3,2},{4,5},{5,4},{6,7},{7,6},{8,9},{9,8},{10,11... | collective-permute-start | bytes 1572872 | tf_op jit(solution)/shard_map/ppermute | solution.py:24
  139.7 12.9 %collective-permute-start.23 = (f32[128,1024]{1,0:T(8,128)S(1)}, f32[128,1024]{1,0:T(8,128)S(1)}, u32[]{:S(2)}, u32[]{:S(2)}) collective-permute-start(f32[128,1024]{1,0:T(8,128)S(1)} %get-tuple-element.122), channel_id=1, source_target_pairs={{0,1},{1,0},{2,3},{3,2},{4,5},{5,4},{6,7},{7,6},{8,9},{9,8},{10,11... | collective-permute-start | bytes 1572872 | tf_op jit(solution)/shard_map/ppermute | solution.py:24
  142.1 18.7 %collective-permute-start.27 = (f32[128,1024]{1,0:T(8,128)S(1)}, f32[128,1024]{1,0:T(8,128)S(1)}, u32[]{:S(2)}, u32[]{:S(2)}) collective-permute-start(f32[128,1024]{1,0:T(8,128)S(1)} %add.367), channel_id=1, source_target_pairs={{0,4},{4,8},{8,12},{12,0},{1,5},{5,9},{9,13},{13,1},{2,6},{6,10},{... | collective-permute-start | bytes 1572872 | tf_op jit(solution)/shard_map/ppermute | solution.py:24
  143.5 20.6 %collective-permute-start.28 = (f32[128,1024]{1,0:T(8,128)S(1)}, f32[128,1024]{1,0:T(8,128)S(1)}, u32[]{:S(2)}, u32[]{:S(2)}) collective-permute-start(f32[128,1024]{1,0:T(8,128)S(1)} %add.368), channel_id=1, source_target_pairs={{0,12},{4,0},{8,4},{12,8},{1,13},{5,1},{9,5},{13,9},{2,14},{6,2},{... | collective-permute-start | bytes 1572872 | tf_op jit(solution)/shard_map/ppermute | solution.py:24
  145.4 18.6 %collective-permute-start.29 = (f32[128,1024]{1,0:T(8,128)S(1)}, f32[128,1024]{1,0:T(8,128)S(1)}, u32[]{:S(2)}, u32[]{:S(2)}) collective-permute-start(f32[128,1024]{1,0:T(8,128)S(1)} %add.369), channel_id=1, source_target_pairs={{0,2},{2,0},{1,3},{3,1},{4,6},{6,4},{5,7},{7,5},{8,10},{10,8},{9,1... | collective-permute-start | bytes 1572872 | tf_op jit(solution)/shard_map/ppermute | solution.py:24
  152.4 14.7 %collective-permute-start.30 = (f32[128,1024]{1,0:T(8,128)S(1)}, f32[128,1024]{1,0:T(8,128)S(1)}, u32[]{:S(2)}, u32[]{:S(2)}) collective-permute-start(f32[128,1024]{1,0:T(8,128)S(1)} %get-tuple-element.138), channel_id=1, source_target_pairs={{0,32},{32,64},{64,96},{96,0},{1,33},{33,65},{65,97},{97,1},{2,34}... | collective-permute-start | bytes 1572872 | tf_op jit(solution)/shard_map/ppermute | solution.py:24
  152.6 21.2 %collective-permute-start.32 = (f32[128,1024]{1,0:T(8,128)S(1)}, f32[128,1024]{1,0:T(8,128)S(1)}, u32[]{:S(2)}, u32[]{:S(2)}) collective-permute-start(f32[128,1024]{1,0:T(8,128)S(1)} %get-tuple-element.139), channel_id=1, source_target_pairs={{0,18},{18,0},{2,16},{16,2},{1,19},{19,1},{3,17},{17,3},{4,22},{22... | collective-permute-start | bytes 1572872 | tf_op jit(solution)/shard_map/ppermute | solution.py:28
  160.8 13.7 %collective-permute-start.31 = (f32[128,1024]{1,0:T(8,128)S(1)}, f32[128,1024]{1,0:T(8,128)S(1)}, u32[]{:S(2)}, u32[]{:S(2)}) collective-permute-start(f32[128,1024]{1,0:T(8,128)S(1)} %get-tuple-element.140), channel_id=1, source_target_pairs={{0,96},{32,0},{64,32},{96,64},{1,97},{33,1},{65,33},{97,65},{2,98}... | collective-permute-start | bytes 1572872 | tf_op jit(solution)/shard_map/ppermute | solution.py:24
  164.2 12.9 %collective-permute-start.35 = (f32[128,1024]{1,0:T(8,128)S(1)}, f32[128,1024]{1,0:T(8,128)S(1)}, u32[]{:S(2)}, u32[]{:S(2)}) collective-permute-start(f32[128,1024]{1,0:T(8,128)S(1)} %add_add_fusion.1), channel_id=1, source_target_pairs={{0,2},{2,0},{1,3},{3,1},{4,6},{6,4},{5,7},{7,5},{8,10},{10,8},{9,1... | collective-permute-start | bytes 1572872 | tf_op jit(solution)/shard_map/ppermute | solution.py:24
  166.0 8.4 %collective-permute-start.34 = (f32[64,1024]{1,0:T(8,128)S(1)}, f32[64,1024]{1,0:T(8,128)S(1)}, u32[]{:S(2)}, u32[]{:S(2)}) collective-permute-start(f32[64,1024]{1,0:T(8,128)S(1)} %get-tuple-element.192), channel_id=1, source_target_pairs={{0,12},{4,0},{8,4},{12,8},{1,13},{5,1},{9,5},{13,9},{2,14},{6,2},{... | collective-permute-start | bytes 786440 | tf_op jit(solution)/shard_map/ppermute | solution.py:24
  167.1 8.1 %collective-permute-start.33 = (f32[64,1024]{1,0:T(8,128)S(1)}, f32[64,1024]{1,0:T(8,128)S(1)}, u32[]{:S(2)}, u32[]{:S(2)}) collective-permute-start(f32[64,1024]{1,0:T(8,128)S(1)} %get-tuple-element.193), channel_id=1, source_target_pairs={{0,4},{4,8},{8,12},{12,0},{1,5},{5,9},{9,13},{13,1},{2,6},{6,10},{... | collective-permute-start | bytes 786440 | tf_op jit(solution)/shard_map/ppermute | solution.py:24
  177.2 7.7 %collective-permute-start.41 = (f32[64,1024]{1,0:T(8,128)S(1)}, f32[64,1024]{1,0:T(8,128)S(1)}, u32[]{:S(2)}, u32[]{:S(2)}) collective-permute-start(f32[64,1024]{1,0:T(8,128)S(1)} %get-tuple-element.184), channel_id=1, source_target_pairs={{0,32},{32,64},{64,96},{96,0},{1,33},{33,65},{65,97},{97,1},{2,34}... | collective-permute-start | bytes 786440 | tf_op jit(solution)/shard_map/ppermute | solution.py:24
  177.3 9.6 %collective-permute-start.43 = (f32[64,1024]{1,0:T(8,128)S(1)}, f32[64,1024]{1,0:T(8,128)S(1)}, u32[]{:S(2)}, u32[]{:S(2)}) collective-permute-start(f32[64,1024]{1,0:T(8,128)S(1)} %get-tuple-element.185), channel_id=1, source_target_pairs={{0,96},{32,0},{64,32},{96,64},{1,97},{33,1},{65,33},{97,65},{2,98}... | collective-permute-start | bytes 786440 | tf_op jit(solution)/shard_map/ppermute | solution.py:24
  180.5 7.9 %collective-permute-start.36 = (f32[128,1024]{1,0:T(8,128)S(1)}, f32[128,1024]{1,0:T(8,128)S(1)}, u32[]{:S(2)}, u32[]{:S(2)}) collective-permute-start(f32[128,1024]{1,0:T(8,128)S(1)} %get-tuple-element.163), channel_id=1, source_target_pairs={{0,1},{1,0},{2,3},{3,2},{4,5},{5,4},{6,7},{7,6},{8,9},{9,8},{10,11... | collective-permute-start | bytes 1572872 | tf_op jit(solution)/shard_map/ppermute | solution.py:24
  180.5 8.8 %collective-permute-start.37 = (f32[128,1024]{1,0:T(8,128)S(1)}, f32[128,1024]{1,0:T(8,128)S(1)}, u32[]{:S(2)}, u32[]{:S(2)}) collective-permute-start(f32[128,1024]{1,0:T(8,128)S(1)} %get-tuple-element.165), channel_id=1, source_target_pairs={{0,1},{1,0},{2,3},{3,2},{4,5},{5,4},{6,7},{7,6},{8,9},{9,8},{10,11... | collective-permute-start | bytes 1572872 | tf_op jit(solution)/shard_map/ppermute | solution.py:24
  181.0 8.4 %collective-permute-start.38 = (f32[128,1024]{1,0:T(8,128)S(1)}, f32[128,1024]{1,0:T(8,128)S(1)}, u32[]{:S(2)}, u32[]{:S(2)}) collective-permute-start(f32[128,1024]{1,0:T(8,128)S(1)} %get-tuple-element.167), channel_id=1, source_target_pairs={{0,1},{1,0},{2,3},{3,2},{4,5},{5,4},{6,7},{7,6},{8,9},{9,8},{10,11... | collective-permute-start | bytes 1572872 | tf_op jit(solution)/shard_map/ppermute | solution.py:24
  184.8 11.9 %collective-permute-start.45 = (f32[128,1024]{1,0:T(8,128)S(1)}, f32[128,1024]{1,0:T(8,128)S(1)}, u32[]{:S(2)}, u32[]{:S(2)}) collective-permute-start(f32[128,1024]{1,0:T(8,128)S(1)} %add_add_fusion), channel_id=1, source_target_pairs={{0,18},{18,0},{2,16},{16,2},{1,19},{19,1},{3,17},{17,3},{4,22},{22... | collective-permute-start | bytes 1572872 | tf_op jit(solution)/shard_map/ppermute | solution.py:28
  187.1 10.5 %collective-permute-start.44 = (f32[128,1024]{1,0:T(8,128)S(1)}, f32[128,1024]{1,0:T(8,128)S(1)}, u32[]{:S(2)}, u32[]{:S(2)}) collective-permute-start(f32[128,1024]{1,0:T(8,128)S(1)} %pad_maximum_fusion.3), channel_id=1, source_target_pairs={{0,96},{32,0},{64,32},{96,64},{1,97},{33,1},{65,33},{97,65},{2,98}... | collective-permute-start | bytes 1572872 | tf_op jit(solution)/shard_map/ppermute | solution.py:24
  188.4 11.2 %collective-permute-start.42 = (f32[128,1024]{1,0:T(8,128)S(1)}, f32[128,1024]{1,0:T(8,128)S(1)}, u32[]{:S(2)}, u32[]{:S(2)}) collective-permute-start(f32[128,1024]{1,0:T(8,128)S(1)} %pad_maximum_fusion.2), channel_id=1, source_target_pairs={{0,32},{32,64},{64,96},{96,0},{1,33},{33,65},{65,97},{97,1},{2,34}... | collective-permute-start | bytes 1572872 | tf_op jit(solution)/shard_map/ppermute | solution.py:24
  189.7 10.9 %collective-permute-start.40 = (f32[128,1024]{1,0:T(8,128)S(1)}, f32[128,1024]{1,0:T(8,128)S(1)}, u32[]{:S(2)}, u32[]{:S(2)}) collective-permute-start(f32[128,1024]{1,0:T(8,128)S(1)} %pad_maximum_fusion.1), channel_id=1, source_target_pairs={{0,12},{4,0},{8,4},{12,8},{1,13},{5,1},{9,5},{13,9},{2,14},{6,2},{... | collective-permute-start | bytes 1572872 | tf_op jit(solution)/shard_map/ppermute | solution.py:24
  190.9 10.9 %collective-permute-start.39 = (f32[128,1024]{1,0:T(8,128)S(1)}, f32[128,1024]{1,0:T(8,128)S(1)}, u32[]{:S(2)}, u32[]{:S(2)}) collective-permute-start(f32[128,1024]{1,0:T(8,128)S(1)} %pad_maximum_fusion), channel_id=1, source_target_pairs={{0,4},{4,8},{8,12},{12,0},{1,5},{5,9},{9,13},{13,1},{2,6},{6,10},{... | collective-permute-start | bytes 1572872 | tf_op jit(solution)/shard_map/ppermute | solution.py:24
Sparse Core Ops, SparseCore 0:
  9.7 54.5 all-gather.1

commit v4 on v3

--- a/solution.py
+++ b/solution.py
@@ -370,7 +370,7 @@
 
 def page_kernel(*refs):
     order, wh, wl, load, ph, pl_, th, tl = refs[:8]
-    page_blocks([order[p] for p in SECOND], refs[8:], wh, wl, load, ph, pl_, th, tl, 3)
+    page_blocks([order[p] for p in SECOND], refs[8:], wh, wl, load, ph, pl_, th, tl, 6)
 
 
 def page_part(order, wh, wl, load, ph, pl_, th, tl):
@@ -387,13 +387,13 @@
 
 def text_kernel(start, heavy, wh, wl, ph, pl_, th, tl, *outs):
     load = jnp.sum(heavy[...], axis=0, keepdims=True)
-    for j in range(start, start + 512, 256):
-        folded = dot3(wh[:, j : j + 256], wl[:, j : j + 256], ph[...], pl_[...], TN)
-        for i in range(2):
-            q = j + i * 128
-            t = th[q : q + 128, :].astype(F32) + tl[q : q + 128, :].astype(F32)
-            column = as_column(load[:, q : q + 128])[:, :1]
-            outs[(q - start) // 128][...] = folded[i * 128 : i * 128 + 128] - column * t
+    cut = slice(start, start + 512)
+    folded = dot3(wh[:, cut], wl[:, cut], ph[...], pl_[...], TN)
+    for i in range(4):
+        q = start + i * 128
+        t = th[q : q + 128, :].astype(F32) + tl[q : q + 128, :].astype(F32)
+        column = as_column(load[:, q : q + 128])[:, :1]
+        outs[i][...] = folded[i * 128 : i * 128 + 128] - column * t
 
 
 def text_part(start, heavy, wh, wl, ph, pl_, th, tl):
@@ -483,20 +483,22 @@
 
 
 def statistics(r, c):
-    r = merged(row_merge, 1, r, from_core(r))
-    r_got, c_got = together(from_side(r), from_twin(c))
+    c_got = from_twin(c)
+    r_core, c = together(from_core(r), c)
+    r = merged(row_merge, 1, r, r_core)
+    r_got = from_side(r)
     r, c = merged(row_merge, 2, r, r_got), merged(column_merge, 1, c, c_got)
-    r_got, c_got = together(from_pair(r, "y", 1), from_pair(c, "z", 1))
+    r_got, c_got = (from_pair(r, "y", 1), from_pair(c, "z", 1))
     r, c = merged(row_merge, 4, r, r_got), merged(column_merge, 2, c, c_got)
-    r_got, c_got = together(from_pair(r, "y", 3), from_pair(c, "z", 3))
+    r_got, c_got = (from_pair(r, "y", 3), from_pair(c, "z", 3))
     r, c = merged(row_merge, 8, r, r_got), merged(column_merge, 4, c, c_got)
     s, u = small(row_facts, 8, r), small(block_facts, 8, c)
     u = merged(block_merge, 1, u, from_core(u))
-    s_got, u_got = together(from_twin(s), from_side(u))
+    s_got, u_got = (from_twin(s), from_side(u))
     s, u = small(plain_merge, 8, s, s_got), merged(block_merge, 2, u, u_got)
-    s_got, u_got = together(from_pair(s, "z", 1), from_pair(u, "y", 1))
+    s_got, u_got = (from_pair(s, "z", 1), from_pair(u, "y", 1))
     s, u = small(plain_merge, 8, s, s_got), merged(block_merge, 4, u, u_got)
-    s_got, u_got = together(from_pair(s, "z", 3), from_pair(u, "y", 3))
+    s_got, u_got = (from_pair(s, "z", 3), from_pair(u, "y", 3))
     s, u = small(plain_merge, 8, s, s_got), merged(block_merge, 8, u, u_got)
     return r, c, small(last_merge, 8, s, u)
 

time: 213 us -> 209 us (0.981)
  waiting for transfers between devices: 71.3 us -> 66.7 us
    ppermute x8, waiting for transfers between devices: 9.07 us -> 6.85 us  [from_pair(): lax.ppermute(x, axis, [(i, i ^ bit) for i in range(lax.axis_size(axis))])]
where the time goes in v4:
time: 209 us; the launch traced here: 206 us
  waiting for transfers between devices  66.7 us (32%)
  Pallas kernels  61.7 us (30%)
  starting transfers between devices  58.2 us (28%)
  between operations  15.3 us (7%)
  other arithmetic  3.14 us (2%)
    ppermute x32, starting transfers between devices, from_next(): return lax.ppermute(x, axis, [(i, (i - step) % n) for i in range(n)])  32.9 us
    ppermute x32, waiting for transfers between devices, from_next(): return lax.ppermute(x, axis, [(i, (i - step) % n) for i in range(n)])  31.1 us
    pallas_call x1, Pallas kernels, cross(): pl.pallas_call(cross_kernel, out_shape=[pltpu.HBM((HEIGHT, WIDTH), F32),...  22.5 us
    ppermute x6, waiting for transfers between devices, from_twin(): return lax.ppermute(x, ('xh', 'xl'), [(0, 3), (3, 0), (1, 2), (2, 1)])  19.1 us
    pallas_call x1, Pallas kernels, weigh(): pl.pallas_call(weight_kernel, out_shape=[pltpu.VMEM((SHARE, DEPTH), F32)]...  15.3 us
    ppermute x8, starting transfers between devices, from_pair(): lax.ppermute(x, axis, [(i, i ^ bit) for i in range(lax.axis_size(axis))])  14.2 us
    pallas_call x2, Pallas kernels, text_part(): pl.pallas_call(functools.partial(text_kernel, start), out_shape=[pltpu.VM...  13.5 us
    ppermute x6, starting transfers between devices, from_twin(): return lax.ppermute(x, ('xh', 'xl'), [(0, 3), (3, 0), (1, 2), (2, 1)])  11.1 us
  transfers between devices with their start and end apart: 47, of which 28 were waited for; matrix products, arithmetic and copies ran while one was open for 1% of the time, Pallas kernels for 11%

profile of v4, /device:TPU:0, one launch (start us, length us, event | category | flops | bytes accessed | tf_op | source)
XLA Modules:
  0.0 206.5 jit_solution(12609442639900430223)
XLA Ops:
  7.9 4.2 %collective-permute-start.1 = (f32[128,1024]{1,0:T(8,128)}, f32[128,1024]{1,0:T(8,128)S(1)}, u32[]{:S(2)}, u32[]{:S(2)}) collective-permute-start(f32[128,1024]{1,0:T(8,128)} %refs_0_.1), channel_id=1, source_target_pairs={{0,96},{32,0},{64,32},{96,64},{1,97},{33,1},{65,33},{97,65},{2,98}... | collective-permute-start | bytes 1572872 | tf_op jit(solution)/shard_map/ppermute | solution.py:24
  12.1 2.8 %collective-permute-start = (f32[128,1024]{1,0:T(8,128)}, f32[128,1024]{1,0:T(8,128)S(1)}, u32[]{:S(2)}, u32[]{:S(2)}) collective-permute-start(f32[128,1024]{1,0:T(8,128)} %refs_0_.1), channel_id=1, source_target_pairs={{0,18},{18,0},{2,16},{16,2},{1,19},{19,1},{3,17},{17,3},{4,22},{22... | collective-permute-start | bytes 1572872 | tf_op jit(solution)/shard_map/ppermute | solution.py:28
  14.8 8.7 %collective-permute-done.1.refs_1_ = f32[128,1024]{1,0:T(8,128)S(1)} collective-permute-done((f32[128,1024]{1,0:T(8,128)}, f32[128,1024]{1,0:T(8,128)S(1)}, u32[]{:S(2)}, u32[]{:S(2)}) %collective-permute-start.1) | collective-permute-done | bytes 524320 | tf_op jit(solution)/shard_map/ppermute | solution.py:24
  23.6 3.3 %collective-permute-done.refs_4_ = f32[128,1024]{1,0:T(8,128)S(1)} collective-permute-done((f32[128,1024]{1,0:T(8,128)}, f32[128,1024]{1,0:T(8,128)S(1)}, u32[]{:S(2)}, u32[]{:S(2)}) %collective-permute-start) | collective-permute-done | bytes 524320 | tf_op jit(solution)/shard_map/ppermute | solution.py:28
  26.9 2.5 %collective-permute-done.2.refs_3_ = f32[128,1024]{1,0:T(8,128)S(1)} collective-permute-done((f32[128,1024]{1,0:T(8,128)}, f32[128,1024]{1,0:T(8,128)S(1)}, u32[]{:S(2)}, u32[]{:S(2)}) %collective-permute-start.2) | collective-permute-done | bytes 524320 | tf_op jit(solution)/shard_map/ppermute | solution.py:24
  29.5 3.2 %collective-permute-start.3 = (f32[64,1024]{1,0:T(8,128)S(1)}, f32[64,1024]{1,0:T(8,128)S(1)}, u32[]{:S(2)}, u32[]{:S(2)}) collective-permute-start(f32[64,1024]{1,0:T(8,128)S(1)} %slice.42), channel_id=1, source_target_pairs={{0,96},{32,0},{64,32},{96,64},{1,97},{33,1},{65,33},{97,65},{2,98}... | collective-permute-start | bytes 786440 | tf_op jit(solution)/shard_map/ppermute | solution.py:24
  32.7 4.5 %collective-permute-done.4 = f32[64,1024]{1,0:T(8,128)S(1)} collective-permute-done((f32[64,1024]{1,0:T(8,128)S(1)}, f32[64,1024]{1,0:T(8,128)S(1)}, u32[]{:S(2)}, u32[]{:S(2)}) %collective-permute-start.4) | collective-permute-done | bytes 262176 | tf_op jit(solution)/shard_map/ppermute | solution.py:24
  38.0 3.4 %collective-permute-start.5 = (f32[128,1024]{1,0:T(8,128)S(1)}, f32[128,1024]{1,0:T(8,128)}, u32[]{:S(2)}, u32[]{:S(2)}) collective-permute-start(f32[128,1024]{1,0:T(8,128)S(1)} %collective-permute-done.refs_4_), channel_id=1, source_target_pairs={{0,96},{32,0},{64,32},{96,64},{1,97},{33,1},{65,33},{97,65},{2,98}... | collective-permute-start | bytes 1572872 | tf_op jit(solution)/shard_map/ppermute | solution.py:24
  42.2 7.7 %collective-permute-done.6.refs_6_ = f32[128,1024]{1,0:T(8,128)S(1)} collective-permute-done((f32[128,1024]{1,0:T(8,128)S(1)}, f32[128,1024]{1,0:T(8,128)S(1)}, u32[]{:S(2)}, u32[]{:S(2)}) %collective-permute-start.6) | collective-permute-done | bytes 524320 | tf_op jit(solution)/shard_map/ppermute | solution.py:28
  50.3 1.0 copy-done
  51.3 4.0 %text_split.1 = (f32[1,1024]{1,0:T(1,128)S(1)}, bf16[1024,1024]{1,0:T(8,128)(2,1)}, bf16[1024,1024]{1,0:T(8,128)(2,1)}) custom-call(f32[128,1024]{1,0:T(8,128)S(1)} %copy-done, f32[128,1024]{1,0:T(8,128)S(1)} %collective-permute-done.1.refs_1_, f32[128,1024]{1,0:T(8,128)S(1)} %constant_dynamic-update-slice_fusion.refs_2_, ...), custom_call_target="tpu_custom_call" | custom-call | flops 16777216 | bytes 8388608 | tf_op jit(solution)/shard_map/text_split/pallas_call | solution.py:125
  55.3 9.0 %all-gather.2.cloned.1.call-done.pages = f32[2048,1024]{1,0:T(8,128)} async-done(((f32[128,1024]{1,0:T(8,128)}), f32[2048,1024]{1,0:T(8,128)}) %all-gather.2.cloned.1.call-update) | async-done | bytes 8388624 | tf_op jit(solution)/shard_map/all_gather | solution.py:510
  64.3 22.5 %cross.1 = (f32[2048,1024]{1,0:T(8,128)}, bf16[2048,1024]{1,0:T(8,128)(2,1)}, bf16[2048,1024]{1,0:T(8,128)(2,1)}, f32[24,128]{1,0:T(8,128)S(1)}, f32[16,128]{1,0:T(8,128)S(1)}) custom-call(f32[1]{0:T(128)} %bitcast.1.inverse_ref, s32[16]{0:T(128)S(1)} %iota_add_fusion.row_ids.refs_1_, s32[8]{0:T(128)S(1)} %stack.86.col_ids.refs_2_, ...), custom_call_target="tpu_custom_call" | custom-call | flops 12884901888 | bytes 8388608 | tf_op jit(solution)/shard_map/cross/pallas_call | solution.py:224
  88.1 1.5 collective-permute-start.9
  89.6 2.1 %collective-permute-start.15 = (f32[16,128]{1,0:T(8,128)S(1)}, f32[16,128]{1,0:T(8,128)S(1)}, u32[]{:S(2)}, u32[]{:S(2)}) collective-permute-start(f32[16,128]{1,0:T(8,128)S(1)} %get-tuple-element.95.c), channel_id=1, source_target_pairs={{0,18},{18,0},{2,16},{16,2},{1,19},{19,1},{3,17},{17,3},{4,22},{22... | collective-permute-start | bytes 24584 | tf_op jit(solution)/shard_map/ppermute | solution.py:28
  91.9 1.5 collective-permute-start.10
  93.4 1.1 collective-permute-done.15.c_got
  94.6 1.5 collective-permute-start.16
  96.1 2.2 %collective-permute-done.16.c_got = f32[16,128]{1,0:T(8,128)S(1)} collective-permute-done((f32[16,128]{1,0:T(8,128)S(1)}, f32[16,128]{1,0:T(8,128)S(1)}, u32[]{:S(2)}, u32[]{:S(2)}) %collective-permute-start.16) | collective-permute-done | bytes 8224 | tf_op jit(solution)/shard_map/ppermute | solution.py:478
  98.4 2.9 %collective-permute-start.17 = (f32[16,128]{1,0:T(8,128)S(1)}, f32[16,128]{1,0:T(8,128)S(1)}, u32[]{:S(2)}, u32[]{:S(2)}) collective-permute-start(f32[16,128]{1,0:T(8,128)S(1)} %small.26.c), channel_id=1, source_target_pairs={{0,96},{32,64},{64,32},{96,0},{1,97},{33,65},{65,33},{97,1},{2,98}... | collective-permute-start | bytes 24584 | tf_op jit(solution)/shard_map/ppermute | solution.py:478
  101.4 2.3 %collective-permute-start.11 = (f32[24,128]{1,0:T(8,128)S(1)}, f32[24,128]{1,0:T(8,128)S(1)}, u32[]{:S(2)}, u32[]{:S(2)}) collective-permute-start(f32[24,128]{1,0:T(8,128)S(1)} %small.19.r), channel_id=1, source_target_pairs={{0,12},{4,8},{8,4},{12,0},{1,13},{5,9},{9,5},{13,1},{2,14},{6,10},... | collective-permute-start | bytes 36872 | tf_op jit(solution)/shard_map/ppermute | solution.py:478
  104.1 1.2 collective-permute-done.18.u_got
  105.2 1.1 collective-permute-done.11.r_got
  106.4 2.2 %collective-permute-start.12 = (f32[8,128]{1,0:T(8,128)S(1)}, f32[8,128]{1,0:T(8,128)S(1)}, u32[]{:S(2)}, u32[]{:S(2)}) collective-permute-start(f32[8,128]{1,0:T(8,128)S(1)} %small.21.s), channel_id=1, source_target_pairs={{0,18},{18,0},{2,16},{16,2},{1,19},{19,1},{3,17},{17,3},{4,22},{22... | collective-permute-start | bytes 12296 | tf_op jit(solution)/shard_map/ppermute | solution.py:28
  108.8 1.1 collective-permute-start.20
  109.9 1.4 collective-permute-done.12.s_got
  111.5 1.0 collective-permute-done.20.u_got
  112.5 2.4 %collective-permute-start.21 = (f32[8,128]{1,0:T(8,128)S(1)}, f32[8,128]{1,0:T(8,128)S(1)}, u32[]{:S(2)}, u32[]{:S(2)}) collective-permute-start(f32[8,128]{1,0:T(8,128)S(1)} %small.31.u), channel_id=1, source_target_pairs={{0,12},{4,8},{8,4},{12,0},{1,13},{5,9},{9,5},{13,1},{2,14},{6,10},... | collective-permute-start | bytes 12296 | tf_op jit(solution)/shard_map/ppermute | solution.py:478
  114.9 2.3 %collective-permute-start.14 = (f32[8,128]{1,0:T(8,128)S(1)}, f32[8,128]{1,0:T(8,128)S(1)}, u32[]{:S(2)}, u32[]{:S(2)}) collective-permute-start(f32[8,128]{1,0:T(8,128)S(1)} %small.23.s), channel_id=1, source_target_pairs={{0,96},{32,64},{64,32},{96,0},{1,97},{33,65},{65,33},{97,1},{2,98}... | collective-permute-start | bytes 12296 | tf_op jit(solution)/shard_map/ppermute | solution.py:478
  117.3 2.4 %collective-permute-done.14.s_got = f32[8,128]{1,0:T(8,128)S(1)} collective-permute-done((f32[8,128]{1,0:T(8,128)S(1)}, f32[8,128]{1,0:T(8,128)S(1)}, u32[]{:S(2)}, u32[]{:S(2)}) %collective-permute-start.14) | collective-permute-done | bytes 4128 | tf_op jit(solution)/shard_map/ppermute | solution.py:478
  120.0 15.3 %weigh.1 = (f32[128,1024]{1,0:T(8,128)S(1)}, f32[128,1024]{1,0:T(8,128)S(1)}, f32[128,1024]{1,0:T(8,128)S(1)}, f32[128,1024]{1,0:T(8,128)S(1)}, f32[128,1024]{1,...) custom-call(f32[8,128]{1,0:T(8,128)S(1)} %small.33.refs_0_, ...), custom_call_target="tpu_custom_call" | custom-call | flops 10000 | bytes 100000 | tf_op jit(solution)/shard_map/weigh/pallas_call | solution.py:347
  139.2 3.0 %collective-permute-start.28 = (f32[128,1024]{1,0:T(8,128)S(1)}, f32[128,1024]{1,0:T(8,128)S(1)}, u32[]{:S(2)}, u32[]{:S(2)}) collective-permute-start(f32[128,1024]{1,0:T(8,128)S(1)} %add.368), channel_id=1, source_target_pairs={{0,12},{4,0},{8,4},{12,8},{1,13},{5,1},{9,5},{13,9},{2,14},{6,2},{... | collective-permute-start | bytes 1572872 | tf_op jit(solution)/shard_map/ppermute | solution.py:24
  142.3 6.7 %text_part.2 = (f32[128,1024]{1,0:T(8,128)S(1)}, f32[128,1024]{1,0:T(8,128)S(1)}, f32[128,1024]{1,0:T(8,128)S(1)}, f32[128,1024]{1,0:T(8,128)S(1)}) custom-call(f32[8,1024]{1,0:T(8,128)S(1)} %get-tuple-element.121.heavy, bf16[2048,1024]{1,0:T(8,128)(2,1)S(1)} %get-tuple-element.111.wh.refs_1_, bf16[2048,1024]{1,0:T(8,128)(2,1)S(1)} %get-tuple-element.112.wl.refs_2_, ...), custom_call_target="tpu_custom_call" | custom-call | flops 10000 | bytes 100000 | tf_op jit(solution)/shard_map/text_part/pallas_call | solution.py:400
  149.2 2.2 %collective-permute-start.32 = (f32[128,1024]{1,0:T(8,128)S(1)}, f32[128,1024]{1,0:T(8,128)S(1)}, u32[]{:S(2)}, u32[]{:S(2)}) collective-permute-start(f32[128,1024]{1,0:T(8,128)S(1)} %get-tuple-element.119), channel_id=1, source_target_pairs={{0,18},{18,0},{2,16},{16,2},{1,19},{19,1},{3,17},{17,3},{4,22},{22... | collective-permute-start | bytes 1572872 | tf_op jit(solution)/shard_map/ppermute | solution.py:28
  151.5 6.7 %text_part.3 = (f32[128,1024]{1,0:T(8,128)S(1)}, f32[128,1024]{1,0:T(8,128)S(1)}, f32[128,1024]{1,0:T(8,128)S(1)}, f32[128,1024]{1,0:T(8,128)S(1)}) custom-call(f32[8,1024]{1,0:T(8,128)S(1)} %get-tuple-element.121.heavy, bf16[2048,1024]{1,0:T(8,128)(2,1)S(1)} %get-tuple-element.111.wh.refs_1_, bf16[2048,1024]{1,0:T(8,128)(2,1)S(1)} %get-tuple-element.112.wl.refs_2_, ...), custom_call_target="tpu_custom_call" | custom-call | flops 10000 | bytes 100000 | tf_op jit(solution)/shard_map/text_part/pallas_call | solution.py:400
  158.2 3.3 %collective-permute-start.31 = (f32[128,1024]{1,0:T(8,128)S(1)}, f32[128,1024]{1,0:T(8,128)S(1)}, u32[]{:S(2)}, u32[]{:S(2)}) collective-permute-start(f32[128,1024]{1,0:T(8,128)S(1)} %get-tuple-element.120), channel_id=1, source_target_pairs={{0,96},{32,0},{64,32},{96,64},{1,97},{33,1},{65,33},{97,65},{2,98}... | collective-permute-start | bytes 1572872 | tf_op jit(solution)/shard_map/ppermute | solution.py:24
  161.7 1.5 collective-permute-start.35
  163.3 1.4 collective-permute-start.34
  165.5 5.7 %page_part.1 = (f32[128,1024]{1,0:T(8,128)S(1)}, f32[128,1024]{1,0:T(8,128)S(1)}, f32[128,1024]{1,0:T(8,128)S(1)}, f32[128,1024]{1,0:T(8,128)S(1)}, f32[128,1024]{1,0:T(8,128)S(1)}, /*index=5*/f32[128,1024]{1,0:T(8,128)S(1)}) custom-call(s32[16]{0:T(128)S(1)} %stack.103.refs_3_.refs_0_, bf16[2048,1024]{1,0:T(8,128)(2,1)S(1)} %get-tuple-element.111.wh.refs_1_, ...), custom_call_target="tpu_custom_call" | custom-call | flops 10000 | bytes 100000 | tf_op jit(solution)/shard_map/page_part/pallas_call | solution.py:377
  172.4 1.9 collective-permute-done.35
  174.5 3.2 %collective-permute-start.43 = (f32[64,1024]{1,0:T(8,128)S(1)}, f32[64,1024]{1,0:T(8,128)S(1)}, u32[]{:S(2)}, u32[]{:S(2)}) collective-permute-start(f32[64,1024]{1,0:T(8,128)S(1)} %get-tuple-element.165), channel_id=1, source_target_pairs={{0,96},{32,0},{64,32},{96,64},{1,97},{33,1},{65,33},{97,65},{2,98}... | collective-permute-start | bytes 786440 | tf_op jit(solution)/shard_map/ppermute | solution.py:24
  178.4 3.7 %collective-permute-done.41 = f32[64,1024]{1,0:T(8,128)S(1)} collective-permute-done((f32[64,1024]{1,0:T(8,128)S(1)}, f32[64,1024]{1,0:T(8,128)S(1)}, u32[]{:S(2)}, u32[]{:S(2)}) %collective-permute-start.41) | collective-permute-done | bytes 262176 | tf_op jit(solution)/shard_map/ppermute | solution.py:24
  182.1 1.1 collective-permute-start.45
  183.4 2.2 %collective-permute-start.44 = (f32[128,1024]{1,0:T(8,128)S(1)}, f32[128,1024]{1,0:T(8,128)S(1)}, u32[]{:S(2)}, u32[]{:S(2)}) collective-permute-start(f32[128,1024]{1,0:T(8,128)S(1)} %pad_maximum_fusion.3), channel_id=1, source_target_pairs={{0,96},{32,0},{64,32},{96,64},{1,97},{33,1},{65,33},{97,65},{2,98}... | collective-permute-start | bytes 1572872 | tf_op jit(solution)/shard_map/ppermute | solution.py:24
  186.1 1.4 collective-permute-start.40
  188.3 5.7 %collective-permute-done.45 = f32[128,1024]{1,0:T(8,128)S(1)} collective-permute-done((f32[128,1024]{1,0:T(8,128)S(1)}, f32[128,1024]{1,0:T(8,128)S(1)}, u32[]{:S(2)}, u32[]{:S(2)}) %collective-permute-start.45) | collective-permute-done | bytes 524320 | tf_op jit(solution)/shard_map/ppermute | solution.py:28
  194.0 2.8 %collective-permute-done.42 = f32[128,1024]{1,0:T(8,128)S(1)} collective-permute-done((f32[128,1024]{1,0:T(8,128)S(1)}, f32[128,1024]{1,0:T(8,128)S(1)}, u32[]{:S(2)}, u32[]{:S(2)}) %collective-permute-start.42) | collective-permute-done | bytes 524320 | tf_op jit(solution)/shard_map/ppermute | solution.py:24
  198.5 1.0 negate_divide_fusion
  (101 shorter events, 15.3 us)
Async XLA Ops:
  7.2 57.1 %all-gather.2.cloned.1.call-start = ((), (), s32[]{:S(2)}) async-start(), calls=%async_computation | async-start | bytes 8912896 | tf_op jit(solution)/shard_map/all_gather | solution.py:510
  7.9 15.7 %collective-permute-start.1 = (f32[128,1024]{1,0:T(8,128)}, f32[128,1024]{1,0:T(8,128)S(1)}, u32[]{:S(2)}, u32[]{:S(2)}) collective-permute-start(f32[128,1024]{1,0:T(8,128)} %refs_0_.1), channel_id=1, source_target_pairs={{0,96},{32,0},{64,32},{96,64},{1,97},{33,1},{65,33},{97,65},{2,98}... | collective-permute-start | bytes 1572872 | tf_op jit(solution)/shard_map/ppermute | solution.py:24
  12.1 14.8 %collective-permute-start = (f32[128,1024]{1,0:T(8,128)}, f32[128,1024]{1,0:T(8,128)S(1)}, u32[]{:S(2)}, u32[]{:S(2)}) collective-permute-start(f32[128,1024]{1,0:T(8,128)} %refs_0_.1), channel_id=1, source_target_pairs={{0,18},{18,0},{2,16},{16,2},{1,19},{19,1},{3,17},{17,3},{4,22},{22... | collective-permute-start | bytes 1572872 | tf_op jit(solution)/shard_map/ppermute | solution.py:28
  14.8 14.5 %collective-permute-start.2 = (f32[128,1024]{1,0:T(8,128)}, f32[128,1024]{1,0:T(8,128)S(1)}, u32[]{:S(2)}, u32[]{:S(2)}) collective-permute-start(f32[128,1024]{1,0:T(8,128)} %refs_0_.1), channel_id=1, source_target_pairs={{0,32},{32,64},{64,96},{96,0},{1,33},{33,65},{65,97},{97,1},{2,34}... | collective-permute-start | bytes 1572872 | tf_op jit(solution)/shard_map/ppermute | solution.py:24
  29.4 7.8 %collective-permute-start.4 = (f32[64,1024]{1,0:T(8,128)S(1)}, f32[64,1024]{1,0:T(8,128)S(1)}, u32[]{:S(2)}, u32[]{:S(2)}) collective-permute-start(f32[64,1024]{1,0:T(8,128)S(1)} %slice.43), channel_id=1, source_target_pairs={{0,32},{32,64},{64,96},{96,0},{1,33},{33,65},{65,97},{97,1},{2,34}... | collective-permute-start | bytes 786440 | tf_op jit(solution)/shard_map/ppermute | solution.py:24
  29.5 7.8 %collective-permute-start.3 = (f32[64,1024]{1,0:T(8,128)S(1)}, f32[64,1024]{1,0:T(8,128)S(1)}, u32[]{:S(2)}, u32[]{:S(2)}) collective-permute-start(f32[64,1024]{1,0:T(8,128)S(1)} %slice.42), channel_id=1, source_target_pairs={{0,96},{32,0},{64,32},{96,64},{1,97},{33,1},{65,33},{97,65},{2,98}... | collective-permute-start | bytes 786440 | tf_op jit(solution)/shard_map/ppermute | solution.py:24
  37.3 12.5 %collective-permute-start.6 = (f32[128,1024]{1,0:T(8,128)S(1)}, f32[128,1024]{1,0:T(8,128)S(1)}, u32[]{:S(2)}, u32[]{:S(2)}) collective-permute-start(f32[128,1024]{1,0:T(8,128)S(1)} %constant_dynamic-update-slice_fusion.refs_2_), channel_id=1, source_target_pairs={{0,18},{18,0},{2,16},{16,2},{1,19},{19,1},{3,17},{17,3},{4,22},{22... | collective-permute-start | bytes 1572872 | tf_op jit(solution)/shard_map/ppermute | solution.py:28
  38.0 12.3 %collective-permute-start.7 = (f32[128,1024]{1,0:T(8,128)S(1)}, f32[128,1024]{1,0:T(8,128)S(1)}, u32[]{:S(2)}, u32[]{:S(2)}) collective-permute-start(f32[128,1024]{1,0:T(8,128)S(1)} %collective-permute-done.refs_4_), channel_id=1, source_target_pairs={{0,32},{32,64},{64,96},{96,0},{1,33},{33,65},{65,97},{97,1},{2,34}... | collective-permute-start | bytes 1572872 | tf_op jit(solution)/shard_map/ppermute | solution.py:24
  38.0 12.3 %collective-permute-start.5 = (f32[128,1024]{1,0:T(8,128)S(1)}, f32[128,1024]{1,0:T(8,128)}, u32[]{:S(2)}, u32[]{:S(2)}) collective-permute-start(f32[128,1024]{1,0:T(8,128)S(1)} %collective-permute-done.refs_4_), channel_id=1, source_target_pairs={{0,96},{32,0},{64,32},{96,64},{1,97},{33,1},{65,33},{97,65},{2,98}... | collective-permute-start | bytes 1572872 | tf_op jit(solution)/shard_map/ppermute | solution.py:24
  50.3 1.0 copy-start
  86.8 1.3 collective-permute-start.8
  88.1 3.8 %collective-permute-start.9 = (f32[24,128]{1,0:T(8,128)S(1)}, f32[24,128]{1,0:T(8,128)S(1)}, u32[]{:S(2)}, u32[]{:S(2)}) collective-permute-start(f32[24,128]{1,0:T(8,128)S(1)} %small.17.r), channel_id=1, source_target_pairs={{0,2},{2,0},{1,3},{3,1},{4,6},{6,4},{5,7},{7,5},{8,10},{10,8},{9,1... | collective-permute-start | bytes 36872 | tf_op jit(solution)/shard_map/ppermute | solution.py:24
  89.6 4.9 %collective-permute-start.15 = (f32[16,128]{1,0:T(8,128)S(1)}, f32[16,128]{1,0:T(8,128)S(1)}, u32[]{:S(2)}, u32[]{:S(2)}) collective-permute-start(f32[16,128]{1,0:T(8,128)S(1)} %get-tuple-element.95.c), channel_id=1, source_target_pairs={{0,18},{18,0},{2,16},{16,2},{1,19},{19,1},{3,17},{17,3},{4,22},{22... | collective-permute-start | bytes 24584 | tf_op jit(solution)/shard_map/ppermute | solution.py:28
  91.9 9.5 %collective-permute-start.10 = (f32[24,128]{1,0:T(8,128)S(1)}, f32[24,128]{1,0:T(8,128)S(1)}, u32[]{:S(2)}, u32[]{:S(2)}) collective-permute-start(f32[24,128]{1,0:T(8,128)S(1)} %small.18.r), channel_id=1, source_target_pairs={{0,4},{4,0},{8,12},{12,8},{1,5},{5,1},{9,13},{13,9},{2,6},{6,2},{1... | collective-permute-start | bytes 36872 | tf_op jit(solution)/shard_map/ppermute | solution.py:478
  94.6 3.7 %collective-permute-start.16 = (f32[16,128]{1,0:T(8,128)S(1)}, f32[16,128]{1,0:T(8,128)S(1)}, u32[]{:S(2)}, u32[]{:S(2)}) collective-permute-start(f32[16,128]{1,0:T(8,128)S(1)} %small.25.c), channel_id=1, source_target_pairs={{0,32},{32,0},{64,96},{96,64},{1,33},{33,1},{65,97},{97,65},{2,34}... | collective-permute-start | bytes 24584 | tf_op jit(solution)/shard_map/ppermute | solution.py:478
  98.4 5.3 %collective-permute-start.17 = (f32[16,128]{1,0:T(8,128)S(1)}, f32[16,128]{1,0:T(8,128)S(1)}, u32[]{:S(2)}, u32[]{:S(2)}) collective-permute-start(f32[16,128]{1,0:T(8,128)S(1)} %small.26.c), channel_id=1, source_target_pairs={{0,96},{32,64},{64,32},{96,0},{1,97},{33,65},{65,33},{97,1},{2,98}... | collective-permute-start | bytes 24584 | tf_op jit(solution)/shard_map/ppermute | solution.py:478
  101.4 5.0 %collective-permute-start.11 = (f32[24,128]{1,0:T(8,128)S(1)}, f32[24,128]{1,0:T(8,128)S(1)}, u32[]{:S(2)}, u32[]{:S(2)}) collective-permute-start(f32[24,128]{1,0:T(8,128)S(1)} %small.19.r), channel_id=1, source_target_pairs={{0,12},{4,8},{8,4},{12,0},{1,13},{5,9},{9,5},{13,1},{2,14},{6,10},... | collective-permute-start | bytes 36872 | tf_op jit(solution)/shard_map/ppermute | solution.py:478
  104.0 1.2 collective-permute-start.18
  105.2 3.6 %collective-permute-start.19 = (f32[8,128]{1,0:T(8,128)S(1)}, f32[8,128]{1,0:T(8,128)S(1)}, u32[]{:S(2)}, u32[]{:S(2)}) collective-permute-start(f32[8,128]{1,0:T(8,128)S(1)} %small.29.u), channel_id=1, source_target_pairs={{0,2},{2,0},{1,3},{3,1},{4,6},{6,4},{5,7},{7,5},{8,10},{10,8},{9,1... | collective-permute-start | bytes 12296 | tf_op jit(solution)/shard_map/ppermute | solution.py:24
  106.4 4.9 %collective-permute-start.12 = (f32[8,128]{1,0:T(8,128)S(1)}, f32[8,128]{1,0:T(8,128)S(1)}, u32[]{:S(2)}, u32[]{:S(2)}) collective-permute-start(f32[8,128]{1,0:T(8,128)S(1)} %small.21.s), channel_id=1, source_target_pairs={{0,18},{18,0},{2,16},{16,2},{1,19},{19,1},{3,17},{17,3},{4,22},{22... | collective-permute-start | bytes 12296 | tf_op jit(solution)/shard_map/ppermute | solution.py:28
  108.8 3.6 %collective-permute-start.20 = (f32[8,128]{1,0:T(8,128)S(1)}, f32[8,128]{1,0:T(8,128)S(1)}, u32[]{:S(2)}, u32[]{:S(2)}) collective-permute-start(f32[8,128]{1,0:T(8,128)S(1)} %small.30.u), channel_id=1, source_target_pairs={{0,4},{4,0},{8,12},{12,8},{1,5},{5,1},{9,13},{13,9},{2,6},{6,2},{1... | collective-permute-start | bytes 12296 | tf_op jit(solution)/shard_map/ppermute | solution.py:478
  111.3 3.6 %collective-permute-start.13 = (f32[8,128]{1,0:T(8,128)S(1)}, f32[8,128]{1,0:T(8,128)S(1)}, u32[]{:S(2)}, u32[]{:S(2)}) collective-permute-start(f32[8,128]{1,0:T(8,128)S(1)} %small.22.s), channel_id=1, source_target_pairs={{0,32},{32,0},{64,96},{96,64},{1,33},{33,1},{65,97},{97,65},{2,34}... | collective-permute-start | bytes 12296 | tf_op jit(solution)/shard_map/ppermute | solution.py:478
  112.5 4.8 %collective-permute-start.21 = (f32[8,128]{1,0:T(8,128)S(1)}, f32[8,128]{1,0:T(8,128)S(1)}, u32[]{:S(2)}, u32[]{:S(2)}) collective-permute-start(f32[8,128]{1,0:T(8,128)S(1)} %small.31.u), channel_id=1, source_target_pairs={{0,12},{4,8},{8,4},{12,0},{1,13},{5,9},{9,5},{13,1},{2,14},{6,10},... | collective-permute-start | bytes 12296 | tf_op jit(solution)/shard_map/ppermute | solution.py:478
  114.9 4.8 %collective-permute-start.14 = (f32[8,128]{1,0:T(8,128)S(1)}, f32[8,128]{1,0:T(8,128)S(1)}, u32[]{:S(2)}, u32[]{:S(2)}) collective-permute-start(f32[8,128]{1,0:T(8,128)S(1)} %small.23.s), channel_id=1, source_target_pairs={{0,96},{32,64},{64,32},{96,0},{1,97},{33,65},{65,33},{97,1},{2,98}... | collective-permute-start | bytes 12296 | tf_op jit(solution)/shard_map/ppermute | solution.py:478
  135.3 2.0 collective-permute-start.24
  135.4 2.6 %collective-permute-start.25 = (f32[128,1024]{1,0:T(8,128)S(1)}, f32[128,1024]{1,0:T(8,128)S(1)}, u32[]{:S(2)}, u32[]{:S(2)}) collective-permute-start(f32[128,1024]{1,0:T(8,128)S(1)} %get-tuple-element.106), channel_id=1, source_target_pairs={{0,1},{1,0},{2,3},{3,2},{4,5},{5,4},{6,7},{7,6},{8,9},{9,8},{10,11... | collective-permute-start | bytes 1572872 | tf_op jit(solution)/shard_map/ppermute | solution.py:24
  135.8 2.9 %collective-permute-start.26 = (f32[128,1024]{1,0:T(8,128)S(1)}, f32[128,1024]{1,0:T(8,128)S(1)}, u32[]{:S(2)}, u32[]{:S(2)}) collective-permute-start(f32[128,1024]{1,0:T(8,128)S(1)} %get-tuple-element.108), channel_id=1, source_target_pairs={{0,1},{1,0},{2,3},{3,2},{4,5},{5,4},{6,7},{7,6},{8,9},{9,8},{10,11... | collective-permute-start | bytes 1572872 | tf_op jit(solution)/shard_map/ppermute | solution.py:24
  135.9 13.1 %collective-permute-start.22 = (f32[128,1024]{1,0:T(8,128)S(1)}, f32[128,1024]{1,0:T(8,128)S(1)}, u32[]{:S(2)}, u32[]{:S(2)}) collective-permute-start(f32[128,1024]{1,0:T(8,128)S(1)} %get-tuple-element.100), channel_id=1, source_target_pairs={{0,1},{1,0},{2,3},{3,2},{4,5},{5,4},{6,7},{7,6},{8,9},{9,8},{10,11... | collective-permute-start | bytes 1572872 | tf_op jit(solution)/shard_map/ppermute | solution.py:24
  136.4 12.8 %collective-permute-start.23 = (f32[128,1024]{1,0:T(8,128)S(1)}, f32[128,1024]{1,0:T(8,128)S(1)}, u32[]{:S(2)}, u32[]{:S(2)}) collective-permute-start(f32[128,1024]{1,0:T(8,128)S(1)} %get-tuple-element.102), channel_id=1, source_target_pairs={{0,1},{1,0},{2,3},{3,2},{4,5},{5,4},{6,7},{7,6},{8,9},{9,8},{10,11... | collective-permute-start | bytes 1572872 | tf_op jit(solution)/shard_map/ppermute | solution.py:24
  138.8 19.4 %collective-permute-start.27 = (f32[128,1024]{1,0:T(8,128)S(1)}, f32[128,1024]{1,0:T(8,128)S(1)}, u32[]{:S(2)}, u32[]{:S(2)}) collective-permute-start(f32[128,1024]{1,0:T(8,128)S(1)} %add.367), channel_id=1, source_target_pairs={{0,4},{4,8},{8,12},{12,0},{1,5},{5,9},{9,13},{13,1},{2,6},{6,10},{... | collective-permute-start | bytes 1572872 | tf_op jit(solution)/shard_map/ppermute | solution.py:24
  139.2 22.4 %collective-permute-start.28 = (f32[128,1024]{1,0:T(8,128)S(1)}, f32[128,1024]{1,0:T(8,128)S(1)}, u32[]{:S(2)}, u32[]{:S(2)}) collective-permute-start(f32[128,1024]{1,0:T(8,128)S(1)} %add.368), channel_id=1, source_target_pairs={{0,12},{4,0},{8,4},{12,8},{1,13},{5,1},{9,5},{13,9},{2,14},{6,2},{... | collective-permute-start | bytes 1572872 | tf_op jit(solution)/shard_map/ppermute | solution.py:24
  142.1 19.4 %collective-permute-start.29 = (f32[128,1024]{1,0:T(8,128)S(1)}, f32[128,1024]{1,0:T(8,128)S(1)}, u32[]{:S(2)}, u32[]{:S(2)}) collective-permute-start(f32[128,1024]{1,0:T(8,128)S(1)} %add.369), channel_id=1, source_target_pairs={{0,2},{2,0},{1,3},{3,1},{4,6},{6,4},{5,7},{7,5},{8,10},{10,8},{9,1... | collective-permute-start | bytes 1572872 | tf_op jit(solution)/shard_map/ppermute | solution.py:24
  149.0 15.6 %collective-permute-start.30 = (f32[128,1024]{1,0:T(8,128)S(1)}, f32[128,1024]{1,0:T(8,128)S(1)}, u32[]{:S(2)}, u32[]{:S(2)}) collective-permute-start(f32[128,1024]{1,0:T(8,128)S(1)} %get-tuple-element.118), channel_id=1, source_target_pairs={{0,32},{32,64},{64,96},{96,0},{1,33},{33,65},{65,97},{97,1},{2,34}... | collective-permute-start | bytes 1572872 | tf_op jit(solution)/shard_map/ppermute | solution.py:24
  149.2 22.1 %collective-permute-start.32 = (f32[128,1024]{1,0:T(8,128)S(1)}, f32[128,1024]{1,0:T(8,128)S(1)}, u32[]{:S(2)}, u32[]{:S(2)}) collective-permute-start(f32[128,1024]{1,0:T(8,128)S(1)} %get-tuple-element.119), channel_id=1, source_target_pairs={{0,18},{18,0},{2,16},{16,2},{1,19},{19,1},{3,17},{17,3},{4,22},{22... | collective-permute-start | bytes 1572872 | tf_op jit(solution)/shard_map/ppermute | solution.py:28
  158.2 13.7 %collective-permute-start.31 = (f32[128,1024]{1,0:T(8,128)S(1)}, f32[128,1024]{1,0:T(8,128)S(1)}, u32[]{:S(2)}, u32[]{:S(2)}) collective-permute-start(f32[128,1024]{1,0:T(8,128)S(1)} %get-tuple-element.120), channel_id=1, source_target_pairs={{0,96},{32,0},{64,32},{96,64},{1,97},{33,1},{65,33},{97,65},{2,98}... | collective-permute-start | bytes 1572872 | tf_op jit(solution)/shard_map/ppermute | solution.py:24
  161.7 12.6 %collective-permute-start.35 = (f32[128,1024]{1,0:T(8,128)S(1)}, f32[128,1024]{1,0:T(8,128)S(1)}, u32[]{:S(2)}, u32[]{:S(2)}) collective-permute-start(f32[128,1024]{1,0:T(8,128)S(1)} %add_add_fusion.1), channel_id=1, source_target_pairs={{0,2},{2,0},{1,3},{3,1},{4,6},{6,4},{5,7},{7,5},{8,10},{10,8},{9,1... | collective-permute-start | bytes 1572872 | tf_op jit(solution)/shard_map/ppermute | solution.py:24
  163.3 8.6 %collective-permute-start.34 = (f32[64,1024]{1,0:T(8,128)S(1)}, f32[64,1024]{1,0:T(8,128)S(1)}, u32[]{:S(2)}, u32[]{:S(2)}) collective-permute-start(f32[64,1024]{1,0:T(8,128)S(1)} %get-tuple-element.172), channel_id=1, source_target_pairs={{0,12},{4,0},{8,4},{12,8},{1,13},{5,1},{9,5},{13,9},{2,14},{6,2},{... | collective-permute-start | bytes 786440 | tf_op jit(solution)/shard_map/ppermute | solution.py:24
  164.6 7.8 %collective-permute-start.33 = (f32[64,1024]{1,0:T(8,128)S(1)}, f32[64,1024]{1,0:T(8,128)S(1)}, u32[]{:S(2)}, u32[]{:S(2)}) collective-permute-start(f32[64,1024]{1,0:T(8,128)S(1)} %get-tuple-element.173), channel_id=1, source_target_pairs={{0,4},{4,8},{8,12},{12,0},{1,5},{5,9},{9,13},{13,1},{2,6},{6,10},{... | collective-permute-start | bytes 786440 | tf_op jit(solution)/shard_map/ppermute | solution.py:24
  174.4 7.7 %collective-permute-start.41 = (f32[64,1024]{1,0:T(8,128)S(1)}, f32[64,1024]{1,0:T(8,128)S(1)}, u32[]{:S(2)}, u32[]{:S(2)}) collective-permute-start(f32[64,1024]{1,0:T(8,128)S(1)} %get-tuple-element.164), channel_id=1, source_target_pairs={{0,32},{32,64},{64,96},{96,0},{1,33},{33,65},{65,97},{97,1},{2,34}... | collective-permute-start | bytes 786440 | tf_op jit(solution)/shard_map/ppermute | solution.py:24
  174.5 8.7 %collective-permute-start.43 = (f32[64,1024]{1,0:T(8,128)S(1)}, f32[64,1024]{1,0:T(8,128)S(1)}, u32[]{:S(2)}, u32[]{:S(2)}) collective-permute-start(f32[64,1024]{1,0:T(8,128)S(1)} %get-tuple-element.165), channel_id=1, source_target_pairs={{0,96},{32,0},{64,32},{96,64},{1,97},{33,1},{65,33},{97,65},{2,98}... | collective-permute-start | bytes 786440 | tf_op jit(solution)/shard_map/ppermute | solution.py:24
  177.7 7.9 %collective-permute-start.36 = (f32[128,1024]{1,0:T(8,128)S(1)}, f32[128,1024]{1,0:T(8,128)S(1)}, u32[]{:S(2)}, u32[]{:S(2)}) collective-permute-start(f32[128,1024]{1,0:T(8,128)S(1)} %get-tuple-element.143), channel_id=1, source_target_pairs={{0,1},{1,0},{2,3},{3,2},{4,5},{5,4},{6,7},{7,6},{8,9},{9,8},{10,11... | collective-permute-start | bytes 1572872 | tf_op jit(solution)/shard_map/ppermute | solution.py:24
  177.7 8.0 %collective-permute-start.37 = (f32[128,1024]{1,0:T(8,128)S(1)}, f32[128,1024]{1,0:T(8,128)S(1)}, u32[]{:S(2)}, u32[]{:S(2)}) collective-permute-start(f32[128,1024]{1,0:T(8,128)S(1)} %get-tuple-element.145), channel_id=1, source_target_pairs={{0,1},{1,0},{2,3},{3,2},{4,5},{5,4},{6,7},{7,6},{8,9},{9,8},{10,11... | collective-permute-start | bytes 1572872 | tf_op jit(solution)/shard_map/ppermute | solution.py:24
  178.2 7.6 %collective-permute-start.38 = (f32[128,1024]{1,0:T(8,128)S(1)}, f32[128,1024]{1,0:T(8,128)S(1)}, u32[]{:S(2)}, u32[]{:S(2)}) collective-permute-start(f32[128,1024]{1,0:T(8,128)S(1)} %get-tuple-element.147), channel_id=1, source_target_pairs={{0,1},{1,0},{2,3},{3,2},{4,5},{5,4},{6,7},{7,6},{8,9},{9,8},{10,11... | collective-permute-start | bytes 1572872 | tf_op jit(solution)/shard_map/ppermute | solution.py:24
  182.1 11.9 %collective-permute-start.45 = (f32[128,1024]{1,0:T(8,128)S(1)}, f32[128,1024]{1,0:T(8,128)S(1)}, u32[]{:S(2)}, u32[]{:S(2)}) collective-permute-start(f32[128,1024]{1,0:T(8,128)S(1)} %add_add_fusion), channel_id=1, source_target_pairs={{0,18},{18,0},{2,16},{16,2},{1,19},{19,1},{3,17},{17,3},{4,22},{22... | collective-permute-start | bytes 1572872 | tf_op jit(solution)/shard_map/ppermute | solution.py:28
  183.4 10.6 %collective-permute-start.44 = (f32[128,1024]{1,0:T(8,128)S(1)}, f32[128,1024]{1,0:T(8,128)S(1)}, u32[]{:S(2)}, u32[]{:S(2)}) collective-permute-start(f32[128,1024]{1,0:T(8,128)S(1)} %pad_maximum_fusion.3), channel_id=1, source_target_pairs={{0,96},{32,0},{64,32},{96,64},{1,97},{33,1},{65,33},{97,65},{2,98}... | collective-permute-start | bytes 1572872 | tf_op jit(solution)/shard_map/ppermute | solution.py:24
  185.6 11.2 %collective-permute-start.42 = (f32[128,1024]{1,0:T(8,128)S(1)}, f32[128,1024]{1,0:T(8,128)S(1)}, u32[]{:S(2)}, u32[]{:S(2)}) collective-permute-start(f32[128,1024]{1,0:T(8,128)S(1)} %pad_maximum_fusion.2), channel_id=1, source_target_pairs={{0,32},{32,64},{64,96},{96,0},{1,33},{33,65},{65,97},{97,1},{2,34}... | collective-permute-start | bytes 1572872 | tf_op jit(solution)/shard_map/ppermute | solution.py:24
  186.1 11.7 %collective-permute-start.40 = (f32[128,1024]{1,0:T(8,128)S(1)}, f32[128,1024]{1,0:T(8,128)S(1)}, u32[]{:S(2)}, u32[]{:S(2)}) collective-permute-start(f32[128,1024]{1,0:T(8,128)S(1)} %pad_maximum_fusion.1), channel_id=1, source_target_pairs={{0,12},{4,0},{8,4},{12,8},{1,13},{5,1},{9,5},{13,9},{2,14},{6,2},{... | collective-permute-start | bytes 1572872 | tf_op jit(solution)/shard_map/ppermute | solution.py:24
  187.5 10.9 %collective-permute-start.39 = (f32[128,1024]{1,0:T(8,128)S(1)}, f32[128,1024]{1,0:T(8,128)S(1)}, u32[]{:S(2)}, u32[]{:S(2)}) collective-permute-start(f32[128,1024]{1,0:T(8,128)S(1)} %pad_maximum_fusion), channel_id=1, source_target_pairs={{0,4},{4,8},{8,12},{12,0},{1,5},{5,9},{9,13},{13,1},{2,6},{6,10},{... | collective-permute-start | bytes 1572872 | tf_op jit(solution)/shard_map/ppermute | solution.py:24
Sparse Core Ops, SparseCore 0:
  9.7 54.5 all-gather.1
